TPU v7x, 32 devices: a whole 2x2x4 slice. The times are simulated.
32 devices in a mesh: groups: 2 (over y), seq: 16 (over z, x, core).
Axes of the slice: x: 2, y: 2, z: 4, core: 2. Of those that a mesh axis runs over, the one named last changes fastest.
Arguments:
- projected: bfloat16 [4096, 6144], P(('groups', 'seq')), parts along dimension 0, may hold values from -6 to 6
- filters: float32 [3, 7, 2048], replicated, may hold values from -3 to 3
- upstream: bfloat16 [4096, 2048], P(('groups', 'seq')), parts along dimension 0, may hold values from -20 to 20
Outputs:
- gated: bfloat16 [4096, 2048], P(('groups', 'seq')), parts along dimension 0
- grad_projected: bfloat16 [4096, 6144], P(('groups', 'seq')), parts along dimension 0
- grad_filters: float32 [6, 7, 2048], P('groups'), parts along dimension 0
There are 2 independent parts, one for each index of `groups`. A program takes and returns all parts, laid end to end along the dimension named above; an argument that names none is the same for every part. Nothing has to cross between parts.
All inputs are finite; a program needn't handle non-finite values.
Results may differ from a plain program's by a relative error of at most 0.005.
Values may be sent and summed in bfloat16 or wider, within the bound.
No kernel may reach another device: no remote copies, remote signals or barrier semaphores. Data moves between devices by JAX's collectives and lax.ppermute only.
A program may use at most 64 MiB of HBM per device.

v0:
```python
import jax
import jax.numpy as jnp
from jax import lax
from jax.sharding import PartitionSpec as P


def from_behind(array, axis, by):
    devices = lax.axis_size(axis)
    pairs = [(i, i + by) for i in range(devices) if 0 <= i + by < devices]
    return lax.ppermute(array, axis, pairs)


def filter_rows(padded, tap_table, count):
    rim_rows = tap_table.shape[0] - 1
    result = jnp.zeros((count, padded.shape[1]), jnp.float32)
    for tap_index in range(tap_table.shape[0]):
        result = (
            result
            + tap_table[tap_index] * padded[rim_rows - tap_index : rim_rows - tap_index + count]
        )
    return result


def gate_grads(convolved, cotangent, chans):
    query = convolved[:, :chans]
    keys_conv = convolved[:, chans : 2 * chans]
    values_conv = convolved[:, 2 * chans :]
    return jnp.concatenate(
        [
            cotangent * keys_conv * values_conv,
            cotangent * query * values_conv,
            cotangent * query * keys_conv,
        ],
        1,
    ).astype(jnp.bfloat16)


def shards(projected, filters, upstream):
    tok_rows, columns = projected.shape
    ways = lax.axis_size("seq")
    tap_count = filters.shape[1]
    rim_rows = tap_count - 1
    chans = columns // 3
    scale = float(tok_rows * ways) ** (-0.5)
    tap_table = jnp.transpose(filters, (1, 0, 2)).reshape(tap_count, columns)
    prior = from_behind(projected[tok_rows - rim_rows :], "seq", 1)
    padded = jnp.concatenate([prior, projected], 0).astype(jnp.float32)
    convolved = filter_rows(padded, tap_table, tok_rows)
    grad_conv = gate_grads(convolved, upstream.astype(jnp.float32), chans)
    following = from_behind(grad_conv[:rim_rows], "seq", -1)
    grad_padded = jnp.concatenate([grad_conv, following], 0).astype(jnp.float32)
    grad_float = grad_padded[:tok_rows]
    query = convolved[:, :chans]
    keys_conv = convolved[:, chans : 2 * chans]
    values_conv = convolved[:, 2 * chans :]
    gated = (query * keys_conv * values_conv).astype(jnp.bfloat16)
    grad_proj = jnp.zeros((tok_rows, columns), jnp.float32)
    tap_grads = []
    for tap_index in range(tap_count):
        grad_proj = grad_proj + tap_table[tap_index] * grad_padded[tap_index : tap_index + tok_rows]
        tap_grads.append(
            jnp.sum(grad_float * padded[rim_rows - tap_index : rim_rows - tap_index + tok_rows], 0)
        )
    total_taps = lax.psum(jnp.stack(tap_grads, 0), "seq") * scale
    grad_filters = jnp.transpose(total_taps.reshape(tap_count, 3, chans), (1, 0, 2))
    return (gated, grad_proj.astype(jnp.bfloat16), grad_filters)


def solution(mesh):
    placed = (P(("groups", "seq"), None), P(), P(("groups", "seq"), None))
    return jax.shard_map(
        shards,
        mesh=mesh,
        in_specs=placed,
        out_specs=(P(("groups", "seq"), None), P(("groups", "seq"), None), P("groups", None, None)),
        check_vma=False,
    )
```

profile of v0, /device:TPU:0, one launch (start us, length us, event | category | flops | bytes accessed | tf_op | source)
XLA Modules:
  0.0 132.0 jit_solution(10928697603930333947)
XLA Ops:
  7.2 0.0 all-reduce.2.cloned.1.call-start
  7.2 0.9 slice.104
  8.1 2.4 %collective-permute-start = (bf16[6,6144]{1,0:T(8,128)(2,1)S(1)}, bf16[6,6144]{1,0:T(8,128)(2,1)S(1)}, u32[]{:S(2)}, u32[]{:S(2)}) collective-permute-start(bf16[6,6144]{1,0:T(8,128)(2,1)S(1)} %slice.104), channel_id=1, source_target_pairs={{0,1},{1,2},{2,3},{3,4},{4,5},{5,6},{6,7},{7,8},{8,9},{9,10},{10,1... | collective-permute-start | bytes 221192 | tf_op jit(solution)/shard_map/ppermute | solution.py:10
  10.5 1.8 %fusion.9 = (f32[1,3,2048]{2,0,1:T(1,128)S(1)}, f32[1,3,2048]{2,0,1:T(1,128)S(1)}, f32[1,3,2048]{2,0,1:T(1,128)S(1)}, f32[1,3,2048]{2,0,1:T(1,128)S(1)}, f32[1,3...) fusion(f32[7,3,2048]{2,0,1:T(8,128)} %bitcast.33), kind=kLoop, calls=%fused_computation.33 | loop fusion | bytes 344064 | tf_op jit(solution)/shard_map/slice | solution.py:19
  12.3 0.0 collective-permute-done
  12.3 1.9 %maximum_convert_fusion = f32[134,6144]{1,0:T(8,128)S(1)} fusion(bf16[128,6144]{1,0:T(8,128)(2,1)} %param.3, bf16[6,6144]{1,0:T(8,128)(2,1)S(1)} %collective-permute-done), kind=kLoop, calls=%fused_computation.21 | loop fusion | flops 3293184 | bytes 4939776 | tf_op jit(solution)/shard_map/convert_element_type | solution.py:47
  14.2 0.0 copy-start
  14.2 2.6 %multiply_add_fusion = f32[128,6144]{1,0:T(8,128)S(1)} fusion(f32[134,6144]{1,0:T(8,128)S(1)} %maximum_convert_fusion, f32[6144]{0:T(1024)S(1)} %bitcast.20, f32[6144]{0:T(1024)S(1)} %bitcast.22, f32[6144]{0:T(1024)S(1)} %bitcast.24, f32[6144]{0:T(1024)S(1)} %bitcast.26, f32[6144]{0:T(1024)S(1)} %bitcast.28, f32[6144]{0:T(1024)S(1)} %bitcast.30, ...), kind=kLoop, calls=%fused_computation.20 | loop fusion | flops 10223616 | bytes 25337856 | tf_op jit(solution)/shard_map/add | solution.py:18
  16.8 0.0 copy-done
  16.8 1.3 fusion.8
  18.1 1.3 collective-permute-start.1
  19.4 4.0 %collective-permute-done.1 = bf16[6,6144]{1,0:T(8,128)(2,1)S(1)} collective-permute-done((bf16[6,6144]{1,0:T(8,128)(2,1)S(1)}, bf16[6,6144]{1,0:T(8,128)(2,1)S(1)}, u32[]{:S(2)}, u32[]{:S(2)}) %collective-permute-start.1) | collective-permute-done | bytes 73760 | tf_op jit(solution)/shard_map/ppermute | solution.py:10
  23.4 0.3 maximum_convert_fusion.1
  23.8 3.7 %multiply_reduce_fusion = (f32[6144]{0:T(1024)S(1)}, f32[6144]{0:T(1024)}, f32[6144]{0:T(1024)}, f32[6144]{0:T(1024)}, f32[6144]{0:T(1024)}, /*index=5*/f32[6144]{0:T(1024)}, f32[6144]{0:T(1024)}) fusion(f32[134,6144]{1,0:T(8,128)S(1)} %maximum_convert_fusion, f32[134,6144]{1,0:T(8,128)S(1)} %maximum_convert_fusion.1), kind=kLoop, calls=%fused_computation.13 | loop fusion | flops 10967040 | bytes 25337856 | tf_op jit(solution)/shard_map/reduce_sum | solution.py:62
  27.5 1.7 %stack.31 = f32[7,6144]{1,0:T(8,128)} concatenate(f32[1,6144]{1,0:T(1,128)} %bitcast.40, f32[1,6144]{1,0:T(1,128)} %bitcast.39, f32[1,6144]{1,0:T(1,128)} %bitcast.38, f32[1,6144]{1,0:T(1,128)} %bitcast.37, f32[1,6144]{1,0:T(1,128)} %bitcast.36, f32[1,6144]{1,0:T(1,128)} %bitcast.35, f32[1,6144]{1,0:T(1,128)S(1)} %bitcast.34), dimensions={0} | concatenate | bytes 344064 | tf_op jit(solution)/shard_map/stack | solution.py:64
  29.2 0.0 all-reduce.2.cloned.1.call-update
  29.2 3.5 %fusion.1 = bf16[128,6144]{1,0:T(8,128)(2,1)} fusion(f32[134,6144]{1,0:T(8,128)S(1)} %maximum_convert_fusion.1, f32[6144]{0:T(1024)S(1)} %bitcast.21, f32[6144]{0:T(1024)S(1)} %bitcast.23, f32[6144]{0:T(1024)S(1)} %bitcast.25, f32[6144]{0:T(1024)S(1)} %bitcast.27, f32[6144]{0:T(1024)S(1)} %bitcast.29, f32[6144]{0:T(1024)S(1)} %bitcast.31, f32[6144]{0:T(1024)S(1)} %bitcast.19), kind=kLoop, calls=%fused_computation.2 | loop fusion | flops 11010048 | bytes 23764992 | tf_op jit(solution)/shard_map/convert_element_type | solution.py:66
  32.8 90.8 %all-reduce.2.cloned.1.call-done = f32[7,6144]{1,0:T(8,128)} async-done(((f32[7,6144]{1,0:T(8,128)}), f32[7,6144]{1,0:T(8,128)}) %all-reduce.2.cloned.1.call-update) | async-done | bytes 172048 | tf_op jit(solution)/shard_map/psum | solution.py:64
  123.6 1.6 %broadcast_multiply_fusion = f32[7,6144]{1,0:T(8,128)} fusion(f32[7,6144]{1,0:T(8,128)} %all-reduce.2.cloned.1.call-done), kind=kLoop, calls=%fused_computation.32 | loop fusion | flops 43008 | bytes 344064 | tf_op jit(solution)/shard_map/mul | solution.py:64
  (1 shorter events, 0.0 us)
Async XLA Ops:
  7.2 116.4 %all-reduce.2.cloned.1.call-start = ((), (), s32[]{:S(2)}) async-start(), calls=%async_computation | async-start | bytes 393216 | tf_op jit(solution)/shard_map/psum | solution.py:64
  8.1 4.2 %collective-permute-start = (bf16[6,6144]{1,0:T(8,128)(2,1)S(1)}, bf16[6,6144]{1,0:T(8,128)(2,1)S(1)}, u32[]{:S(2)}, u32[]{:S(2)}) collective-permute-start(bf16[6,6144]{1,0:T(8,128)(2,1)S(1)} %slice.104), channel_id=1, source_target_pairs={{0,1},{1,2},{2,3},{3,4},{4,5},{5,6},{6,7},{7,8},{8,9},{9,10},{10,1... | collective-permute-start | bytes 221192 | tf_op jit(solution)/shard_map/ppermute | solution.py:10
  14.2 2.6 %copy-start = (bf16[128,2048]{1,0:T(8,128)(2,1)S(1)}, bf16[128,2048]{1,0:T(8,128)(2,1)}, u32[]{:S(2)}) copy-start(bf16[128,2048]{1,0:T(8,128)(2,1)} %param.5) | copy-start | bytes 1572868
  18.1 5.3 %collective-permute-start.1 = (bf16[6,6144]{1,0:T(8,128)(2,1)S(1)}, bf16[6,6144]{1,0:T(8,128)(2,1)S(1)}, u32[]{:S(2)}, u32[]{:S(2)}) collective-permute-start(bf16[6,6144]{1,0:T(8,128)(2,1)S(1)} %pad_maximum_fusion), channel_id=1, source_target_pairs={{1,0},{2,1},{3,2},{4,3},{5,4},{6,5},{7,6},{8,7},{9,8},{10,9},{11,1... | collective-permute-start | bytes 221192 | tf_op jit(solution)/shard_map/ppermute | solution.py:10
Sparse Core Ops, SparseCore 0:
  29.4 94.1 all-reduce.1
where the time goes:
time: 132 us
  waiting for transfers between devices  94.8 us (72%)
  other arithmetic  14.9 us (11%)
  between operations  14.1 us (11%)
  local copies, waits for them, and re-layouts  4.49 us (3%)
  starting transfers between devices  3.69 us (3%)
    psum x1, waiting for transfers between devices, shards(): total_taps = lax.psum(jnp.stack(tap_grads, 0), 'seq') * scale  90.8 us
    ppermute x2, waiting for transfers between devices, from_behind(): return lax.ppermute(array, axis, pairs)  4 us
    reduce_sum x1, other arithmetic, shards(): jnp.sum(grad_float * padded[rim_rows - tap_index:rim_rows - tap_index + t...  3.71 us
    ppermute x2, starting transfers between devices, from_behind(): return lax.ppermute(array, axis, pairs)  3.65 us
    convert_element_type x1, other arithmetic, shards(): return (gated, grad_proj.astype(jnp.bfloat16), grad_filters)  3.52 us
  transfers between devices with their start and end apart: 3, of which 2 were waited for; matrix products, arithmetic and copies ran while one was open for 4% of the time, Pallas kernels for 0%

commit v1 on v0

v1 whole, which is shorter than its diff:
```python
import jax, jax.numpy as jnp
from jax import lax
from jax.experimental import pallas as pl
from jax.experimental.pallas import tpu as pltpu
from jax.sharding import PartitionSpec as P

F32 = jnp.float32
BF = jnp.bfloat16
L = 128
SUB = 8
RIM = 8
def filter_kernel(p_ref, u_ref, f_ref, prior_ref, next_ref, gated_ref, g_ref, taps_ref, p_slab, u_slab, o_slab):
    rows, columns = p_ref.shape
    chans = columns // 3
    taps = f_ref.shape[1]
    pitch = rows // SUB
    half = chans // 2
    def group(n, carry):
        col = pl.multiple_of(n * L, L)
        for s in range(3):
            c = pl.multiple_of(s * chans + n * L, L)
            p_slab[s, 0:8, :] = prior_ref[:, pl.ds(c, L)].astype(F32)
            p_slab[s, 8:8 + rows, :] = p_ref[:, pl.ds(c, L)].astype(F32)
            p_slab[s, 8 + rows:16 + rows, :] = next_ref[:, pl.ds(c, L)].astype(F32)
        u_slab[...] = u_ref[:, pl.ds(col, L)].astype(F32)
        tap = [[jnp.broadcast_to(f_ref[s, j:j + 1, pl.ds(col, L)], (SUB, L)) for j in range(taps)] for s in range(3)]
        window = [[p_slab[s, pl.ds(8 + r, SUB, stride=pitch), :] for r in range(1 - taps, 0)] for s in range(3)]
        for r in range(pitch):
            conv = []
            for s in range(3):
                window[s].append(p_slab[s, pl.ds(8 + r, SUB, stride=pitch), :])
                w = window[s]
                conv.append(sum(tap[s][j] * w[-1 - j] for j in range(taps)))
                window[s] = w[1:]
            u = u_slab[pl.ds(r, SUB, stride=pitch), :]
            q, k, v = conv
            kv = k * v
            uq = u * q
            o_slab[pl.ds(r, SUB, stride=pitch), :] = q * kv
            for s, g in enumerate((u * kv, uq * v, uq * k)):
                g_ref[s, n, pl.ds(r, SUB, stride=pitch), :] = g.astype(BF).astype(F32)
        gated_ref[:, pl.ds(col, L)] = o_slab[...].astype(BF)
        un = next_ref[:, pl.ds(pl.multiple_of(columns + n * L, L), L)].astype(F32)
        conv = [sum(tap[s][j] * p_slab[s, 8 + rows - j:16 + rows - j, :] for j in range(taps)) for s in range(3)]
        q, k, v = conv
        for s, g in enumerate((un * (k * v), un * q * v, un * q * k)):
            g_ref[s, n, rows:rows + 8, :] = g.astype(BF).astype(F32)
        h = n // (half // L)
        hcol = pl.multiple_of((n % (half // L)) * L, L)
        for s in range(3):
            w = [p_slab[s, pl.ds(8 + r, SUB, stride=pitch), :] for r in range(1 - taps, 0)]
            acc = [jnp.zeros((SUB, L), F32)] * taps
            for r in range(pitch):
                w.append(p_slab[s, pl.ds(8 + r, SUB, stride=pitch), :])
                g = g_ref[s, n, pl.ds(r, SUB, stride=pitch), :]
                acc = [acc[j] + g * w[-1 - j] for j in range(taps)]
                w = w[1:]
            for j in range(taps):
                taps_ref[h, 8 * s + j:8 * s + j + 1, pl.ds(hcol, L)] = jnp.sum(acc[j], 0, keepdims=True)
            taps_ref[h, 8 * s + taps:8 * s + 8, pl.ds(hcol, L)] = jnp.zeros((8 - taps, L), F32)
        return carry
    lax.fori_loop(0, chans // L, group, 0)

def back_kernel(f_ref, g_ref, out_ref, o_slab):
    rows, columns = out_ref.shape
    chans = columns // 3
    taps = f_ref.shape[1]
    pitch = rows // SUB
    def group(n, carry):
        col = pl.multiple_of(n * L, L)
        for s in range(3):
            tap = [jnp.broadcast_to(f_ref[s, j:j + 1, pl.ds(col, L)], (SUB, L)) for j in range(taps)]
            w = [g_ref[s, n, pl.ds(r, SUB, stride=pitch), :] for r in range(taps - 1)]
            for r in range(pitch):
                w.append(g_ref[s, n, pl.ds(r + taps - 1, SUB, stride=pitch), :])
                o_slab[s, pl.ds(r, SUB, stride=pitch), :] = sum(tap[j] * w[j] for j in range(taps))
                w = w[1:]
            out_ref[:, pl.ds(pl.multiple_of(s * chans + n * L, L), L)] = o_slab[s].astype(BF)
        return carry
    lax.fori_loop(0, chans // L, group, 0)

V = pl.BlockSpec(memory_space=pltpu.VMEM)
def call_filter(p, u, f, prior, nxt):
    rows, columns = p.shape; chans = columns // 3
    return pl.pallas_call(filter_kernel,
        out_shape=(jax.ShapeDtypeStruct((rows, chans), BF), jax.ShapeDtypeStruct((3, chans // L, rows + 8, L), F32), jax.ShapeDtypeStruct((2, 24, chans // 2), F32)),
        in_specs=[V]*5, out_specs=(V, V, V),
        scratch_shapes=[pltpu.VMEM((3, rows + 16, L), F32), pltpu.VMEM((rows, L), F32), pltpu.VMEM((rows, L), F32)],
        cost_estimate=pl.CostEstimate(flops=2*2*7*rows*columns, bytes_accessed=2*rows*(columns+chans), transcendentals=0),
        compiler_params=pltpu.CompilerParams(vmem_limit_bytes=24*2**20), name="filter")(p, u, f, prior, nxt)
def call_back(f, g, rows, columns):
    return pl.pallas_call(back_kernel, out_shape=jax.ShapeDtypeStruct((rows, columns), BF),
        in_specs=[V]*2, out_specs=V, scratch_shapes=[pltpu.VMEM((3, rows, L), F32)],
        cost_estimate=pl.CostEstimate(flops=2*7*rows*columns, bytes_accessed=2*rows*columns, transcendentals=0),
        compiler_params=pltpu.CompilerParams(vmem_limit_bytes=24*2**20), name="back")(f, g)


def swap(array, partner):
    ways = lax.axis_size("seq")
    return lax.ppermute(array, "seq", [(i, partner(i)) for i in range(ways)])


def rims(projected, upstream):
    rows, columns = projected.shape
    chans = upstream.shape[1]
    ways = lax.axis_size("seq")
    me = lax.axis_index("seq")
    even = me % 2 == 0
    first = jnp.concatenate([projected[:RIM], upstream[:RIM]], 1)
    last = jnp.concatenate([projected[rows - RIM :], jnp.zeros((RIM, chans), BF)], 1)
    far = swap(jnp.where(even, first, last), lambda i: (((i + 1) % ways) ^ 1) - 1 if 0 < i < ways - 1 else ways - 1 - i)
    near = swap(jnp.where(even, last, first), lambda i: i ^ 1)
    before = jnp.where(even, far, near)[:, :columns]
    after = jnp.where(even, near, far)
    before = jnp.where(me == 0, jnp.zeros_like(before), before)
    after = jnp.where(me == ways - 1, jnp.zeros_like(after), after)
    return before, after


def total_over_seq(halves):
    ways = lax.axis_size("seq")
    me = lax.axis_index("seq")
    bits = ways.bit_length() - 1
    odd = sum((me >> b) & 1 for b in range(bits)) % 2 == 1
    mine = jnp.where(odd, halves[1], halves[0])
    other = jnp.where(odd, halves[0], halves[1])
    mine = mine + swap(other, lambda i: i ^ 1)
    for b in range(1, bits):
        sent = mine.astype(BF)
        mine = sent.astype(F32) + swap(sent, lambda i: i ^ (1 << b) ^ 1).astype(F32)
    other = swap(mine, lambda i: i ^ 1)
    return jnp.where(odd, other, mine), jnp.where(odd, mine, other)


def shards(projected, filters, upstream):
    rows, columns = projected.shape
    ways = lax.axis_size("seq")
    taps = filters.shape[1]
    chans = columns // 3
    before, after = rims(projected, upstream)
    gated, grad_conv, tap_grads = call_filter(projected, upstream, filters, before, after)
    low, high = total_over_seq(tap_grads)
    grad_projected = call_back(filters, grad_conv, rows, columns)
    total = jnp.concatenate([low, high], 1).reshape(3, 8, chans)[:, :taps]
    return gated, grad_projected, total * float(rows * ways) ** -0.5


def solution(mesh):
    placed = (P(("groups", "seq"), None), P(), P(("groups", "seq"), None))
    return jax.shard_map(
        shards,
        mesh=mesh,
        in_specs=placed,
        out_specs=(P(("groups", "seq"), None), P(("groups", "seq"), None), P("groups", None, None)),
        check_vma=False,
    )
```

time: 132 us -> 40.1 us (0.30)
  waiting for transfers between devices: 94.8 us -> 14.8 us
  other arithmetic: 14.9 us -> 0.88 us
  between operations: 14.1 us -> 0.74 us
  Pallas kernels: 0 us -> 11.5 us
  starting transfers between devices: 3.69 us -> 8.13 us
    psum x1 -> x0, waiting for transfers between devices: 90.8 us -> none  [shards(): total_taps = lax.psum(jnp.stack(tap_grads, 0), 'seq') * scale]
    pallas_call x0 -> x2, Pallas kernels: none -> 11.5 us  [the longest x1 7.9 us: call_filter(): pl.pallas_call(filter_kernel, out_shape=(jax.ShapeDtypeStruct((rows, chan...]
    ppermute x2 -> x7, waiting for transfers between devices: 4 us -> 14.8 us  [swap(): return lax.ppermute(array, 'seq', [(i, partner(i)) for i in range(ways)])]
    convert_element_type x3, other arithmetic: 5.72 us -> 0.05 us  [total_over_seq(): sent = mine.astype(BF)]
    ppermute x2 -> x7, starting transfers between devices: 3.65 us -> 8.13 us  [swap(): return lax.ppermute(array, 'seq', [(i, partner(i)) for i in range(ways)])]
    reduce_sum x1 -> x0, other arithmetic: 3.71 us -> none  [shards(): jnp.sum(grad_float * padded[rim_rows - tap_index:rim_rows - tap_index + t...]
    add x1, other arithmetic: 2.59 us -> 0.01 us  [total_over_seq(): mine = sent.astype(F32) + swap(sent, lambda i: i ^ 1 << b ^ 1).astype(F32)]
    unnamed x2 -> x6, local copies, waits for them, and re-layouts: 0.01 us -> 1.97 us
  transfers between devices with their start and end apart: 3 -> 7, of which waited for: 2 -> 5; matrix products, arithmetic and copies ran while one was open for 4% -> 0% of each run, Pallas kernels for 0% -> 9%
where the time goes in v1:
time: 40.1 us; the launch traced here: 39.9 us
  waiting for transfers between devices  14.8 us (37%)
  Pallas kernels  11.5 us (29%)
  starting transfers between devices  8.13 us (20%)
  local copies, waits for them, and re-layouts  3.8 us (9%)
  other arithmetic  0.88 us (2%)
  between operations  0.74 us (2%)
    ppermute x7, waiting for transfers between devices, swap(): return lax.ppermute(array, 'seq', [(i, partner(i)) for i in range(ways)])  14.8 us
    ppermute x7, starting transfers between devices, swap(): return lax.ppermute(array, 'seq', [(i, partner(i)) for i in range(ways)])  8.13 us
    pallas_call x1, Pallas kernels, call_filter(): pl.pallas_call(filter_kernel, out_shape=(jax.ShapeDtypeStruct((rows, chan...  7.9 us
    pallas_call x1, Pallas kernels, call_back(): pl.pallas_call(back_kernel, out_shape=jax.ShapeDtypeStruct((rows, columns...  3.62 us
    unnamed x6, local copies, waits for them, and re-layouts  1.97 us
    slice x2, local copies, waits for them, and re-layouts, rims(): first = jnp.concatenate([projected[:RIM], upstream[:RIM]], 1)  1.83 us
  transfers between devices with their start and end apart: 7, of which 5 were waited for; matrix products, arithmetic and copies ran while one was open for 0% of the time, Pallas kernels for 9%

profile of v1, /device:TPU:0, one launch (start us, length us, event | category | flops | bytes accessed | tf_op | source)
XLA Modules:
  0.0 39.9 jit_solution(1094945328085693205)
XLA Ops:
  0.6 0.0 copy-start
  0.7 0.9 %slice.24 = bf16[8,2048]{1,0:T(8,128)(2,1)S(1)} slice(bf16[128,2048]{1,0:T(8,128)(2,1)} %u_ref.1), slice={[0:8], [0:2048]} | slice | bytes 65536 | tf_op jit(solution)/shard_map/slice | solution.py:109
  1.5 1.0 %fusion.2 = (bf16[8,6144]{1,0:T(8,128)(2,1)S(1)}, bf16[8,6144]{1,0:T(8,128)(2,1)S(1)}) fusion(bf16[128,6144]{1,0:T(8,128)(2,1)} %p_ref.1), kind=kLoop, calls=%fused_computation.16 | loop fusion | bytes 393216 | tf_op jit(solution)/shard_map/slice | solution.py:109
  2.5 5.5 %collective-permute-start = (bf16[8,8192]{1,0:T(8,128)(2,1)S(1)}, bf16[8,8192]{1,0:T(8,128)(2,1)S(1)}, u32[]{:S(2)}, u32[]{:S(2)}) collective-permute-start(bf16[8,8192]{1,0:T(8,128)(2,1)S(1)} %get-tuple-element.11), channel_id=1, source_target_pairs={{0,15},{1,2},{2,1},{3,4},{4,3},{5,6},{6,5},{7,8},{8,7},{9,10},{10,... | collective-permute-start | bytes 393224 | tf_op jit(solution)/shard_map/ppermute | solution.py:100
  8.0 0.0 collective-permute-start.1
  8.0 2.6 %collective-permute-done = bf16[8,8192]{1,0:T(8,128)(2,1)S(1)} collective-permute-done((bf16[8,8192]{1,0:T(8,128)(2,1)S(1)}, bf16[8,8192]{1,0:T(8,128)(2,1)S(1)}, u32[]{:S(2)}, u32[]{:S(2)}) %collective-permute-start) | collective-permute-done | bytes 131104 | tf_op jit(solution)/shard_map/ppermute | solution.py:100
  10.7 0.0 collective-permute-done.1
  10.7 0.0 copy-done
  10.7 0.0 copy-start.1
  10.7 0.9 %copy-done.1 = f32[3,7,2048]{2,1,0:T(8,128)S(1)} copy-done((f32[3,7,2048]{2,1,0:T(8,128)S(1)}, f32[3,7,2048]{2,1,0:T(8,128)}, u32[]{:S(2)}) %copy-start.1) | copy-done | bytes 172056
  11.7 0.0 copy-start.2
  11.7 1.0 %copy-done.2 = bf16[128,2048]{1,0:T(8,128)(2,1)S(1)} copy-done((bf16[128,2048]{1,0:T(8,128)(2,1)S(1)}, bf16[128,2048]{1,0:T(8,128)(2,1)}, u32[]{:S(2)}) %copy-start.2) | copy-done | bytes 524312
  12.7 7.9 %filter.1 = (bf16[128,2048]{1,0:T(8,128)(2,1)}, f32[3,16,136,128]{3,2,1,0:T(8,128)S(1)}, f32[2,24,1024]{2,1,0:T(8,128)S(1)}) custom-call(bf16[128,6144]{1,0:T(8,128)(2,1)S(1)} %copy-done, bf16[128,2048]{1,0:T(8,128)(2,1)S(1)} %copy-done.2, f32[3,7,2048]{2,1,0:T(8,128)S(1)} %copy-done.1, bf16[8,6144]{1,0:T(8,128)(2,1)S(1)} %fusion.prior_ref, ...), custom_call_target="tpu_custom_call" | custom-call | flops 22020096 | bytes 2097152 | tf_op jit(solution)/shard_map/filter/pallas_call | solution.py:85
  20.6 0.1 collective-permute-start.2
  20.7 1.3 %collective-permute-done.2 = f32[24,1024]{1,0:T(8,128)S(1)} collective-permute-done((f32[24,1024]{1,0:T(8,128)S(1)}, f32[24,1024]{1,0:T(8,128)S(1)}, u32[]{:S(2)}, u32[]{:S(2)}) %collective-permute-start.2) | collective-permute-done | bytes 98336 | tf_op jit(solution)/shard_map/ppermute | solution.py:100
  22.0 0.5 %collective-permute-start.3 = (bf16[24,1024]{1,0:T(8,128)(2,1)S(1)}, bf16[24,1024]{1,0:T(8,128)(2,1)S(1)}, u32[]{:S(2)}, u32[]{:S(2)}) collective-permute-start(bf16[24,1024]{1,0:T(8,128)(2,1)S(1)} %fusion.1), channel_id=1, source_target_pairs={{0,3},{1,2},{2,1},{3,0},{4,7},{5,6},{6,5},{7,4},{8,11},{9,10},{10,... | collective-permute-start | bytes 147464 | tf_op jit(solution)/shard_map/ppermute | solution.py:100
  22.5 3.3 %collective-permute-done.3 = bf16[24,1024]{1,0:T(8,128)(2,1)S(1)} collective-permute-done((bf16[24,1024]{1,0:T(8,128)(2,1)S(1)}, bf16[24,1024]{1,0:T(8,128)(2,1)S(1)}, u32[]{:S(2)}, u32[]{:S(2)}) %collective-permute-start.3) | collective-permute-done | bytes 49184 | tf_op jit(solution)/shard_map/ppermute | solution.py:100
  25.8 0.2 collective-permute-start.4
  26.0 3.6 %collective-permute-done.4 = bf16[24,1024]{1,0:T(8,128)(2,1)S(1)} collective-permute-done((bf16[24,1024]{1,0:T(8,128)(2,1)S(1)}, bf16[24,1024]{1,0:T(8,128)(2,1)S(1)}, u32[]{:S(2)}, u32[]{:S(2)}) %collective-permute-start.4) | collective-permute-done | bytes 49184 | tf_op jit(solution)/shard_map/ppermute | solution.py:100
  29.6 1.7 %collective-permute-start.5 = (bf16[24,1024]{1,0:T(8,128)(2,1)S(1)}, bf16[24,1024]{1,0:T(8,128)(2,1)S(1)}, u32[]{:S(2)}, u32[]{:S(2)}) collective-permute-start(bf16[24,1024]{1,0:T(8,128)(2,1)S(1)} %add_convert_fusion), channel_id=1, source_target_pairs={{0,9},{1,8},{2,11},{3,10},{4,13},{5,12},{6,15},{7,14},{8,1},{9,0},... | collective-permute-start | bytes 147464 | tf_op jit(solution)/shard_map/ppermute | solution.py:100
  31.3 4.0 %collective-permute-done.5 = bf16[24,1024]{1,0:T(8,128)(2,1)S(1)} collective-permute-done((bf16[24,1024]{1,0:T(8,128)(2,1)S(1)}, bf16[24,1024]{1,0:T(8,128)(2,1)S(1)}, u32[]{:S(2)}, u32[]{:S(2)}) %collective-permute-start.5) | collective-permute-done | bytes 49184 | tf_op jit(solution)/shard_map/ppermute | solution.py:100
  35.3 0.2 collective-permute-start.6
  35.6 3.6 %back.1 = bf16[128,6144]{1,0:T(8,128)(2,1)} custom-call(f32[3,7,2048]{2,1,0:T(8,128)S(1)} %copy-done.1, f32[3,16,136,128]{3,2,1,0:T(8,128)S(1)} %get-tuple-element.7.g_ref), custom_call_target="tpu_custom_call" | custom-call | flops 11010048 | bytes 1572864 | tf_op jit(solution)/shard_map/back/pallas_call | solution.py:92
  39.2 0.0 collective-permute-done.6
  39.2 0.7 %slice_multiply_fusion = f32[3,7,2048]{2,1,0:T(8,128)} fusion(f32[3,8,2048]{2,1,0:T(8,128)S(1)} %maximum_bitcast_fusion), kind=kLoop, calls=%fused_computation | loop fusion | flops 43008 | bytes 344064 | tf_op jit(solution)/shard_map/mul | solution.py:145
  (10 shorter events, 0.2 us)
Async XLA Ops:
  0.6 10.1 %copy-start = (bf16[128,6144]{1,0:T(8,128)(2,1)S(1)}, bf16[128,6144]{1,0:T(8,128)(2,1)}, u32[]{:S(2)}) copy-start(bf16[128,6144]{1,0:T(8,128)(2,1)} %p_ref.1) | copy-start | bytes 4718596
  2.5 8.1 %collective-permute-start = (bf16[8,8192]{1,0:T(8,128)(2,1)S(1)}, bf16[8,8192]{1,0:T(8,128)(2,1)S(1)}, u32[]{:S(2)}, u32[]{:S(2)}) collective-permute-start(bf16[8,8192]{1,0:T(8,128)(2,1)S(1)} %get-tuple-element.11), channel_id=1, source_target_pairs={{0,15},{1,2},{2,1},{3,4},{4,3},{5,6},{6,5},{7,8},{8,7},{9,10},{10,... | collective-permute-start | bytes 393224 | tf_op jit(solution)/shard_map/ppermute | solution.py:100
  8.0 2.7 %collective-permute-start.1 = (bf16[8,8192]{1,0:T(8,128)(2,1)S(1)}, bf16[8,8192]{1,0:T(8,128)(2,1)S(1)}, u32[]{:S(2)}, u32[]{:S(2)}) collective-permute-start(bf16[8,8192]{1,0:T(8,128)(2,1)S(1)} %get-tuple-element.12), channel_id=1, source_target_pairs={{0,1},{1,0},{2,3},{3,2},{4,5},{5,4},{6,7},{7,6},{8,9},{9,8},{10,11... | collective-permute-start | bytes 393224 | tf_op jit(solution)/shard_map/ppermute | solution.py:100
  10.7 0.9 %copy-start.1 = (f32[3,7,2048]{2,1,0:T(8,128)S(1)}, f32[3,7,2048]{2,1,0:T(8,128)}, u32[]{:S(2)}) copy-start(f32[3,7,2048]{2,1,0:T(8,128)} %f_ref.3) | copy-start | bytes 516100
  11.7 1.0 %copy-start.2 = (bf16[128,2048]{1,0:T(8,128)(2,1)S(1)}, bf16[128,2048]{1,0:T(8,128)(2,1)}, u32[]{:S(2)}) copy-start(bf16[128,2048]{1,0:T(8,128)(2,1)} %u_ref.1) | copy-start | bytes 1572868
  20.6 1.4 %collective-permute-start.2 = (f32[24,1024]{1,0:T(8,128)S(1)}, f32[24,1024]{1,0:T(8,128)S(1)}, u32[]{:S(2)}, u32[]{:S(2)}) collective-permute-start(f32[24,1024]{1,0:T(8,128)S(1)} %select_bitcast_fusion), channel_id=1, source_target_pairs={{0,1},{1,0},{2,3},{3,2},{4,5},{5,4},{6,7},{7,6},{8,9},{9,8},{10,11... | collective-permute-start | bytes 294920 | tf_op jit(solution)/shard_map/ppermute | solution.py:100
  22.0 3.8 %collective-permute-start.3 = (bf16[24,1024]{1,0:T(8,128)(2,1)S(1)}, bf16[24,1024]{1,0:T(8,128)(2,1)S(1)}, u32[]{:S(2)}, u32[]{:S(2)}) collective-permute-start(bf16[24,1024]{1,0:T(8,128)(2,1)S(1)} %fusion.1), channel_id=1, source_target_pairs={{0,3},{1,2},{2,1},{3,0},{4,7},{5,6},{6,5},{7,4},{8,11},{9,10},{10,... | collective-permute-start | bytes 147464 | tf_op jit(solution)/shard_map/ppermute | solution.py:100
  25.8 3.8 %collective-permute-start.4 = (bf16[24,1024]{1,0:T(8,128)(2,1)S(1)}, bf16[24,1024]{1,0:T(8,128)(2,1)S(1)}, u32[]{:S(2)}, u32[]{:S(2)}) collective-permute-start(bf16[24,1024]{1,0:T(8,128)(2,1)S(1)} %add_convert_fusion.1), channel_id=1, source_target_pairs={{0,5},{1,4},{2,7},{3,6},{4,1},{5,0},{6,3},{7,2},{8,13},{9,12},{10,... | collective-permute-start | bytes 147464 | tf_op jit(solution)/shard_map/ppermute | solution.py:100
  29.6 5.7 %collective-permute-start.5 = (bf16[24,1024]{1,0:T(8,128)(2,1)S(1)}, bf16[24,1024]{1,0:T(8,128)(2,1)S(1)}, u32[]{:S(2)}, u32[]{:S(2)}) collective-permute-start(bf16[24,1024]{1,0:T(8,128)(2,1)S(1)} %add_convert_fusion), channel_id=1, source_target_pairs={{0,9},{1,8},{2,11},{3,10},{4,13},{5,12},{6,15},{7,14},{8,1},{9,0},... | collective-permute-start | bytes 147464 | tf_op jit(solution)/shard_map/ppermute | solution.py:100
  35.3 3.8 %collective-permute-start.6 = (f32[24,1024]{1,0:T(8,128)S(1)}, f32[24,1024]{1,0:T(8,128)S(1)}, u32[]{:S(2)}, u32[]{:S(2)}) collective-permute-start(f32[24,1024]{1,0:T(8,128)S(1)} %convert_add_fusion), channel_id=1, source_target_pairs={{0,1},{1,0},{2,3},{3,2},{4,5},{5,4},{6,7},{7,6},{8,9},{9,8},{10,11... | collective-permute-start | bytes 294920 | tf_op jit(solution)/shard_map/ppermute | solution.py:100

commit v2 on v0

v2 whole, which is shorter than its diff:
```python
import jax
import jax.numpy as jnp
from jax import lax
from jax.experimental import pallas as pl
from jax.experimental.pallas import tpu as pltpu
from jax.sharding import PartitionSpec as P

F32 = jnp.float32
BF = jnp.bfloat16
LANES = 128
SUB = 8
RIM = 8
VMEM = pl.BlockSpec(memory_space=pltpu.VMEM)
UNROLL = 4


def lanes_at(start):
    return pl.ds(pl.multiple_of(start, LANES), LANES)


def tap_rows(filters, s, n):
    return [
        jnp.broadcast_to(filters[s, j : j + 1, lanes_at(n * LANES)], (SUB, LANES))
        for j in range(filters.shape[1])
    ]


def convolve(tap, slab, s, start):
    return sum(tap[s][j] * slab[s, start - j : start - j + SUB, :] for j in range(len(tap[s])))


def gates(query, key, value, cotangent):
    product = key * value
    scaled = cotangent * query
    grads = (cotangent * product, scaled * value, scaled * key)
    return query * product, [g.astype(BF).astype(F32) for g in grads]


def inner_kernel(p_ref, u_ref, filters, gated, grads, sums, p_slab, u_slab):
    rows, columns = p_ref.shape
    chans = columns // 3
    taps = filters.shape[1]

    def group(n, carry):
        for s in range(3):
            p_slab[s] = p_ref[:, lanes_at(s * chans + n * LANES)].astype(F32)
        u_slab[...] = u_ref[:, lanes_at(n * LANES)].astype(F32)
        tap = [tap_rows(filters, s, n) for s in range(3)]
        for r in range(RIM, rows, SUB):
            conv = [convolve(tap, p_slab, s, r) for s in range(3)]
            product, grad = gates(*conv, u_slab[r : r + SUB, :])
            gated[n, r : r + SUB, :] = product
            for s in range(3):
                grads[s, n, r : r + SUB, :] = grad[s]
        for s in range(3):
            acc = [None] * taps
            for r in range(RIM, rows, SUB):
                grad = grads[s, n, r : r + SUB, :]
                for j in range(taps):
                    term = grad * p_slab[s, r - j : r - j + SUB, :]
                    acc[j] = term if r == RIM else acc[j] + term
            for j in range(taps):
                sums[n, s, j] = acc[j]
        return carry

    lax.fori_loop(0, chans // LANES, group, 0, unroll=UNROLL)


def fold(arrays):
    sub = lax.broadcasted_iota(jnp.int32, (SUB, LANES), 0)
    arrays = arrays + [jnp.zeros((SUB, LANES), F32)] * (SUB - len(arrays))
    step = 1
    while step < SUB:
        low = (sub & step) == 0
        arrays = [
            jnp.where(low, a, b) + pltpu.roll(jnp.where(low, b, a), SUB - step, 0)
            for a, b in zip(arrays[::2], arrays[1::2])
        ]
        step *= 2
    return arrays[0]


def rim_kernel(p_ref, u_ref, filters, before, after, sums, gated, head, following, totals, slab):
    rows, columns = p_ref.shape
    chans = columns // 3
    taps = filters.shape[1]
    half = chans // 2 // LANES

    def group(n, carry):
        for s in range(3):
            c = lanes_at(s * chans + n * LANES)
            slab[s, 0:RIM, :] = before[:, c].astype(F32)
            slab[s, RIM : RIM + 16, :] = p_ref[0:16, c].astype(F32)
            slab[s, RIM + 16 : RIM + 32, :] = p_ref[rows - 16 : rows, c].astype(F32)
            slab[s, RIM + 32 : RIM + 40, :] = after[:, c].astype(F32)
        tap = [tap_rows(filters, s, n) for s in range(3)]
        conv = [convolve(tap, slab, s, RIM + 32) for s in range(3)]
        _, grad = gates(*conv, after[:, lanes_at(columns + n * LANES)].astype(F32))
        for s in range(3):
            following[s, n] = grad[s]
        conv = [convolve(tap, slab, s, RIM) for s in range(3)]
        product, grad = gates(*conv, u_ref[0:16, lanes_at(n * LANES)].astype(F32)[0:RIM])
        gated[n] = product
        c = lanes_at(lax.rem(n, half) * LANES)
        for s in range(3):
            head[s, n] = grad[s]
            acc = [sums[n, s, j] + grad[s] * slab[s, RIM - j : RIM - j + SUB, :] for j in range(taps)]
            totals[n // half, s * SUB : s * SUB + SUB, c] = fold(acc)
        return carry

    lax.fori_loop(0, chans // LANES, group, 0, unroll=UNROLL)


def back_kernel(filters, gated_in, grads, gated_head, head, following, gated, out, slab):
    rows, columns = out.shape
    chans = columns // 3
    taps = filters.shape[1]

    def group(n, carry):
        c = lanes_at(n * LANES)
        gated[0:16, c] = jnp.concatenate([gated_head[n], gated_in[n, RIM:16, :]], 0).astype(BF)
        gated[16:rows, c] = gated_in[n, 16:rows, :].astype(BF)
        for s in range(3):
            tap = tap_rows(filters, s, n)
            slab[s, 0:RIM, :] = head[s, n]
            slab[s, RIM : 2 * RIM, :] = grads[s, n, RIM : 2 * RIM, :]
            slab[s, 2 * RIM : 3 * RIM, :] = grads[s, n, rows - RIM : rows, :]
            slab[s, 3 * RIM : 4 * RIM, :] = following[s, n]
            result = []
            for r in range(0, rows, SUB):
                if r == 0:
                    terms = [tap[j] * slab[s, j : j + SUB, :] for j in range(taps)]
                elif r == rows - SUB:
                    terms = [tap[j] * slab[s, 2 * RIM + j : 2 * RIM + j + SUB, :] for j in range(taps)]
                else:
                    terms = [tap[j] * grads[s, n, r + j : r + j + SUB, :] for j in range(taps)]
                result.append(sum(terms))
                if r % 16 == SUB:
                    out[r - SUB : r + SUB, lanes_at(s * chans + n * LANES)] = jnp.concatenate(result, 0).astype(BF)
                    result = []
        return carry

    lax.fori_loop(0, chans // LANES, group, 0, unroll=UNROLL)


def params(**kw):
    return pltpu.CompilerParams(vmem_limit_bytes=28 * 2**20, **kw)


def call_inner(projected, upstream, filters):
    rows, columns = projected.shape
    chans = columns // 3
    groups = chans // LANES
    taps = filters.shape[1]
    return pl.pallas_call(
        inner_kernel,
        out_shape=(
            jax.ShapeDtypeStruct((groups, rows, LANES), F32),
            jax.ShapeDtypeStruct((3, groups, rows, LANES), F32),
            jax.ShapeDtypeStruct((groups, 3, taps, SUB, LANES), F32),
        ),
        in_specs=[VMEM] * 3,
        out_specs=(VMEM,) * 3,
        scratch_shapes=[pltpu.VMEM((3, rows, LANES), F32), pltpu.VMEM((rows, LANES), F32)],
        cost_estimate=pl.CostEstimate(flops=4 * taps * rows * columns, bytes_accessed=2 * rows * (columns + chans), transcendentals=0),
        compiler_params=params(),
        name="inner",
    )(projected, upstream, filters)


def call_rim(projected, upstream, filters, before, after, sums):
    chans = upstream.shape[1]
    groups = chans // LANES
    return pl.pallas_call(
        rim_kernel,
        out_shape=(
            jax.ShapeDtypeStruct((groups, RIM, LANES), F32),
            jax.ShapeDtypeStruct((3, groups, RIM, LANES), F32),
            jax.ShapeDtypeStruct((3, groups, RIM, LANES), F32),
            jax.ShapeDtypeStruct((2, 3 * SUB, chans // 2), F32),
        ),
        in_specs=[VMEM] * 6,
        out_specs=(VMEM,) * 4,
        scratch_shapes=[pltpu.VMEM((3, 6 * RIM, LANES), F32)],
        compiler_params=params(),
        name="rim",
    )(projected, upstream, filters, before, after, sums)


def call_back(filters, gated, grads, gated_head, head, following):
    taps = filters.shape[1]
    groups, rows, _ = gated.shape
    chans = groups * LANES
    return pl.pallas_call(
        back_kernel,
        out_shape=(jax.ShapeDtypeStruct((rows, chans), BF), jax.ShapeDtypeStruct((rows, 3 * chans), BF)),
        in_specs=[VMEM] * 6,
        out_specs=(VMEM,) * 2,
        scratch_shapes=[pltpu.VMEM((3, 4 * RIM, LANES), F32)],
        cost_estimate=pl.CostEstimate(flops=6 * taps * rows * chans, bytes_accessed=8 * rows * chans, transcendentals=0),
        compiler_params=params(),
        name="back",
    )(filters, gated, grads, gated_head, head, following)

def rounds(bits):
    return [[(1 << b) ^ 1] for b in reversed(range(3, bits))] + [[m for m in (3, 5, 6) if m < 1 << bits]]


def pack_kernel(head, tail, u_head, near, far):
    columns = head.shape[1]
    forward_near = lax.rem(lax.axis_index("seq"), 2) == 0

    first = head[...].astype(F32)[:RIM]
    last = tail[...].astype(F32)[16 - RIM :]
    near[:, :columns] = jnp.where(forward_near, last, first).astype(BF)
    far[:, :columns] = jnp.where(forward_near, first, last).astype(BF)
    cotangent = u_head[...].astype(F32)[:RIM].astype(BF)
    near[:, columns:] = cotangent
    far[:, columns:] = cotangent


def call_pack(projected, upstream):
    rows, columns = projected.shape
    chans = upstream.shape[1]
    shape = jax.ShapeDtypeStruct((RIM, columns + chans), BF)
    return pl.pallas_call(
        pack_kernel,
        grid=(1,),
        out_shape=(shape, shape),
        in_specs=[
            pl.BlockSpec((16, columns), lambda _: (0, 0)),
            pl.BlockSpec((16, columns), lambda _: (rows // 16 - 1, 0)),
            pl.BlockSpec((16, chans), lambda _: (0, 0)),
        ],
        out_specs=(VMEM,) * 2,
        name="pack",
    )(projected, projected, upstream)


def swap(array, partner):
    ways = lax.axis_size("seq")
    return lax.ppermute(array, "seq", [(i, partner(i)) for i in range(ways)])


def rims(projected, upstream):
    columns = projected.shape[1]
    ways = lax.axis_size("seq")
    me = lax.axis_index("seq")
    even = me % 2 == 0
    near, far = call_pack(projected, upstream)
    far = swap(far, lambda i: ways - 1 - i if i in (0, ways - 1) else ((i + 1) ^ 1) - 1)
    near = swap(near, lambda i: i ^ 1)
    before = jnp.where(even, far, near)[:, :columns]
    after = jnp.where(even, near, far)
    before = jnp.where(me == 0, jnp.zeros_like(before), before)
    after = jnp.where(me == ways - 1, jnp.zeros_like(after), after)
    return before, after


def shards(projected, filters, upstream):
    rows, columns = projected.shape
    ways = lax.axis_size("seq")
    me = lax.axis_index("seq")
    taps = filters.shape[1]
    chans = columns // 3
    before, after = rims(projected, upstream)
    gated, grads, sums = call_inner(projected, upstream, filters)
    *edges, halves = call_rim(projected, upstream, filters, before, after, sums)
    bits = ways.bit_length() - 1
    odd = sum((me >> b) & 1 for b in range(bits)) % 2 == 1
    mine = jnp.where(odd, halves[1], halves[0])
    mine = mine + swap(jnp.where(odd, halves[0], halves[1]), lambda i: i ^ 1)
    for step, masks in enumerate(rounds(bits)):
        sent = mine.astype(BF)
        if step == 0:
            sent, grads = lax.optimization_barrier((sent, grads))
        got = [swap(sent, lambda i: i ^ m) for m in masks]
        if step == 0:
            gated, grad_projected = call_back(filters, gated, grads, *edges)
            got, gated, grad_projected = lax.optimization_barrier((got, gated, grad_projected))
        terms = [sent.astype(F32)] + [g.astype(F32) for g in got]
        while len(terms) > 1:
            terms = [sum(terms[k : k + 2]) for k in range(0, len(terms), 2)]
        mine = terms[0]
    other = swap(mine, lambda i: i ^ 1)
    total = jnp.concatenate([jnp.where(odd, other, mine), jnp.where(odd, mine, other)], 1)
    total = total.reshape(3, SUB, chans)[:, :taps] * float(rows * ways) ** -0.5
    return gated, grad_projected, total


def solution(mesh):
    placed = (P(("groups", "seq"), None), P(), P(("groups", "seq"), None))
    return jax.shard_map(
        shards,
        mesh=mesh,
        in_specs=placed,
        out_specs=(P(("groups", "seq"), None), P(("groups", "seq"), None), P("groups", None, None)),
        check_vma=False,
    )
```

time: 132 us -> 27.4 us (0.21)
  waiting for transfers between devices: 94.8 us -> 6.76 us
  other arithmetic: 14.9 us -> 0.83 us
  between operations: 14.1 us -> 0.75 us
  Pallas kernels: 0 us -> 9.3 us
  starting transfers between devices: 3.69 us -> 9.61 us
  local copies, waits for them, and re-layouts: 4.49 us -> 0.01 us
    psum x1 -> x0, waiting for transfers between devices: 90.8 us -> none  [shards(): total_taps = lax.psum(jnp.stack(tap_grads, 0), 'seq') * scale]
    pallas_call x0 -> x4, Pallas kernels: none -> 9.3 us  [the longest x1 3.79 us: call_inner(): pl.pallas_call(inner_kernel, out_shape=(jax.ShapeDtypeStruct((groups, row...]
    ppermute x2 -> x8, starting transfers between devices: 3.65 us -> 9.61 us  [swap(): return lax.ppermute(array, 'seq', [(i, partner(i)) for i in range(ways)])]
    convert_element_type x3 -> x2, other arithmetic: 5.72 us -> 0.03 us  [shards(): sent = mine.astype(BF)]
    reduce_sum x1 -> x0, other arithmetic: 3.71 us -> none  [shards(): jnp.sum(grad_float * padded[rim_rows - tap_index:rim_rows - tap_index + t...]
    ppermute x2 -> x8, waiting for transfers between devices: 4 us -> 6.76 us  [swap(): return lax.ppermute(array, 'seq', [(i, partner(i)) for i in range(ways)])]
    slice x2 -> x0, local copies, waits for them, and re-layouts: 2.75 us -> none  [the longest x1 1.83 us: filter_rows(): tap_table[tap_index]]
    add x1, other arithmetic: 2.59 us -> 0.03 us  [shards(): terms = [sum(terms[k:k + 2]) for k in range(0, len(terms), 2)]]
  transfers between devices with their start and end apart: 3 -> 8, of which waited for: 2 -> 6; matrix products, arithmetic and copies ran while one was open for 4% -> 0% of each run, Pallas kernels for 0% -> 25%
where the time goes in v2:
time: 27.4 us; the launch traced here: 27.3 us
  starting transfers between devices  9.61 us (35%)
  Pallas kernels  9.3 us (34%)
  waiting for transfers between devices  6.76 us (25%)
  other arithmetic  0.83 us (3%)
  between operations  0.75 us (3%)
    ppermute x8, starting transfers between devices, swap(): return lax.ppermute(array, 'seq', [(i, partner(i)) for i in range(ways)])  9.61 us
    ppermute x8, waiting for transfers between devices, swap(): return lax.ppermute(array, 'seq', [(i, partner(i)) for i in range(ways)])  6.76 us
    pallas_call x1, Pallas kernels, call_inner(): pl.pallas_call(inner_kernel, out_shape=(jax.ShapeDtypeStruct((groups, row...  3.79 us
    pallas_call x1, Pallas kernels, call_back(): pl.pallas_call(back_kernel, out_shape=(jax.ShapeDtypeStruct((rows, chans)...  2.93 us
    pallas_call x1, Pallas kernels, call_pack(): pl.pallas_call(pack_kernel, grid=(1,), out_shape=(shape, shape), in_specs...  1.91 us
    mul x1, other arithmetic, shards(): total.reshape(3, SUB, chans)[:, :taps] * float(rows * ways) ** (-0.5)  0.7 us
    pallas_call x1, Pallas kernels, call_rim(): pl.pallas_call(rim_kernel, out_shape=(jax.ShapeDtypeStruct((groups, RIM,...  0.67 us
  transfers between devices with their start and end apart: 8, of which 6 were waited for; matrix products, arithmetic and copies ran while one was open for 0% of the time, Pallas kernels for 25%

profile of v2, /device:TPU:0, one launch (start us, length us, event | category | flops | bytes accessed | tf_op | source)
XLA Modules:
  0.0 27.3 jit_solution(12315898433314504969)
XLA Ops:
  0.6 0.0 copy-start.1
  0.6 0.0 copy-start
  0.7 0.0 copy-start.2
  0.7 1.9 %pack.1 = (bf16[8,8192]{1,0:T(8,128)(2,1)}, bf16[8,8192]{1,0:T(8,128)(2,1)}) custom-call(bf16[128,6144]{1,0:T(8,128)(2,1)} %p_ref.3, bf16[128,6144]{1,0:T(8,128)(2,1)} %p_ref.3, bf16[128,2048]{1,0:T(8,128)(2,1)} %u_ref.3), custom_call_target="tpu_custom_call" | custom-call | tf_op jit(solution)/shard_map/pack/pallas_call | solution.py:226
  2.6 5.4 %collective-permute-start = (bf16[8,8192]{1,0:T(8,128)(2,1)}, bf16[8,8192]{1,0:T(8,128)(2,1)S(1)}, u32[]{:S(2)}, u32[]{:S(2)}) collective-permute-start(bf16[8,8192]{1,0:T(8,128)(2,1)} %get-tuple-element.19), channel_id=1, source_target_pairs={{0,15},{1,2},{2,1},{3,4},{4,3},{5,6},{6,5},{7,8},{8,7},{9,10},{10,... | collective-permute-start | bytes 393224 | tf_op jit(solution)/shard_map/ppermute | solution.py:242
  8.0 0.0 collective-permute-start.1
  8.0 0.0 copy-done.1
  8.0 0.0 copy-done
  8.0 0.0 copy-done.2
  8.0 3.8 %inner.1 = (f32[16,128,128]{2,1,0:T(8,128)S(1)}, f32[3,16,128,128]{3,2,1,0:T(8,128)S(1)}, f32[16,3,7,8,128]{4,3,2,1,0:T(8,128)S(1)}) custom-call(bf16[128,6144]{1,0:T(8,128)(2,1)S(1)} %copy-done, bf16[128,2048]{1,0:T(8,128)(2,1)S(1)} %copy-done.1, f32[3,7,2048]{2,1,0:T(8,128)S(1)} %copy-done.2), custom_call_target="tpu_custom_call" | custom-call | flops 22020096 | bytes 2097152 | tf_op jit(solution)/shard_map/inner/pallas_call | solution.py:155
  11.8 0.0 collective-permute-done
  11.8 0.0 collective-permute-done.1
  11.9 0.7 %rim.1 = (f32[16,8,128]{2,1,0:T(8,128)S(1)}, f32[3,16,8,128]{3,2,1,0:T(8,128)S(1)}, f32[3,16,8,128]{3,2,1,0:T(8,128)S(1)}, f32[2,24,1024]{2,1,0:T(8,128)S(1)}) custom-call(bf16[128,6144]{1,0:T(8,128)(2,1)S(1)} %copy-done, bf16[128,2048]{1,0:T(8,128)(2,1)S(1)} %copy-done.1, f32[3,7,2048]{2,1,0:T(8,128)S(1)} %copy-done.2, bf16[8,6144]{1,0:T(8,128)(2,1)S(1)} %fusion.before, ...), custom_call_target="tpu_custom_call" | custom-call | tf_op jit(solution)/shard_map/rim/pallas_call | solution.py:174
  12.6 0.6 %collective-permute-start.2 = (f32[24,1024]{1,0:T(8,128)S(1)}, f32[24,1024]{1,0:T(8,128)S(1)}, u32[]{:S(2)}, u32[]{:S(2)}) collective-permute-start(f32[24,1024]{1,0:T(8,128)S(1)} %select_bitcast_fusion), channel_id=1, source_target_pairs={{0,1},{1,0},{2,3},{3,2},{4,5},{5,4},{6,7},{7,6},{8,9},{9,8},{10,11... | collective-permute-start | bytes 294920 | tf_op jit(solution)/shard_map/ppermute | solution.py:242
  13.1 0.9 %collective-permute-done.2 = f32[24,1024]{1,0:T(8,128)S(1)} collective-permute-done((f32[24,1024]{1,0:T(8,128)S(1)}, f32[24,1024]{1,0:T(8,128)S(1)}, u32[]{:S(2)}, u32[]{:S(2)}) %collective-permute-start.2) | collective-permute-done | bytes 98336 | tf_op jit(solution)/shard_map/ppermute | solution.py:242
  14.1 0.2 collective-permute-start.3
  14.3 2.9 %back.1 = (bf16[128,2048]{1,0:T(8,128)(2,1)}, bf16[128,6144]{1,0:T(8,128)(2,1)}) custom-call(f32[3,7,2048]{2,1,0:T(8,128)S(1)} %copy-done.2, f32[16,128,128]{2,1,0:T(8,128)S(1)} %get-tuple-element.25.gated_in, f32[3,16,128,128]{3,2,1,0:T(8,128)S(1)} %get-tuple-element.26.grads, f32[16,8,128]{2,1,0:T(8,128)S(1)} %get-tuple-element.27.gated_head, ...), custom_call_target="tpu_custom_call" | custom-call | flops 11010048 | bytes 2097152 | tf_op jit(solution)/shard_map/back/pallas_call | solution.py:194
  17.2 1.4 %collective-permute-done.3 = bf16[24,1024]{1,0:T(8,128)(2,1)S(1)} collective-permute-done((bf16[24,1024]{1,0:T(8,128)(2,1)S(1)}, bf16[24,1024]{1,0:T(8,128)(2,1)S(1)}, u32[]{:S(2)}, u32[]{:S(2)}) %collective-permute-start.3) | collective-permute-done | bytes 49184 | tf_op jit(solution)/shard_map/ppermute | solution.py:242
  18.6 2.5 %collective-permute-start.6 = (bf16[24,1024]{1,0:T(8,128)(2,1)S(1)}, bf16[24,1024]{1,0:T(8,128)(2,1)S(1)}, u32[]{:S(2)}, u32[]{:S(2)}) collective-permute-start(bf16[24,1024]{1,0:T(8,128)(2,1)S(1)} %add_convert_fusion), channel_id=1, source_target_pairs={{0,6},{1,7},{2,4},{3,5},{4,2},{5,3},{6,0},{7,1},{8,14},{9,15},{10,... | collective-permute-start | bytes 147464 | tf_op jit(solution)/shard_map/ppermute | solution.py:242
  21.1 0.0 collective-permute-start.5
  21.1 0.8 %collective-permute-start.4 = (bf16[24,1024]{1,0:T(8,128)(2,1)S(1)}, bf16[24,1024]{1,0:T(8,128)(2,1)S(1)}, u32[]{:S(2)}, u32[]{:S(2)}) collective-permute-start(bf16[24,1024]{1,0:T(8,128)(2,1)S(1)} %add_convert_fusion), channel_id=1, source_target_pairs={{0,3},{1,2},{2,1},{3,0},{4,7},{5,6},{6,5},{7,4},{8,11},{9,10},{10,... | collective-permute-start | bytes 147464 | tf_op jit(solution)/shard_map/ppermute | solution.py:242
  21.9 2.2 %collective-permute-done.6 = bf16[24,1024]{1,0:T(8,128)(2,1)S(1)} collective-permute-done((bf16[24,1024]{1,0:T(8,128)(2,1)S(1)}, bf16[24,1024]{1,0:T(8,128)(2,1)S(1)}, u32[]{:S(2)}, u32[]{:S(2)}) %collective-permute-start.6) | collective-permute-done | bytes 49184 | tf_op jit(solution)/shard_map/ppermute | solution.py:242
  24.1 0.9 %collective-permute-done.5 = bf16[24,1024]{1,0:T(8,128)(2,1)S(1)} collective-permute-done((bf16[24,1024]{1,0:T(8,128)(2,1)S(1)}, bf16[24,1024]{1,0:T(8,128)(2,1)S(1)}, u32[]{:S(2)}, u32[]{:S(2)}) %collective-permute-start.5) | collective-permute-done | bytes 49184 | tf_op jit(solution)/shard_map/ppermute | solution.py:242
  25.0 0.1 collective-permute-done.4
  25.2 0.2 collective-permute-start.7
  25.3 1.2 %collective-permute-done.7 = f32[24,1024]{1,0:T(8,128)S(1)} collective-permute-done((f32[24,1024]{1,0:T(8,128)S(1)}, f32[24,1024]{1,0:T(8,128)S(1)}, u32[]{:S(2)}, u32[]{:S(2)}) %collective-permute-start.7) | collective-permute-done | bytes 98336 | tf_op jit(solution)/shard_map/ppermute | solution.py:242
  26.6 0.7 %slice_multiply_fusion = f32[3,7,2048]{2,1,0:T(8,128)} fusion(f32[3,8,2048]{2,1,0:T(8,128)S(1)} %maximum_bitcast_fusion), kind=kLoop, calls=%fused_computation | loop fusion | flops 43008 | bytes 344064 | tf_op jit(solution)/shard_map/mul | solution.py:287
  (8 shorter events, 0.1 us)
Async XLA Ops:
  0.6 7.4 %copy-start.1 = (bf16[128,2048]{1,0:T(8,128)(2,1)S(1)}, bf16[128,2048]{1,0:T(8,128)(2,1)}, u32[]{:S(2)}) copy-start(bf16[128,2048]{1,0:T(8,128)(2,1)} %u_ref.3) | copy-start | bytes 1572868
  0.6 7.4 %copy-start = (bf16[128,6144]{1,0:T(8,128)(2,1)S(1)}, bf16[128,6144]{1,0:T(8,128)(2,1)}, u32[]{:S(2)}) copy-start(bf16[128,6144]{1,0:T(8,128)(2,1)} %p_ref.3) | copy-start | bytes 4718596
  0.7 7.4 %copy-start.2 = (f32[3,7,2048]{2,1,0:T(8,128)S(1)}, f32[3,7,2048]{2,1,0:T(8,128)}, u32[]{:S(2)}) copy-start(f32[3,7,2048]{2,1,0:T(8,128)} %filters.5) | copy-start | bytes 516100
  2.6 9.2 %collective-permute-start = (bf16[8,8192]{1,0:T(8,128)(2,1)}, bf16[8,8192]{1,0:T(8,128)(2,1)S(1)}, u32[]{:S(2)}, u32[]{:S(2)}) collective-permute-start(bf16[8,8192]{1,0:T(8,128)(2,1)} %get-tuple-element.19), channel_id=1, source_target_pairs={{0,15},{1,2},{2,1},{3,4},{4,3},{5,6},{6,5},{7,8},{8,7},{9,10},{10,... | collective-permute-start | bytes 393224 | tf_op jit(solution)/shard_map/ppermute | solution.py:242
  8.0 3.8 %collective-permute-start.1 = (bf16[8,8192]{1,0:T(8,128)(2,1)}, bf16[8,8192]{1,0:T(8,128)(2,1)S(1)}, u32[]{:S(2)}, u32[]{:S(2)}) collective-permute-start(bf16[8,8192]{1,0:T(8,128)(2,1)} %get-tuple-element.20), channel_id=1, source_target_pairs={{0,1},{1,0},{2,3},{3,2},{4,5},{5,4},{6,7},{7,6},{8,9},{9,8},{10,11... | collective-permute-start | bytes 393224 | tf_op jit(solution)/shard_map/ppermute | solution.py:242
  12.6 1.5 %collective-permute-start.2 = (f32[24,1024]{1,0:T(8,128)S(1)}, f32[24,1024]{1,0:T(8,128)S(1)}, u32[]{:S(2)}, u32[]{:S(2)}) collective-permute-start(f32[24,1024]{1,0:T(8,128)S(1)} %select_bitcast_fusion), channel_id=1, source_target_pairs={{0,1},{1,0},{2,3},{3,2},{4,5},{5,4},{6,7},{7,6},{8,9},{9,8},{10,11... | collective-permute-start | bytes 294920 | tf_op jit(solution)/shard_map/ppermute | solution.py:242
  14.1 4.5 %collective-permute-start.3 = (bf16[24,1024]{1,0:T(8,128)(2,1)S(1)}, bf16[24,1024]{1,0:T(8,128)(2,1)S(1)}, u32[]{:S(2)}, u32[]{:S(2)}) collective-permute-start(bf16[24,1024]{1,0:T(8,128)(2,1)S(1)} %fusion.1), channel_id=1, source_target_pairs={{0,9},{1,8},{2,11},{3,10},{4,13},{5,12},{6,15},{7,14},{8,1},{9,0},... | collective-permute-start | bytes 147464 | tf_op jit(solution)/shard_map/ppermute | solution.py:242
  18.6 5.5 %collective-permute-start.6 = (bf16[24,1024]{1,0:T(8,128)(2,1)S(1)}, bf16[24,1024]{1,0:T(8,128)(2,1)S(1)}, u32[]{:S(2)}, u32[]{:S(2)}) collective-permute-start(bf16[24,1024]{1,0:T(8,128)(2,1)S(1)} %add_convert_fusion), channel_id=1, source_target_pairs={{0,6},{1,7},{2,4},{3,5},{4,2},{5,3},{6,0},{7,1},{8,14},{9,15},{10,... | collective-permute-start | bytes 147464 | tf_op jit(solution)/shard_map/ppermute | solution.py:242
  21.1 4.0 %collective-permute-start.5 = (bf16[24,1024]{1,0:T(8,128)(2,1)S(1)}, bf16[24,1024]{1,0:T(8,128)(2,1)S(1)}, u32[]{:S(2)}, u32[]{:S(2)}) collective-permute-start(bf16[24,1024]{1,0:T(8,128)(2,1)S(1)} %add_convert_fusion), channel_id=1, source_target_pairs={{0,5},{1,4},{2,7},{3,6},{4,1},{5,0},{6,3},{7,2},{8,13},{9,12},{10,... | collective-permute-start | bytes 147464 | tf_op jit(solution)/shard_map/ppermute | solution.py:242
  21.1 4.1 %collective-permute-start.4 = (bf16[24,1024]{1,0:T(8,128)(2,1)S(1)}, bf16[24,1024]{1,0:T(8,128)(2,1)S(1)}, u32[]{:S(2)}, u32[]{:S(2)}) collective-permute-start(bf16[24,1024]{1,0:T(8,128)(2,1)S(1)} %add_convert_fusion), channel_id=1, source_target_pairs={{0,3},{1,2},{2,1},{3,0},{4,7},{5,6},{6,5},{7,4},{8,11},{9,10},{10,... | collective-permute-start | bytes 147464 | tf_op jit(solution)/shard_map/ppermute | solution.py:242
  25.2 1.4 %collective-permute-start.7 = (f32[24,1024]{1,0:T(8,128)S(1)}, f32[24,1024]{1,0:T(8,128)S(1)}, u32[]{:S(2)}, u32[]{:S(2)}) collective-permute-start(f32[24,1024]{1,0:T(8,128)S(1)} %add_add_fusion), channel_id=1, source_target_pairs={{0,1},{1,0},{2,3},{3,2},{4,5},{5,4},{6,7},{7,6},{8,9},{9,8},{10,11... | collective-permute-start | bytes 294920 | tf_op jit(solution)/shard_map/ppermute | solution.py:242

commit v3 on v2

--- a/solution.py
+++ b/solution.py
@@ -111,16 +111,26 @@
     lax.fori_loop(0, chans // LANES, group, 0, unroll=UNROLL)
 
 
-def back_kernel(filters, gated_in, grads, gated_head, head, following, gated, out, slab):
+def back_kernel(filters, gated_in, grads, gated_head, head, following, gated, out, slab, gated_slab, out_slab, sems):
     rows, columns = out.shape
     chans = columns // 3
     taps = filters.shape[1]
 
-    def group(n, carry):
+    def round_gated(n, carry):
         c = lanes_at(n * LANES)
-        gated[0:16, c] = jnp.concatenate([gated_head[n], gated_in[n, RIM:16, :]], 0).astype(BF)
-        gated[16:rows, c] = gated_in[n, 16:rows, :].astype(BF)
-        for s in range(3):
+        gated_slab[0:16, c] = jnp.concatenate([gated_head[n], gated_in[n, RIM:16, :]], 0).astype(BF)
+        gated_slab[16:rows, c] = gated_in[n, 16:rows, :].astype(BF)
+        return carry
+
+    copies = [pltpu.make_async_copy(gated_slab, gated, sems.at[3])]
+    for s in range(3):
+        copies.append(pltpu.make_async_copy(out_slab.at[s], out.at[:, s * chans : (s + 1) * chans], sems.at[s]))
+
+    lax.fori_loop(0, chans // LANES, round_gated, 0, unroll=UNROLL)
+    copies[0].start()
+    for s in range(3):
+
+        def group(n, carry, s=s):
             tap = tap_rows(filters, s, n)
             slab[s, 0:RIM, :] = head[s, n]
             slab[s, RIM : 2 * RIM, :] = grads[s, n, RIM : 2 * RIM, :]
@@ -136,11 +146,14 @@
                     terms = [tap[j] * grads[s, n, r + j : r + j + SUB, :] for j in range(taps)]
                 result.append(sum(terms))
                 if r % 16 == SUB:
-                    out[r - SUB : r + SUB, lanes_at(s * chans + n * LANES)] = jnp.concatenate(result, 0).astype(BF)
+                    out_slab[s, r - SUB : r + SUB, lanes_at(n * LANES)] = jnp.concatenate(result, 0).astype(BF)
                     result = []
-        return carry
-
-    lax.fori_loop(0, chans // LANES, group, 0, unroll=UNROLL)
+            return carry
+
+        lax.fori_loop(0, chans // LANES, group, 0, unroll=UNROLL)
+        copies[s + 1].start()
+    for copy in copies:
+        copy.wait()
 
 
 def params(**kw):
@@ -195,8 +208,13 @@
         back_kernel,
         out_shape=(jax.ShapeDtypeStruct((rows, chans), BF), jax.ShapeDtypeStruct((rows, 3 * chans), BF)),
         in_specs=[VMEM] * 6,
-        out_specs=(VMEM,) * 2,
-        scratch_shapes=[pltpu.VMEM((3, 4 * RIM, LANES), F32)],
+        out_specs=(pl.BlockSpec(memory_space=pltpu.HBM),) * 2,
+        scratch_shapes=[
+            pltpu.VMEM((3, 4 * RIM, LANES), F32),
+            pltpu.VMEM((rows, chans), BF),
+            pltpu.VMEM((3, rows, chans), BF),
+            pltpu.SemaphoreType.DMA((4,)),
+        ],
         cost_estimate=pl.CostEstimate(flops=6 * taps * rows * chans, bytes_accessed=8 * rows * chans, transcendentals=0),
         compiler_params=params(),
         name="back",
@@ -206,40 +224,57 @@
     return [[(1 << b) ^ 1] for b in reversed(range(3, bits))] + [[m for m in (3, 5, 6) if m < 1 << bits]]
 
 
-def pack_kernel(head, tail, u_head, near, far):
-    columns = head.shape[1]
+def pack_kernel(p_ref, u_ref, u_out, near, far, ends, sems):
+    rows, columns = p_ref.shape
+    copies = [
+        pltpu.make_async_copy(p_ref.at[0:16], ends.at[0:16], sems.at[0]),
+        pltpu.make_async_copy(p_ref.at[rows - 16 : rows], ends.at[16:32], sems.at[1]),
+        pltpu.make_async_copy(u_ref, u_out, sems.at[2]),
+    ]
+    for copy in copies:
+        copy.start()
+    for copy in copies:
+        copy.wait()
     forward_near = lax.rem(lax.axis_index("seq"), 2) == 0
-
-    first = head[...].astype(F32)[:RIM]
-    last = tail[...].astype(F32)[16 - RIM :]
+    first = ends[0:16, :].astype(F32)[:RIM]
+    last = ends[16:32, :].astype(F32)[16 - RIM :]
     near[:, :columns] = jnp.where(forward_near, last, first).astype(BF)
     far[:, :columns] = jnp.where(forward_near, first, last).astype(BF)
-    cotangent = u_head[...].astype(F32)[:RIM].astype(BF)
+    cotangent = u_out[0:16, :].astype(F32)[:RIM].astype(BF)
     near[:, columns:] = cotangent
     far[:, columns:] = cotangent
 
 
 def call_pack(projected, upstream):
-    rows, columns = projected.shape
-    chans = upstream.shape[1]
+    columns, chans = projected.shape[1], upstream.shape[1]
     shape = jax.ShapeDtypeStruct((RIM, columns + chans), BF)
     return pl.pallas_call(
         pack_kernel,
-        grid=(1,),
-        out_shape=(shape, shape),
-        in_specs=[
-            pl.BlockSpec((16, columns), lambda _: (0, 0)),
-            pl.BlockSpec((16, columns), lambda _: (rows // 16 - 1, 0)),
-            pl.BlockSpec((16, chans), lambda _: (0, 0)),
-        ],
-        out_specs=(VMEM,) * 2,
+        out_shape=(jax.ShapeDtypeStruct(upstream.shape, BF), shape, shape),
+        in_specs=[pl.BlockSpec(memory_space=pltpu.HBM)] * 2,
+        out_specs=(VMEM,) * 3,
+        scratch_shapes=[pltpu.VMEM((32, columns), BF), pltpu.SemaphoreType.DMA((3,))],
+        compiler_params=params(),
         name="pack",
-    )(projected, projected, upstream)
+    )(*[pltpu.with_memory_space_constraint(a, pltpu.HBM) for a in (projected, upstream)])
 
 
 def swap(array, partner):
     ways = lax.axis_size("seq")
     return lax.ppermute(array, "seq", [(i, partner(i)) for i in range(ways)])
+
+
+def trade_far(array):
+    groups, ways = lax.axis_size("groups"), lax.axis_size("seq")
+
+    def partner(g, i):
+        if i not in (0, ways - 1):
+            return g, ((i + 1) ^ 1) - 1
+        return (g ^ 1, i) if groups % 2 == 0 else (g, ways - 1 - i)
+
+    places = [(g, i) for g in range(groups) for i in range(ways)]
+    pairs = [(g * ways + i, partner(g, i)[0] * ways + partner(g, i)[1]) for g, i in places]
+    return lax.ppermute(array, ("groups", "seq"), pairs)
 
 
 def rims(projected, upstream):
@@ -247,14 +282,14 @@
     ways = lax.axis_size("seq")
     me = lax.axis_index("seq")
     even = me % 2 == 0
-    near, far = call_pack(projected, upstream)
-    far = swap(far, lambda i: ways - 1 - i if i in (0, ways - 1) else ((i + 1) ^ 1) - 1)
+    upstream, near, far = call_pack(projected, upstream)
+    far = trade_far(far)
     near = swap(near, lambda i: i ^ 1)
     before = jnp.where(even, far, near)[:, :columns]
     after = jnp.where(even, near, far)
     before = jnp.where(me == 0, jnp.zeros_like(before), before)
     after = jnp.where(me == ways - 1, jnp.zeros_like(after), after)
-    return before, after
+    return upstream, before, after
 
 
 def shards(projected, filters, upstream):
@@ -263,7 +298,7 @@
     me = lax.axis_index("seq")
     taps = filters.shape[1]
     chans = columns // 3
-    before, after = rims(projected, upstream)
+    upstream, before, after = rims(projected, upstream)
     gated, grads, sums = call_inner(projected, upstream, filters)
     *edges, halves = call_rim(projected, upstream, filters, before, after, sums)
     bits = ways.bit_length() - 1
@@ -272,10 +307,10 @@
     mine = mine + swap(jnp.where(odd, halves[0], halves[1]), lambda i: i ^ 1)
     for step, masks in enumerate(rounds(bits)):
         sent = mine.astype(BF)
-        if step == 0:
+        if step == len(rounds(bits)) - 1:
             sent, grads = lax.optimization_barrier((sent, grads))
         got = [swap(sent, lambda i: i ^ m) for m in masks]
-        if step == 0:
+        if step == len(rounds(bits)) - 1:
             gated, grad_projected = call_back(filters, gated, grads, *edges)
             got, gated, grad_projected = lax.optimization_barrier((got, gated, grad_projected))
         terms = [sent.astype(F32)] + [g.astype(F32) for g in got]

time: 27.4 us -> 25.1 us (0.916)
  waiting for transfers between devices: 6.76 us -> 5.25 us
  Pallas kernels: 9.3 us -> 8.45 us
    ppermute x0 -> x1, starting transfers between devices: none -> 3.03 us  [trade_far(): return lax.ppermute(array, ('groups', 'seq'), pairs)]
    ppermute x8 -> x7, starting transfers between devices: 9.61 us -> 6.63 us  [swap(): return lax.ppermute(array, 'seq', [(i, partner(i)) for i in range(ways)])]
    ppermute x8 -> x7, waiting for transfers between devices: 6.76 us -> 5.25 us  [swap(): return lax.ppermute(array, 'seq', [(i, partner(i)) for i in range(ways)])]
    pallas_call x1, Pallas kernels: 1.91 us -> 1.43 us  [call_pack(): pl.pallas_call(pack_kernel, out_shape=(jax.ShapeDtypeStruct(upstream.shap...]
    pallas_call x1, Pallas kernels: 2.93 us -> 2.56 us  [call_back(): pl.pallas_call(back_kernel, out_shape=(jax.ShapeDtypeStruct((rows, chans)...]
  transfers between devices with their start and end apart: 8 -> 8, of which waited for: 6 -> 4; matrix products, arithmetic and copies ran while one was open for 0% -> 0% of each run, Pallas kernels for 25% -> 25%
where the time goes in v3:
time: 25.1 us; the launch traced here: 25 us
  starting transfers between devices  9.66 us (38%)
  Pallas kernels  8.45 us (34%)
  waiting for transfers between devices  5.25 us (21%)
  other arithmetic  0.83 us (3%)
  between operations  0.75 us (3%)
    ppermute x7, starting transfers between devices, swap(): return lax.ppermute(array, 'seq', [(i, partner(i)) for i in range(ways)])  6.63 us
    ppermute x7, waiting for transfers between devices, swap(): return lax.ppermute(array, 'seq', [(i, partner(i)) for i in range(ways)])  5.25 us
    pallas_call x1, Pallas kernels, call_inner(): pl.pallas_call(inner_kernel, out_shape=(jax.ShapeDtypeStruct((groups, row...  3.79 us
    ppermute x1, starting transfers between devices, trade_far(): return lax.ppermute(array, ('groups', 'seq'), pairs)  3.03 us
    pallas_call x1, Pallas kernels, call_back(): pl.pallas_call(back_kernel, out_shape=(jax.ShapeDtypeStruct((rows, chans)...  2.56 us
    pallas_call x1, Pallas kernels, call_pack(): pl.pallas_call(pack_kernel, out_shape=(jax.ShapeDtypeStruct(upstream.shap...  1.43 us
    mul x1, other arithmetic, shards(): total.reshape(3, SUB, chans)[:, :taps] * float(rows * ways) ** (-0.5)  0.7 us
    pallas_call x1, Pallas kernels, call_rim(): pl.pallas_call(rim_kernel, out_shape=(jax.ShapeDtypeStruct((groups, RIM,...  0.67 us
  transfers between devices with their start and end apart: 8, of which 4 were waited for; matrix products, arithmetic and copies ran while one was open for 0% of the time, Pallas kernels for 25%

profile of v3, /device:TPU:0, one launch (start us, length us, event | category | flops | bytes accessed | tf_op | source)
XLA Modules:
  0.0 25.0 jit_solution(14131344084246363514)
XLA Ops:
  0.6 0.0 copy-start
  0.6 0.0 copy-start.1
  0.7 1.4 %pack.1 = (bf16[128,2048]{1,0:T(8,128)(2,1)S(1)}, bf16[8,8192]{1,0:T(8,128)(2,1)S(1)}, bf16[8,8192]{1,0:T(8,128)(2,1)S(1)}) custom-call(bf16[128,6144]{1,0:T(8,128)(2,1)} %p_ref.5, bf16[128,2048]{1,0:T(8,128)(2,1)} %u_ref.1), custom_call_target="tpu_custom_call" | custom-call | tf_op jit(solution)/shard_map/pack/pallas_call | solution.py:251
  2.1 3.0 %collective-permute-start = (bf16[8,8192]{1,0:T(8,128)(2,1)S(1)}, bf16[8,8192]{1,0:T(8,128)(2,1)S(1)}, u32[]{:S(2)}, u32[]{:S(2)}) collective-permute-start(bf16[8,8192]{1,0:T(8,128)(2,1)S(1)} %get-tuple-element.23), channel_id=1, source_target_pairs={{0,16},{1,2},{2,1},{3,4},{4,3},{5,6},{6,5},{7,8},{8,7},{9,10},{10,... | collective-permute-start | bytes 393224 | tf_op jit(solution)/shard_map/ppermute | solution.py:277
  5.1 0.1 collective-permute-start.1
  5.2 0.0 copy-done
  5.2 0.0 copy-done.1
  5.2 3.8 %inner.1 = (f32[16,128,128]{2,1,0:T(8,128)S(1)}, f32[3,16,128,128]{3,2,1,0:T(8,128)S(1)}, f32[16,3,7,8,128]{4,3,2,1,0:T(8,128)S(1)}) custom-call(bf16[128,6144]{1,0:T(8,128)(2,1)S(1)} %copy-done, bf16[128,2048]{1,0:T(8,128)(2,1)S(1)} %get-tuple-element.22.u_ref, f32[3,7,2048]{2,1,0:T(8,128)S(1)} %copy-done.1), custom_call_target="tpu_custom_call" | custom-call | flops 22020096 | bytes 2097152 | tf_op jit(solution)/shard_map/inner/pallas_call | solution.py:168
  9.0 0.0 collective-permute-done
  9.0 0.0 collective-permute-done.1
  9.1 0.7 %rim.1 = (f32[16,8,128]{2,1,0:T(8,128)S(1)}, f32[3,16,8,128]{3,2,1,0:T(8,128)S(1)}, f32[3,16,8,128]{3,2,1,0:T(8,128)S(1)}, f32[2,24,1024]{2,1,0:T(8,128)S(1)}) custom-call(bf16[128,6144]{1,0:T(8,128)(2,1)S(1)} %copy-done, bf16[128,2048]{1,0:T(8,128)(2,1)S(1)} %get-tuple-element.22.u_ref, f32[3,7,2048]{2,1,0:T(8,128)S(1)} %copy-done.1, ...), custom_call_target="tpu_custom_call" | custom-call | tf_op jit(solution)/shard_map/rim/pallas_call | solution.py:187
  9.8 0.5 %collective-permute-start.2 = (f32[24,1024]{1,0:T(8,128)S(1)}, f32[24,1024]{1,0:T(8,128)S(1)}, u32[]{:S(2)}, u32[]{:S(2)}) collective-permute-start(f32[24,1024]{1,0:T(8,128)S(1)} %select_bitcast_fusion), channel_id=1, source_target_pairs={{0,1},{1,0},{2,3},{3,2},{4,5},{5,4},{6,7},{7,6},{8,9},{9,8},{10,11... | collective-permute-start | bytes 294920 | tf_op jit(solution)/shard_map/ppermute | solution.py:264
  10.3 0.9 %collective-permute-done.2 = f32[24,1024]{1,0:T(8,128)S(1)} collective-permute-done((f32[24,1024]{1,0:T(8,128)S(1)}, f32[24,1024]{1,0:T(8,128)S(1)}, u32[]{:S(2)}, u32[]{:S(2)}) %collective-permute-start.2) | collective-permute-done | bytes 98336 | tf_op jit(solution)/shard_map/ppermute | solution.py:264
  11.2 2.4 %collective-permute-start.3 = (bf16[24,1024]{1,0:T(8,128)(2,1)S(1)}, bf16[24,1024]{1,0:T(8,128)(2,1)S(1)}, u32[]{:S(2)}, u32[]{:S(2)}) collective-permute-start(bf16[24,1024]{1,0:T(8,128)(2,1)S(1)} %fusion.1), channel_id=1, source_target_pairs={{0,9},{1,8},{2,11},{3,10},{4,13},{5,12},{6,15},{7,14},{8,1},{9,0},... | collective-permute-start | bytes 147464 | tf_op jit(solution)/shard_map/ppermute | solution.py:264
  13.7 2.1 %collective-permute-done.3 = bf16[24,1024]{1,0:T(8,128)(2,1)S(1)} collective-permute-done((bf16[24,1024]{1,0:T(8,128)(2,1)S(1)}, bf16[24,1024]{1,0:T(8,128)(2,1)S(1)}, u32[]{:S(2)}, u32[]{:S(2)}) %collective-permute-start.3) | collective-permute-done | bytes 49184 | tf_op jit(solution)/shard_map/ppermute | solution.py:264
  15.7 3.1 %collective-permute-start.6 = (bf16[24,1024]{1,0:T(8,128)(2,1)S(1)}, bf16[24,1024]{1,0:T(8,128)(2,1)S(1)}, u32[]{:S(2)}, u32[]{:S(2)}) collective-permute-start(bf16[24,1024]{1,0:T(8,128)(2,1)S(1)} %add_convert_fusion), channel_id=1, source_target_pairs={{0,6},{1,7},{2,4},{3,5},{4,2},{5,3},{6,0},{7,1},{8,14},{9,15},{10,... | collective-permute-start | bytes 147464 | tf_op jit(solution)/shard_map/ppermute | solution.py:264
  18.8 0.0 collective-permute-start.5
  18.8 0.4 %collective-permute-start.4 = (bf16[24,1024]{1,0:T(8,128)(2,1)S(1)}, bf16[24,1024]{1,0:T(8,128)(2,1)S(1)}, u32[]{:S(2)}, u32[]{:S(2)}) collective-permute-start(bf16[24,1024]{1,0:T(8,128)(2,1)S(1)} %add_convert_fusion), channel_id=1, source_target_pairs={{0,3},{1,2},{2,1},{3,0},{4,7},{5,6},{6,5},{7,4},{8,11},{9,10},{10,... | collective-permute-start | bytes 147464 | tf_op jit(solution)/shard_map/ppermute | solution.py:264
  19.2 2.6 %back.1 = (bf16[128,2048]{1,0:T(8,128)(2,1)}, bf16[128,6144]{1,0:T(8,128)(2,1)}) custom-call(f32[3,7,2048]{2,1,0:T(8,128)S(1)} %copy-done.1, f32[16,128,128]{2,1,0:T(8,128)S(1)} %get-tuple-element.29.gated_in, f32[3,16,128,128]{3,2,1,0:T(8,128)S(1)} %get-tuple-element.30.grads, f32[16,8,128]{2,1,0:T(8,128)S(1)} %get-tuple-element.31.gated_head, ...), custom_call_target="tpu_custom_call" | custom-call | flops 11010048 | bytes 2097152 | tf_op jit(solution)/shard_map/back/pallas_call | solution.py:207
  21.8 0.0 collective-permute-done.6
  21.8 1.0 %collective-permute-done.5 = bf16[24,1024]{1,0:T(8,128)(2,1)S(1)} collective-permute-done((bf16[24,1024]{1,0:T(8,128)(2,1)S(1)}, bf16[24,1024]{1,0:T(8,128)(2,1)S(1)}, u32[]{:S(2)}, u32[]{:S(2)}) %collective-permute-start.5) | collective-permute-done | bytes 49184 | tf_op jit(solution)/shard_map/ppermute | solution.py:264
  22.8 0.0 collective-permute-done.4
  22.9 0.2 collective-permute-start.7
  23.0 1.2 %collective-permute-done.7 = f32[24,1024]{1,0:T(8,128)S(1)} collective-permute-done((f32[24,1024]{1,0:T(8,128)S(1)}, f32[24,1024]{1,0:T(8,128)S(1)}, u32[]{:S(2)}, u32[]{:S(2)}) %collective-permute-start.7) | collective-permute-done | bytes 98336 | tf_op jit(solution)/shard_map/ppermute | solution.py:264
  24.3 0.7 %slice_multiply_fusion = f32[3,7,2048]{2,1,0:T(8,128)} fusion(f32[3,8,2048]{2,1,0:T(8,128)S(1)} %maximum_bitcast_fusion), kind=kLoop, calls=%fused_computation | loop fusion | flops 43008 | bytes 344064 | tf_op jit(solution)/shard_map/mul | solution.py:322
  (8 shorter events, 0.1 us)
Async XLA Ops:
  0.6 4.6 %copy-start = (bf16[128,6144]{1,0:T(8,128)(2,1)S(1)}, bf16[128,6144]{1,0:T(8,128)(2,1)}, u32[]{:S(2)}) copy-start(bf16[128,6144]{1,0:T(8,128)(2,1)} %p_ref.5) | copy-start | bytes 4718596
  0.6 4.6 %copy-start.1 = (f32[3,7,2048]{2,1,0:T(8,128)S(1)}, f32[3,7,2048]{2,1,0:T(8,128)}, u32[]{:S(2)}) copy-start(f32[3,7,2048]{2,1,0:T(8,128)} %filters.5) | copy-start | bytes 516100
  2.1 6.9 %collective-permute-start = (bf16[8,8192]{1,0:T(8,128)(2,1)S(1)}, bf16[8,8192]{1,0:T(8,128)(2,1)S(1)}, u32[]{:S(2)}, u32[]{:S(2)}) collective-permute-start(bf16[8,8192]{1,0:T(8,128)(2,1)S(1)} %get-tuple-element.23), channel_id=1, source_target_pairs={{0,16},{1,2},{2,1},{3,4},{4,3},{5,6},{6,5},{7,8},{8,7},{9,10},{10,... | collective-permute-start | bytes 393224 | tf_op jit(solution)/shard_map/ppermute | solution.py:277
  5.1 3.9 %collective-permute-start.1 = (bf16[8,8192]{1,0:T(8,128)(2,1)S(1)}, bf16[8,8192]{1,0:T(8,128)(2,1)S(1)}, u32[]{:S(2)}, u32[]{:S(2)}) collective-permute-start(bf16[8,8192]{1,0:T(8,128)(2,1)S(1)} %get-tuple-element.24), channel_id=1, source_target_pairs={{0,1},{1,0},{2,3},{3,2},{4,5},{5,4},{6,7},{7,6},{8,9},{9,8},{10,11... | collective-permute-start | bytes 393224 | tf_op jit(solution)/shard_map/ppermute | solution.py:264
  9.8 1.4 %collective-permute-start.2 = (f32[24,1024]{1,0:T(8,128)S(1)}, f32[24,1024]{1,0:T(8,128)S(1)}, u32[]{:S(2)}, u32[]{:S(2)}) collective-permute-start(f32[24,1024]{1,0:T(8,128)S(1)} %select_bitcast_fusion), channel_id=1, source_target_pairs={{0,1},{1,0},{2,3},{3,2},{4,5},{5,4},{6,7},{7,6},{8,9},{9,8},{10,11... | collective-permute-start | bytes 294920 | tf_op jit(solution)/shard_map/ppermute | solution.py:264
  11.2 4.5 %collective-permute-start.3 = (bf16[24,1024]{1,0:T(8,128)(2,1)S(1)}, bf16[24,1024]{1,0:T(8,128)(2,1)S(1)}, u32[]{:S(2)}, u32[]{:S(2)}) collective-permute-start(bf16[24,1024]{1,0:T(8,128)(2,1)S(1)} %fusion.1), channel_id=1, source_target_pairs={{0,9},{1,8},{2,11},{3,10},{4,13},{5,12},{6,15},{7,14},{8,1},{9,0},... | collective-permute-start | bytes 147464 | tf_op jit(solution)/shard_map/ppermute | solution.py:264
  15.7 6.0 %collective-permute-start.6 = (bf16[24,1024]{1,0:T(8,128)(2,1)S(1)}, bf16[24,1024]{1,0:T(8,128)(2,1)S(1)}, u32[]{:S(2)}, u32[]{:S(2)}) collective-permute-start(bf16[24,1024]{1,0:T(8,128)(2,1)S(1)} %add_convert_fusion), channel_id=1, source_target_pairs={{0,6},{1,7},{2,4},{3,5},{4,2},{5,3},{6,0},{7,1},{8,14},{9,15},{10,... | collective-permute-start | bytes 147464 | tf_op jit(solution)/shard_map/ppermute | solution.py:264
  18.8 4.0 %collective-permute-start.5 = (bf16[24,1024]{1,0:T(8,128)(2,1)S(1)}, bf16[24,1024]{1,0:T(8,128)(2,1)S(1)}, u32[]{:S(2)}, u32[]{:S(2)}) collective-permute-start(bf16[24,1024]{1,0:T(8,128)(2,1)S(1)} %add_convert_fusion), channel_id=1, source_target_pairs={{0,5},{1,4},{2,7},{3,6},{4,1},{5,0},{6,3},{7,2},{8,13},{9,12},{10,... | collective-permute-start | bytes 147464 | tf_op jit(solution)/shard_map/ppermute | solution.py:264
  18.8 4.0 %collective-permute-start.4 = (bf16[24,1024]{1,0:T(8,128)(2,1)S(1)}, bf16[24,1024]{1,0:T(8,128)(2,1)S(1)}, u32[]{:S(2)}, u32[]{:S(2)}) collective-permute-start(bf16[24,1024]{1,0:T(8,128)(2,1)S(1)} %add_convert_fusion), channel_id=1, source_target_pairs={{0,3},{1,2},{2,1},{3,0},{4,7},{5,6},{6,5},{7,4},{8,11},{9,10},{10,... | collective-permute-start | bytes 147464 | tf_op jit(solution)/shard_map/ppermute | solution.py:264
  22.9 1.4 %collective-permute-start.7 = (f32[24,1024]{1,0:T(8,128)S(1)}, f32[24,1024]{1,0:T(8,128)S(1)}, u32[]{:S(2)}, u32[]{:S(2)}) collective-permute-start(f32[24,1024]{1,0:T(8,128)S(1)} %add_add_fusion), channel_id=1, source_target_pairs={{0,1},{1,0},{2,3},{3,2},{4,5},{5,4},{6,7},{7,6},{8,9},{9,8},{10,11... | collective-permute-start | bytes 294920 | tf_op jit(solution)/shard_map/ppermute | solution.py:264

commit v4 on v3

--- a/solution.py
+++ b/solution.py
@@ -1,3 +1,5 @@
+import functools
+
 import jax
 import jax.numpy as jnp
 from jax import lax
@@ -10,6 +12,7 @@
 LANES = 128
 SUB = 8
 RIM = 8
+REACH = 6
 VMEM = pl.BlockSpec(memory_space=pltpu.VMEM)
 UNROLL = 4
 
@@ -80,7 +83,7 @@
     return arrays[0]
 
 
-def rim_kernel(p_ref, u_ref, filters, before, after, sums, gated, head, following, totals, slab):
+def rim_kernel(p_ref, u_ref, filters, before, sums, gated, head, totals, slab):
     rows, columns = p_ref.shape
     chans = columns // 3
     taps = filters.shape[1]
@@ -89,23 +92,41 @@
     def group(n, carry):
         for s in range(3):
             c = lanes_at(s * chans + n * LANES)
-            slab[s, 0:RIM, :] = before[:, c].astype(F32)
+            slab[s, 0:RIM, :] = pltpu.roll(before[:, c].astype(F32), RIM - REACH, 0)
             slab[s, RIM : RIM + 16, :] = p_ref[0:16, c].astype(F32)
-            slab[s, RIM + 16 : RIM + 32, :] = p_ref[rows - 16 : rows, c].astype(F32)
-            slab[s, RIM + 32 : RIM + 40, :] = after[:, c].astype(F32)
         tap = [tap_rows(filters, s, n) for s in range(3)]
-        conv = [convolve(tap, slab, s, RIM + 32) for s in range(3)]
-        _, grad = gates(*conv, after[:, lanes_at(columns + n * LANES)].astype(F32))
-        for s in range(3):
-            following[s, n] = grad[s]
         conv = [convolve(tap, slab, s, RIM) for s in range(3)]
         product, grad = gates(*conv, u_ref[0:16, lanes_at(n * LANES)].astype(F32)[0:RIM])
         gated[n] = product
-        c = lanes_at(lax.rem(n, half) * LANES)
         for s in range(3):
             head[s, n] = grad[s]
             acc = [sums[n, s, j] + grad[s] * slab[s, RIM - j : RIM - j + SUB, :] for j in range(taps)]
-            totals[n // half, s * SUB : s * SUB + SUB, c] = fold(acc)
+            place = pl.ds(s * taps * half + lax.rem(n, half), taps, stride=half)
+            totals[n // half, place, :] = fold(acc)[:taps]
+        return carry
+
+    lax.fori_loop(0, chans // LANES, group, 0, unroll=UNROLL)
+
+
+def next_kernel(p_ref, filters, after, following, slab):
+    rows, columns = p_ref.shape
+    chans = columns // 3
+    sub = lax.broadcasted_iota(jnp.int32, (SUB, LANES), 0)
+
+    def group(n, carry):
+        cotangent = jnp.zeros((SUB, LANES), F32)
+        for s in range(3):
+            c = lanes_at(s * chans + n * LANES)
+            tile = after[:, c].astype(F32)
+            slab[s, 0:16, :] = p_ref[rows - 16 : rows, c].astype(F32)
+            slab[s, 16 : 16 + RIM, :] = tile
+            cotangent = jnp.where(sub == s, pltpu.roll(tile, s + 2, 0), cotangent)
+            cotangent = jnp.where(sub == s + 3, pltpu.roll(tile, s + 4, 0), cotangent)
+        tap = [tap_rows(filters, s, n) for s in range(3)]
+        conv = [convolve(tap, slab, s, 16) for s in range(3)]
+        _, grad = gates(*conv, cotangent)
+        for s in range(3):
+            following[s, n] = grad[s]
         return carry
 
     lax.fori_loop(0, chans // LANES, group, 0, unroll=UNROLL)
@@ -181,23 +202,59 @@
     )(projected, upstream, filters)
 
 
-def call_rim(projected, upstream, filters, before, after, sums):
+def call_rim(projected, upstream, filters, before, sums):
     chans = upstream.shape[1]
     groups = chans // LANES
+    taps = filters.shape[1]
     return pl.pallas_call(
         rim_kernel,
         out_shape=(
             jax.ShapeDtypeStruct((groups, RIM, LANES), F32),
             jax.ShapeDtypeStruct((3, groups, RIM, LANES), F32),
-            jax.ShapeDtypeStruct((3, groups, RIM, LANES), F32),
-            jax.ShapeDtypeStruct((2, 3 * SUB, chans // 2), F32),
+            jax.ShapeDtypeStruct((2, 3 * taps * groups // 2, LANES), F32),
         ),
-        in_specs=[VMEM] * 6,
-        out_specs=(VMEM,) * 4,
-        scratch_shapes=[pltpu.VMEM((3, 6 * RIM, LANES), F32)],
+        in_specs=[VMEM] * 5,
+        out_specs=(VMEM,) * 3,
+        scratch_shapes=[pltpu.VMEM((3, RIM + 16, LANES), F32)],
         compiler_params=params(),
         name="rim",
-    )(projected, upstream, filters, before, after, sums)
+    )(projected, upstream, filters, before, sums)
+
+
+def call_next(projected, filters, after):
+    groups = filters.shape[2] // LANES
+    return pl.pallas_call(
+        next_kernel,
+        out_shape=jax.ShapeDtypeStruct((3, groups, RIM, LANES), F32),
+        in_specs=[VMEM] * 3,
+        out_specs=VMEM,
+        scratch_shapes=[pltpu.VMEM((3, 16 + RIM, LANES), F32)],
+        compiler_params=params(),
+        name="next",
+    )(projected, filters, after)
+
+
+def place_kernel(scale, bits, mine, other, out):
+    _, taps, chans = out.shape
+    half = chans // 2 // LANES
+    me = lax.axis_index("seq")
+    odd = lax.rem(sum(lax.rem(me // 2**b, 2) for b in range(bits)), 2)
+    for s in range(3):
+        for n in range(half):
+            place = pl.ds(s * taps * half + n, taps, stride=half)
+            out[s, :, lanes_at((odd * half + n) * LANES)] = mine[place, :] * scale
+            out[s, :, lanes_at(((1 - odd) * half + n) * LANES)] = other[place, :] * scale
+
+
+def call_place(mine, other, scale, bits, shape):
+    return pl.pallas_call(
+        functools.partial(place_kernel, scale, bits),
+        out_shape=jax.ShapeDtypeStruct(shape, F32),
+        in_specs=[VMEM] * 2,
+        out_specs=VMEM,
+        compiler_params=params(),
+        name="place",
+    )(mine, other)
 
 
 def call_back(filters, gated, grads, gated_head, head, following):
@@ -236,18 +293,27 @@
     for copy in copies:
         copy.wait()
     forward_near = lax.rem(lax.axis_index("seq"), 2) == 0
-    first = ends[0:16, :].astype(F32)[:RIM]
-    last = ends[16:32, :].astype(F32)[16 - RIM :]
-    near[:, :columns] = jnp.where(forward_near, last, first).astype(BF)
-    far[:, :columns] = jnp.where(forward_near, first, last).astype(BF)
-    cotangent = u_out[0:16, :].astype(F32)[:RIM].astype(BF)
-    near[:, columns:] = cotangent
-    far[:, columns:] = cotangent
+    chans = columns // 3
+    sub = lax.broadcasted_iota(jnp.int32, (SUB, LANES), 0)
+
+    def group(n, carry):
+        cotangent = u_out[0:16, lanes_at(n * LANES)].astype(F32)[:RIM]
+        for s in range(3):
+            c = lanes_at(s * chans + n * LANES)
+            last = pltpu.roll(ends[16:32, c].astype(F32)[16 - RIM :], REACH, 0)
+            first = ends[0:16, c].astype(F32)[:RIM]
+            first = jnp.where(sub == 6, pltpu.roll(cotangent, 6 - s, 0), first)
+            first = jnp.where(sub == 7, pltpu.roll(cotangent, 4 - s, 0), first)
+            near[:, c] = jnp.where(forward_near, last, first).astype(BF)
+            far[:, c] = jnp.where(forward_near, first, last).astype(BF)
+        return carry
+
+    lax.fori_loop(0, chans // LANES, group, 0, unroll=UNROLL)
 
 
 def call_pack(projected, upstream):
-    columns, chans = projected.shape[1], upstream.shape[1]
-    shape = jax.ShapeDtypeStruct((RIM, columns + chans), BF)
+    columns = projected.shape[1]
+    shape = jax.ShapeDtypeStruct((RIM, columns), BF)
     return pl.pallas_call(
         pack_kernel,
         out_shape=(jax.ShapeDtypeStruct(upstream.shape, BF), shape, shape),
@@ -278,14 +344,13 @@
 
 
 def rims(projected, upstream):
-    columns = projected.shape[1]
     ways = lax.axis_size("seq")
     me = lax.axis_index("seq")
     even = me % 2 == 0
     upstream, near, far = call_pack(projected, upstream)
     far = trade_far(far)
     near = swap(near, lambda i: i ^ 1)
-    before = jnp.where(even, far, near)[:, :columns]
+    before = jnp.where(even, far, near)
     after = jnp.where(even, near, far)
     before = jnp.where(me == 0, jnp.zeros_like(before), before)
     after = jnp.where(me == ways - 1, jnp.zeros_like(after), after)
@@ -293,33 +358,36 @@
 
 
 def shards(projected, filters, upstream):
-    rows, columns = projected.shape
+    rows = projected.shape[0]
     ways = lax.axis_size("seq")
     me = lax.axis_index("seq")
-    taps = filters.shape[1]
-    chans = columns // 3
     upstream, before, after = rims(projected, upstream)
     gated, grads, sums = call_inner(projected, upstream, filters)
-    *edges, halves = call_rim(projected, upstream, filters, before, after, sums)
+    gated_head, head, halves = call_rim(projected, upstream, filters, before, sums)
     bits = ways.bit_length() - 1
     odd = sum((me >> b) & 1 for b in range(bits)) % 2 == 1
     mine = jnp.where(odd, halves[1], halves[0])
     mine = mine + swap(jnp.where(odd, halves[0], halves[1]), lambda i: i ^ 1)
-    for step, masks in enumerate(rounds(bits)):
+    steps = rounds(bits)
+    for step, masks in enumerate(steps):
         sent = mine.astype(BF)
-        if step == len(rounds(bits)) - 1:
+        if step == 0:
+            sent, after = lax.optimization_barrier((sent, after))
+        if step == len(steps) - 1:
             sent, grads = lax.optimization_barrier((sent, grads))
         got = [swap(sent, lambda i: i ^ m) for m in masks]
-        if step == len(rounds(bits)) - 1:
-            gated, grad_projected = call_back(filters, gated, grads, *edges)
+        if step == 0:
+            following = call_next(projected, filters, after)
+            got, following = lax.optimization_barrier((got, following))
+        if step == len(steps) - 1:
+            gated, grad_projected = call_back(filters, gated, grads, gated_head, head, following)
             got, gated, grad_projected = lax.optimization_barrier((got, gated, grad_projected))
         terms = [sent.astype(F32)] + [g.astype(F32) for g in got]
         while len(terms) > 1:
             terms = [sum(terms[k : k + 2]) for k in range(0, len(terms), 2)]
         mine = terms[0]
     other = swap(mine, lambda i: i ^ 1)
-    total = jnp.concatenate([jnp.where(odd, other, mine), jnp.where(odd, mine, other)], 1)
-    total = total.reshape(3, SUB, chans)[:, :taps] * float(rows * ways) ** -0.5
+    total = call_place(mine, other, float(rows * ways) ** -0.5, bits, filters.shape)
     return gated, grad_projected, total
 
 

time: 25.1 us -> 24.4 us (0.972)
  Pallas kernels: 8.45 us -> 9.39 us
  other arithmetic: 0.83 us -> 0.09 us
  waiting for transfers between devices: 5.25 us -> 4.52 us
    pallas_call x0 -> x2, Pallas kernels: none -> 1.01 us  [the longest x1 0.74 us: call_place(): pl.pallas_call(functools.partial(place_kernel, scale, bits), out_shape=ja...]
    ppermute x7, waiting for transfers between devices: 5.25 us -> 4.52 us  [swap(): return lax.ppermute(array, 'seq', [(i, partner(i)) for i in range(ways)])]
    mul x1 -> x0, other arithmetic: 0.7 us -> none  [shards(): total.reshape(3, SUB, chans)[:, :taps] * float(rows * ways) ** (-0.5)]
  transfers between devices with their start and end apart: 8 -> 8, of which waited for: 4 -> 4; matrix products, arithmetic and copies ran while one was open for 0% -> 0% of each run, Pallas kernels for 25% -> 27%
where the time goes in v4:
time: 24.4 us; the launch traced here: 24.2 us
  starting transfers between devices  9.46 us (39%)
  Pallas kernels  9.39 us (38%)
  waiting for transfers between devices  4.52 us (19%)
  between operations  0.73 us (3%)
    ppermute x7, starting transfers between devices, swap(): return lax.ppermute(array, 'seq', [(i, partner(i)) for i in range(ways)])  6.43 us
    ppermute x7, waiting for transfers between devices, swap(): return lax.ppermute(array, 'seq', [(i, partner(i)) for i in range(ways)])  4.52 us
    pallas_call x1, Pallas kernels, call_inner(): pl.pallas_call(inner_kernel, out_shape=(jax.ShapeDtypeStruct((groups, row...  3.79 us
    ppermute x1, starting transfers between devices, trade_far(): return lax.ppermute(array, ('groups', 'seq'), pairs)  3.03 us
    pallas_call x1, Pallas kernels, call_back(): pl.pallas_call(back_kernel, out_shape=(jax.ShapeDtypeStruct((rows, chans)...  2.57 us
    pallas_call x1, Pallas kernels, call_pack(): pl.pallas_call(pack_kernel, out_shape=(jax.ShapeDtypeStruct(upstream.shap...  1.49 us
    pallas_call x1, Pallas kernels, call_place(): pl.pallas_call(functools.partial(place_kernel, scale, bits), out_shape=ja...  0.74 us
    pallas_call x1, Pallas kernels, call_rim(): pl.pallas_call(rim_kernel, out_shape=(jax.ShapeDtypeStruct((groups, RIM,...  0.53 us
  transfers between devices with their start and end apart: 8, of which 4 were waited for; matrix products, arithmetic and copies ran while one was open for 0% of the time, Pallas kernels for 27%

profile of v4, /device:TPU:0, one launch (start us, length us, event | category | flops | bytes accessed | tf_op | source)
XLA Modules:
  0.0 24.2 jit_solution(7465663462265809212)
XLA Ops:
  0.6 0.0 copy-start
  0.6 0.0 copy-start.1
  0.7 1.5 %pack.1 = (bf16[128,2048]{1,0:T(8,128)(2,1)S(1)}, bf16[8,6144]{1,0:T(8,128)(2,1)S(1)}, bf16[8,6144]{1,0:T(8,128)(2,1)S(1)}) custom-call(bf16[128,6144]{1,0:T(8,128)(2,1)} %p_ref.7, bf16[128,2048]{1,0:T(8,128)(2,1)} %u_ref.1), custom_call_target="tpu_custom_call" | custom-call | tf_op jit(solution)/shard_map/pack/pallas_call | solution.py:317
  2.1 3.0 %collective-permute-start = (bf16[8,6144]{1,0:T(8,128)(2,1)S(1)}, bf16[8,6144]{1,0:T(8,128)(2,1)S(1)}, u32[]{:S(2)}, u32[]{:S(2)}) collective-permute-start(bf16[8,6144]{1,0:T(8,128)(2,1)S(1)} %get-tuple-element.26), channel_id=1, source_target_pairs={{0,16},{1,2},{2,1},{3,4},{4,3},{5,6},{6,5},{7,8},{8,7},{9,10},{10,... | collective-permute-start | bytes 294920 | tf_op jit(solution)/shard_map/ppermute | solution.py:343
  5.2 0.1 collective-permute-start.1
  5.3 0.0 copy-done
  5.3 0.0 copy-done.1
  5.3 3.8 %inner.1 = (f32[16,128,128]{2,1,0:T(8,128)S(1)}, f32[3,16,128,128]{3,2,1,0:T(8,128)S(1)}, f32[16,3,7,8,128]{4,3,2,1,0:T(8,128)S(1)}) custom-call(bf16[128,6144]{1,0:T(8,128)(2,1)S(1)} %copy-done, bf16[128,2048]{1,0:T(8,128)(2,1)S(1)} %get-tuple-element.25.u_ref, f32[3,7,2048]{2,1,0:T(8,128)S(1)} %copy-done.1), custom_call_target="tpu_custom_call" | custom-call | flops 22020096 | bytes 2097152 | tf_op jit(solution)/shard_map/inner/pallas_call | solution.py:189
  9.1 0.0 collective-permute-done
  9.1 0.0 collective-permute-done.1
  9.1 0.5 %rim.1 = (f32[16,8,128]{2,1,0:T(8,128)S(1)}, f32[3,16,8,128]{3,2,1,0:T(8,128)S(1)}, f32[2,168,128]{2,1,0:T(8,128)S(1)}) custom-call(bf16[128,6144]{1,0:T(8,128)(2,1)S(1)} %copy-done, bf16[128,2048]{1,0:T(8,128)(2,1)S(1)} %get-tuple-element.25.u_ref, f32[3,7,2048]{2,1,0:T(8,128)S(1)} %copy-done.1, bf16[8,6144]{1,0:T(8,128)(2,1)S(1)} %get-tuple-element.48.before, ...), custom_call_target="tpu_custom_call" | custom-call | tf_op jit(solution)/shard_map/rim/pallas_call | solution.py:209
  9.7 0.5 %collective-permute-start.2 = (f32[168,128]{1,0:T(8,128)S(1)}, f32[168,128]{1,0:T(8,128)S(1)}, u32[]{:S(2)}, u32[]{:S(2)}) collective-permute-start(f32[168,128]{1,0:T(8,128)S(1)} %select_bitcast_fusion), channel_id=1, source_target_pairs={{0,1},{1,0},{2,3},{3,2},{4,5},{5,4},{6,7},{7,6},{8,9},{9,8},{10,11... | collective-permute-start | bytes 258056 | tf_op jit(solution)/shard_map/ppermute | solution.py:330
  10.2 0.9 %collective-permute-done.2 = f32[168,128]{1,0:T(8,128)S(1)} collective-permute-done((f32[168,128]{1,0:T(8,128)S(1)}, f32[168,128]{1,0:T(8,128)S(1)}, u32[]{:S(2)}, u32[]{:S(2)}) %collective-permute-start.2) | collective-permute-done | bytes 86048 | tf_op jit(solution)/shard_map/ppermute | solution.py:330
  11.1 2.3 %collective-permute-start.3 = (bf16[168,128]{1,0:T(8,128)(2,1)S(1)}, bf16[168,128]{1,0:T(8,128)(2,1)S(1)}, u32[]{:S(2)}, u32[]{:S(2)}) collective-permute-start(bf16[168,128]{1,0:T(8,128)(2,1)S(1)} %fusion), channel_id=1, source_target_pairs={{0,9},{1,8},{2,11},{3,10},{4,13},{5,12},{6,15},{7,14},{8,1},{9,0},... | collective-permute-start | bytes 129032 | tf_op jit(solution)/shard_map/ppermute | solution.py:330
  13.5 0.3 %next.1.following = f32[3,16,8,128]{3,2,1,0:T(8,128)S(1)} custom-call(bf16[128,6144]{1,0:T(8,128)(2,1)S(1)} %copy-done, f32[3,7,2048]{2,1,0:T(8,128)S(1)} %copy-done.1, bf16[8,6144]{1,0:T(8,128)(2,1)S(1)} %get-tuple-element.31.after), custom_call_target="tpu_custom_call" | custom-call | tf_op jit(solution)/shard_map/next/pallas_call | solution.py:226
  13.7 1.8 %collective-permute-done.3 = bf16[168,128]{1,0:T(8,128)(2,1)S(1)} collective-permute-done((bf16[168,128]{1,0:T(8,128)(2,1)S(1)}, bf16[168,128]{1,0:T(8,128)(2,1)S(1)}, u32[]{:S(2)}, u32[]{:S(2)}) %collective-permute-start.3) | collective-permute-done | bytes 43040 | tf_op jit(solution)/shard_map/ppermute | solution.py:330
  15.5 2.7 %collective-permute-start.6 = (bf16[168,128]{1,0:T(8,128)(2,1)S(1)}, bf16[168,128]{1,0:T(8,128)(2,1)S(1)}, u32[]{:S(2)}, u32[]{:S(2)}) collective-permute-start(bf16[168,128]{1,0:T(8,128)(2,1)S(1)} %add_convert_fusion), channel_id=1, source_target_pairs={{0,6},{1,7},{2,4},{3,5},{4,2},{5,3},{6,0},{7,1},{8,14},{9,15},{10,... | collective-permute-start | bytes 129032 | tf_op jit(solution)/shard_map/ppermute | solution.py:330
  18.2 0.0 collective-permute-start.5
  18.2 0.6 %collective-permute-start.4 = (bf16[168,128]{1,0:T(8,128)(2,1)S(1)}, bf16[168,128]{1,0:T(8,128)(2,1)S(1)}, u32[]{:S(2)}, u32[]{:S(2)}) collective-permute-start(bf16[168,128]{1,0:T(8,128)(2,1)S(1)} %add_convert_fusion), channel_id=1, source_target_pairs={{0,3},{1,2},{2,1},{3,0},{4,7},{5,6},{6,5},{7,4},{8,11},{9,10},{10,... | collective-permute-start | bytes 129032 | tf_op jit(solution)/shard_map/ppermute | solution.py:330
  18.8 2.6 %back.1 = (bf16[128,2048]{1,0:T(8,128)(2,1)}, bf16[128,6144]{1,0:T(8,128)(2,1)}) custom-call(f32[3,7,2048]{2,1,0:T(8,128)S(1)} %copy-done.1, f32[16,128,128]{2,1,0:T(8,128)S(1)} %get-tuple-element.35.gated_in, f32[3,16,128,128]{3,2,1,0:T(8,128)S(1)} %get-tuple-element.36.grads, f32[16,8,128]{2,1,0:T(8,128)S(1)} %get-tuple-element.37.gated_head, ...), custom_call_target="tpu_custom_call" | custom-call | flops 11010048 | bytes 2097152 | tf_op jit(solution)/shard_map/back/pallas_call | solution.py:264
  21.4 0.0 collective-permute-done.6
  21.4 0.7 %collective-permute-done.5 = bf16[168,128]{1,0:T(8,128)(2,1)S(1)} collective-permute-done((bf16[168,128]{1,0:T(8,128)(2,1)S(1)}, bf16[168,128]{1,0:T(8,128)(2,1)S(1)}, u32[]{:S(2)}, u32[]{:S(2)}) %collective-permute-start.5) | collective-permute-done | bytes 43040 | tf_op jit(solution)/shard_map/ppermute | solution.py:330
  22.1 0.0 collective-permute-done.4
  22.1 0.2 collective-permute-start.7
  22.3 1.1 %collective-permute-done.7.other = f32[168,128]{1,0:T(8,128)S(1)} collective-permute-done((f32[168,128]{1,0:T(8,128)S(1)}, f32[168,128]{1,0:T(8,128)S(1)}, u32[]{:S(2)}, u32[]{:S(2)}) %collective-permute-start.7) | collective-permute-done | bytes 86048 | tf_op jit(solution)/shard_map/ppermute | solution.py:330
  23.5 0.7 %place.1 = f32[3,7,2048]{2,1,0:T(8,128)} custom-call(f32[168,128]{1,0:T(8,128)S(1)} %add_add_fusion.mine, f32[168,128]{1,0:T(8,128)S(1)} %collective-permute-done.7.other), custom_call_target="tpu_custom_call" | custom-call | tf_op jit(solution)/shard_map/place/pallas_call | solution.py:250
  (5 shorter events, 0.1 us)
Async XLA Ops:
  0.6 4.6 %copy-start = (bf16[128,6144]{1,0:T(8,128)(2,1)S(1)}, bf16[128,6144]{1,0:T(8,128)(2,1)}, u32[]{:S(2)}) copy-start(bf16[128,6144]{1,0:T(8,128)(2,1)} %p_ref.7) | copy-start | bytes 4718596
  0.6 4.6 %copy-start.1 = (f32[3,7,2048]{2,1,0:T(8,128)S(1)}, f32[3,7,2048]{2,1,0:T(8,128)}, u32[]{:S(2)}) copy-start(f32[3,7,2048]{2,1,0:T(8,128)} %filters.7) | copy-start | bytes 516100
  2.1 6.9 %collective-permute-start = (bf16[8,6144]{1,0:T(8,128)(2,1)S(1)}, bf16[8,6144]{1,0:T(8,128)(2,1)S(1)}, u32[]{:S(2)}, u32[]{:S(2)}) collective-permute-start(bf16[8,6144]{1,0:T(8,128)(2,1)S(1)} %get-tuple-element.26), channel_id=1, source_target_pairs={{0,16},{1,2},{2,1},{3,4},{4,3},{5,6},{6,5},{7,8},{8,7},{9,10},{10,... | collective-permute-start | bytes 294920 | tf_op jit(solution)/shard_map/ppermute | solution.py:343
  5.2 3.9 %collective-permute-start.1 = (bf16[8,6144]{1,0:T(8,128)(2,1)S(1)}, bf16[8,6144]{1,0:T(8,128)(2,1)S(1)}, u32[]{:S(2)}, u32[]{:S(2)}) collective-permute-start(bf16[8,6144]{1,0:T(8,128)(2,1)S(1)} %get-tuple-element.27), channel_id=1, source_target_pairs={{0,1},{1,0},{2,3},{3,2},{4,5},{5,4},{6,7},{7,6},{8,9},{9,8},{10,11... | collective-permute-start | bytes 294920 | tf_op jit(solution)/shard_map/ppermute | solution.py:330
  9.7 1.4 %collective-permute-start.2 = (f32[168,128]{1,0:T(8,128)S(1)}, f32[168,128]{1,0:T(8,128)S(1)}, u32[]{:S(2)}, u32[]{:S(2)}) collective-permute-start(f32[168,128]{1,0:T(8,128)S(1)} %select_bitcast_fusion), channel_id=1, source_target_pairs={{0,1},{1,0},{2,3},{3,2},{4,5},{5,4},{6,7},{7,6},{8,9},{9,8},{10,11... | collective-permute-start | bytes 258056 | tf_op jit(solution)/shard_map/ppermute | solution.py:330
  11.1 4.4 %collective-permute-start.3 = (bf16[168,128]{1,0:T(8,128)(2,1)S(1)}, bf16[168,128]{1,0:T(8,128)(2,1)S(1)}, u32[]{:S(2)}, u32[]{:S(2)}) collective-permute-start(bf16[168,128]{1,0:T(8,128)(2,1)S(1)} %fusion), channel_id=1, source_target_pairs={{0,9},{1,8},{2,11},{3,10},{4,13},{5,12},{6,15},{7,14},{8,1},{9,0},... | collective-permute-start | bytes 129032 | tf_op jit(solution)/shard_map/ppermute | solution.py:330
  15.5 5.9 %collective-permute-start.6 = (bf16[168,128]{1,0:T(8,128)(2,1)S(1)}, bf16[168,128]{1,0:T(8,128)(2,1)S(1)}, u32[]{:S(2)}, u32[]{:S(2)}) collective-permute-start(bf16[168,128]{1,0:T(8,128)(2,1)S(1)} %add_convert_fusion), channel_id=1, source_target_pairs={{0,6},{1,7},{2,4},{3,5},{4,2},{5,3},{6,0},{7,1},{8,14},{9,15},{10,... | collective-permute-start | bytes 129032 | tf_op jit(solution)/shard_map/ppermute | solution.py:330
  18.2 3.9 %collective-permute-start.5 = (bf16[168,128]{1,0:T(8,128)(2,1)S(1)}, bf16[168,128]{1,0:T(8,128)(2,1)S(1)}, u32[]{:S(2)}, u32[]{:S(2)}) collective-permute-start(bf16[168,128]{1,0:T(8,128)(2,1)S(1)} %add_convert_fusion), channel_id=1, source_target_pairs={{0,5},{1,4},{2,7},{3,6},{4,1},{5,0},{6,3},{7,2},{8,13},{9,12},{10,... | collective-permute-start | bytes 129032 | tf_op jit(solution)/shard_map/ppermute | solution.py:330
  18.2 3.9 %collective-permute-start.4 = (bf16[168,128]{1,0:T(8,128)(2,1)S(1)}, bf16[168,128]{1,0:T(8,128)(2,1)S(1)}, u32[]{:S(2)}, u32[]{:S(2)}) collective-permute-start(bf16[168,128]{1,0:T(8,128)(2,1)S(1)} %add_convert_fusion), channel_id=1, source_target_pairs={{0,3},{1,2},{2,1},{3,0},{4,7},{5,6},{6,5},{7,4},{8,11},{9,10},{10,... | collective-permute-start | bytes 129032 | tf_op jit(solution)/shard_map/ppermute | solution.py:330
  22.1 1.3 %collective-permute-start.7 = (f32[168,128]{1,0:T(8,128)S(1)}, f32[168,128]{1,0:T(8,128)S(1)}, u32[]{:S(2)}, u32[]{:S(2)}) collective-permute-start(f32[168,128]{1,0:T(8,128)S(1)} %add_add_fusion.mine), channel_id=1, source_target_pairs={{0,1},{1,0},{2,3},{3,2},{4,5},{5,4},{6,7},{7,6},{8,9},{9,8},{10,11... | collective-permute-start | bytes 258056 | tf_op jit(solution)/shard_map/ppermute | solution.py:330

commit v5 on v4

--- a/solution.py
+++ b/solution.py
@@ -14,6 +14,7 @@
 RIM = 8
 REACH = 6
 VMEM = pl.BlockSpec(memory_space=pltpu.VMEM)
+HBM = pl.BlockSpec(memory_space=pltpu.HBM)
 UNROLL = 4
 
 
@@ -28,8 +29,8 @@
     ]
 
 
-def convolve(tap, slab, s, start):
-    return sum(tap[s][j] * slab[s, start - j : start - j + SUB, :] for j in range(len(tap[s])))
+def convolve(tap, slab, s, n, start):
+    return sum(tap[j] * slab[s, n, start - j : start - j + SUB, :] for j in range(len(tap)))
 
 
 def gates(query, key, value, cotangent):
@@ -39,18 +40,25 @@
     return query * product, [g.astype(BF).astype(F32) for g in grads]
 
 
-def inner_kernel(p_ref, u_ref, filters, gated, grads, sums, p_slab, u_slab):
+def inner_kernel(p_ref, u_hbm, filters, gated, grads, sums, p_slab, u_ref, u_slab, sem):
     rows, columns = p_ref.shape
     chans = columns // 3
     taps = filters.shape[1]
-
-    def group(n, carry):
-        for s in range(3):
-            p_slab[s] = p_ref[:, lanes_at(s * chans + n * LANES)].astype(F32)
+    fetch = pltpu.make_async_copy(u_hbm, u_ref, sem)
+    fetch.start()
+
+    def filter_group(n, carry):
+        for s in range(3):
+            p_slab[s, n] = p_ref[:, lanes_at(s * chans + n * LANES)].astype(F32)
+            tap = tap_rows(filters, s, n)
+            for r in range(RIM, rows, SUB):
+                grads[s, n, r : r + SUB, :] = convolve(tap, p_slab, s, n, r)
+        return carry
+
+    def gate_group(n, carry):
         u_slab[...] = u_ref[:, lanes_at(n * LANES)].astype(F32)
-        tap = [tap_rows(filters, s, n) for s in range(3)]
         for r in range(RIM, rows, SUB):
-            conv = [convolve(tap, p_slab, s, r) for s in range(3)]
+            conv = [grads[s, n, r : r + SUB, :] for s in range(3)]
             product, grad = gates(*conv, u_slab[r : r + SUB, :])
             gated[n, r : r + SUB, :] = product
             for s in range(3):
@@ -60,13 +68,16 @@
             for r in range(RIM, rows, SUB):
                 grad = grads[s, n, r : r + SUB, :]
                 for j in range(taps):
-                    term = grad * p_slab[s, r - j : r - j + SUB, :]
+                    term = grad * p_slab[s, n, r - j : r - j + SUB, :]
                     acc[j] = term if r == RIM else acc[j] + term
             for j in range(taps):
                 sums[n, s, j] = acc[j]
         return carry
 
-    lax.fori_loop(0, chans // LANES, group, 0, unroll=UNROLL)
+    groups = chans // LANES
+    lax.fori_loop(0, groups, filter_group, 0, unroll=UNROLL)
+    fetch.wait()
+    lax.fori_loop(0, groups, gate_group, 0, unroll=UNROLL)
 
 
 def fold(arrays):
@@ -83,7 +94,7 @@
     return arrays[0]
 
 
-def rim_kernel(p_ref, u_ref, filters, before, sums, gated, head, totals, slab):
+def rim_kernel(p_ref, u_head, filters, before, sums, gated, head, totals, slab):
     rows, columns = p_ref.shape
     chans = columns // 3
     taps = filters.shape[1]
@@ -92,15 +103,14 @@
     def group(n, carry):
         for s in range(3):
             c = lanes_at(s * chans + n * LANES)
-            slab[s, 0:RIM, :] = pltpu.roll(before[:, c].astype(F32), RIM - REACH, 0)
-            slab[s, RIM : RIM + 16, :] = p_ref[0:16, c].astype(F32)
-        tap = [tap_rows(filters, s, n) for s in range(3)]
-        conv = [convolve(tap, slab, s, RIM) for s in range(3)]
-        product, grad = gates(*conv, u_ref[0:16, lanes_at(n * LANES)].astype(F32)[0:RIM])
+            slab[s, 0, 0:RIM, :] = pltpu.roll(before[:, c].astype(F32), RIM - REACH, 0)
+            slab[s, 0, RIM : RIM + 16, :] = p_ref[0:16, c].astype(F32)
+        conv = [convolve(tap_rows(filters, s, n), slab, s, 0, RIM) for s in range(3)]
+        product, grad = gates(*conv, u_head[:, lanes_at(n * LANES)].astype(F32)[0:RIM])
         gated[n] = product
         for s in range(3):
             head[s, n] = grad[s]
-            acc = [sums[n, s, j] + grad[s] * slab[s, RIM - j : RIM - j + SUB, :] for j in range(taps)]
+            acc = [sums[n, s, j] + grad[s] * slab[s, 0, RIM - j : RIM - j + SUB, :] for j in range(taps)]
             place = pl.ds(s * taps * half + lax.rem(n, half), taps, stride=half)
             totals[n // half, place, :] = fold(acc)[:taps]
         return carry
@@ -118,12 +128,11 @@
         for s in range(3):
             c = lanes_at(s * chans + n * LANES)
             tile = after[:, c].astype(F32)
-            slab[s, 0:16, :] = p_ref[rows - 16 : rows, c].astype(F32)
-            slab[s, 16 : 16 + RIM, :] = tile
+            slab[s, 0, 0:16, :] = p_ref[rows - 16 : rows, c].astype(F32)
+            slab[s, 0, 16 : 16 + RIM, :] = tile
             cotangent = jnp.where(sub == s, pltpu.roll(tile, s + 2, 0), cotangent)
             cotangent = jnp.where(sub == s + 3, pltpu.roll(tile, s + 4, 0), cotangent)
-        tap = [tap_rows(filters, s, n) for s in range(3)]
-        conv = [convolve(tap, slab, s, 16) for s in range(3)]
+        conv = [convolve(tap_rows(filters, s, n), slab, s, 0, 16) for s in range(3)]
         _, grad = gates(*conv, cotangent)
         for s in range(3):
             following[s, n] = grad[s]
@@ -177,6 +186,10 @@
         copy.wait()
 
 
+def in_hbm(array):
+    return pltpu.with_memory_space_constraint(array, pltpu.HBM)
+
+
 def params(**kw):
     return pltpu.CompilerParams(vmem_limit_bytes=28 * 2**20, **kw)
 
@@ -193,17 +206,22 @@
             jax.ShapeDtypeStruct((3, groups, rows, LANES), F32),
             jax.ShapeDtypeStruct((groups, 3, taps, SUB, LANES), F32),
         ),
-        in_specs=[VMEM] * 3,
+        in_specs=[VMEM, HBM, VMEM],
         out_specs=(VMEM,) * 3,
-        scratch_shapes=[pltpu.VMEM((3, rows, LANES), F32), pltpu.VMEM((rows, LANES), F32)],
+        scratch_shapes=[
+            pltpu.VMEM((3, groups, rows, LANES), F32),
+            pltpu.VMEM((rows, chans), BF),
+            pltpu.VMEM((rows, LANES), F32),
+            pltpu.SemaphoreType.DMA,
+        ],
         cost_estimate=pl.CostEstimate(flops=4 * taps * rows * columns, bytes_accessed=2 * rows * (columns + chans), transcendentals=0),
         compiler_params=params(),
         name="inner",
-    )(projected, upstream, filters)
-
-
-def call_rim(projected, upstream, filters, before, sums):
-    chans = upstream.shape[1]
+    )(projected, in_hbm(upstream), filters)
+
+
+def call_rim(projected, u_head, filters, before, sums):
+    chans = u_head.shape[1]
     groups = chans // LANES
     taps = filters.shape[1]
     return pl.pallas_call(
@@ -215,10 +233,10 @@
         ),
         in_specs=[VMEM] * 5,
         out_specs=(VMEM,) * 3,
-        scratch_shapes=[pltpu.VMEM((3, RIM + 16, LANES), F32)],
+        scratch_shapes=[pltpu.VMEM((3, 1, RIM + 16, LANES), F32)],
         compiler_params=params(),
         name="rim",
-    )(projected, upstream, filters, before, sums)
+    )(projected, u_head, filters, before, sums)
 
 
 def call_next(projected, filters, after):
@@ -228,7 +246,7 @@
         out_shape=jax.ShapeDtypeStruct((3, groups, RIM, LANES), F32),
         in_specs=[VMEM] * 3,
         out_specs=VMEM,
-        scratch_shapes=[pltpu.VMEM((3, 16 + RIM, LANES), F32)],
+        scratch_shapes=[pltpu.VMEM((3, 1, 16 + RIM, LANES), F32)],
         compiler_params=params(),
         name="next",
     )(projected, filters, after)
@@ -265,7 +283,7 @@
         back_kernel,
         out_shape=(jax.ShapeDtypeStruct((rows, chans), BF), jax.ShapeDtypeStruct((rows, 3 * chans), BF)),
         in_specs=[VMEM] * 6,
-        out_specs=(pl.BlockSpec(memory_space=pltpu.HBM),) * 2,
+        out_specs=(HBM,) * 2,
         scratch_shapes=[
             pltpu.VMEM((3, 4 * RIM, LANES), F32),
             pltpu.VMEM((rows, chans), BF),
@@ -281,12 +299,12 @@
     return [[(1 << b) ^ 1] for b in reversed(range(3, bits))] + [[m for m in (3, 5, 6) if m < 1 << bits]]
 
 
-def pack_kernel(p_ref, u_ref, u_out, near, far, ends, sems):
+def pack_kernel(p_ref, u_ref, u_head, near, far, ends, sems):
     rows, columns = p_ref.shape
     copies = [
         pltpu.make_async_copy(p_ref.at[0:16], ends.at[0:16], sems.at[0]),
         pltpu.make_async_copy(p_ref.at[rows - 16 : rows], ends.at[16:32], sems.at[1]),
-        pltpu.make_async_copy(u_ref, u_out, sems.at[2]),
+        pltpu.make_async_copy(u_ref.at[0:16], u_head, sems.at[2]),
     ]
     for copy in copies:
         copy.start()
@@ -297,7 +315,7 @@
     sub = lax.broadcasted_iota(jnp.int32, (SUB, LANES), 0)
 
     def group(n, carry):
-        cotangent = u_out[0:16, lanes_at(n * LANES)].astype(F32)[:RIM]
+        cotangent = u_head[:, lanes_at(n * LANES)].astype(F32)[:RIM]
         for s in range(3):
             c = lanes_at(s * chans + n * LANES)
             last = pltpu.roll(ends[16:32, c].astype(F32)[16 - RIM :], REACH, 0)
@@ -316,13 +334,13 @@
     shape = jax.ShapeDtypeStruct((RIM, columns), BF)
     return pl.pallas_call(
         pack_kernel,
-        out_shape=(jax.ShapeDtypeStruct(upstream.shape, BF), shape, shape),
-        in_specs=[pl.BlockSpec(memory_space=pltpu.HBM)] * 2,
+        out_shape=(jax.ShapeDtypeStruct((16, upstream.shape[1]), BF), shape, shape),
+        in_specs=[HBM] * 2,
         out_specs=(VMEM,) * 3,
         scratch_shapes=[pltpu.VMEM((32, columns), BF), pltpu.SemaphoreType.DMA((3,))],
         compiler_params=params(),
         name="pack",
-    )(*[pltpu.with_memory_space_constraint(a, pltpu.HBM) for a in (projected, upstream)])
+    )(in_hbm(projected), in_hbm(upstream))
 
 
 def swap(array, partner):
@@ -347,23 +365,23 @@
     ways = lax.axis_size("seq")
     me = lax.axis_index("seq")
     even = me % 2 == 0
-    upstream, near, far = call_pack(projected, upstream)
+    u_head, near, far = call_pack(projected, upstream)
     far = trade_far(far)
     near = swap(near, lambda i: i ^ 1)
     before = jnp.where(even, far, near)
     after = jnp.where(even, near, far)
     before = jnp.where(me == 0, jnp.zeros_like(before), before)
     after = jnp.where(me == ways - 1, jnp.zeros_like(after), after)
-    return upstream, before, after
+    return u_head, before, after
 
 
 def shards(projected, filters, upstream):
     rows = projected.shape[0]
     ways = lax.axis_size("seq")
     me = lax.axis_index("seq")
-    upstream, before, after = rims(projected, upstream)
+    u_head, before, after = rims(projected, upstream)
     gated, grads, sums = call_inner(projected, upstream, filters)
-    gated_head, head, halves = call_rim(projected, upstream, filters, before, sums)
+    gated_head, head, halves = call_rim(projected, u_head, filters, before, sums)
     bits = ways.bit_length() - 1
     odd = sum((me >> b) & 1 for b in range(bits)) % 2 == 1
     mine = jnp.where(odd, halves[1], halves[0])

time: 24.4 us -> 23.8 us (0.975)
  Pallas kernels: 9.39 us -> 8.76 us
    pallas_call x1, Pallas kernels: 3.79 us -> 3.36 us  [call_inner(): pl.pallas_call(inner_kernel, out_shape=(jax.ShapeDtypeStruct((groups, row...]
  transfers between devices with their start and end apart: 8 -> 8, of which waited for: 4 -> 4; matrix products, arithmetic and copies ran while one was open for 0% -> 0% of each run, Pallas kernels for 27% -> 26%
where the time goes in v5:
time: 23.8 us; the launch traced here: 23.6 us
  starting transfers between devices  9.5 us (40%)
  Pallas kernels  8.76 us (37%)
  waiting for transfers between devices  4.52 us (19%)
  between operations  0.73 us (3%)
    ppermute x7, starting transfers between devices, swap(): return lax.ppermute(array, 'seq', [(i, partner(i)) for i in range(ways)])  6.47 us
    ppermute x7, waiting for transfers between devices, swap(): return lax.ppermute(array, 'seq', [(i, partner(i)) for i in range(ways)])  4.52 us
    pallas_call x1, Pallas kernels, call_inner(): pl.pallas_call(inner_kernel, out_shape=(jax.ShapeDtypeStruct((groups, row...  3.36 us
    ppermute x1, starting transfers between devices, trade_far(): return lax.ppermute(array, ('groups', 'seq'), pairs)  3.03 us
    pallas_call x1, Pallas kernels, call_back(): pl.pallas_call(back_kernel, out_shape=(jax.ShapeDtypeStruct((rows, chans)...  2.57 us
    pallas_call x1, Pallas kernels, call_pack(): pl.pallas_call(pack_kernel, out_shape=(jax.ShapeDtypeStruct((16, upstream...  1.28 us
    pallas_call x1, Pallas kernels, call_place(): pl.pallas_call(functools.partial(place_kernel, scale, bits), out_shape=ja...  0.74 us
    pallas_call x1, Pallas kernels, call_rim(): pl.pallas_call(rim_kernel, out_shape=(jax.ShapeDtypeStruct((groups, RIM,...  0.54 us
  transfers between devices with their start and end apart: 8, of which 4 were waited for; matrix products, arithmetic and copies ran while one was open for 0% of the time, Pallas kernels for 26%

profile of v5, /device:TPU:0, one launch (start us, length us, event | category | flops | bytes accessed | tf_op | source)
XLA Modules:
  0.0 23.6 jit_solution(2541271937780599508)
XLA Ops:
  0.6 0.0 copy-start
  0.6 0.0 copy-start.1
  0.6 1.3 %pack.1 = (bf16[16,2048]{1,0:T(8,128)(2,1)S(1)}, bf16[8,6144]{1,0:T(8,128)(2,1)S(1)}, bf16[8,6144]{1,0:T(8,128)(2,1)S(1)}) custom-call(bf16[128,6144]{1,0:T(8,128)(2,1)} %p_ref.7, bf16[128,2048]{1,0:T(8,128)(2,1)} %u_hbm.1), custom_call_target="tpu_custom_call" | custom-call | tf_op jit(solution)/shard_map/pack/pallas_call | solution.py:335
  1.9 3.0 %collective-permute-start = (bf16[8,6144]{1,0:T(8,128)(2,1)S(1)}, bf16[8,6144]{1,0:T(8,128)(2,1)S(1)}, u32[]{:S(2)}, u32[]{:S(2)}) collective-permute-start(bf16[8,6144]{1,0:T(8,128)(2,1)S(1)} %get-tuple-element.26), channel_id=1, source_target_pairs={{0,16},{1,2},{2,1},{3,4},{4,3},{5,6},{6,5},{7,8},{8,7},{9,10},{10,... | collective-permute-start | bytes 294920 | tf_op jit(solution)/shard_map/ppermute | solution.py:361
  5.0 0.1 collective-permute-start.1
  5.1 0.0 copy-done
  5.1 0.0 copy-done.1
  5.1 3.4 %inner.1 = (f32[16,128,128]{2,1,0:T(8,128)S(1)}, f32[3,16,128,128]{3,2,1,0:T(8,128)S(1)}, f32[16,3,7,8,128]{4,3,2,1,0:T(8,128)S(1)}) custom-call(bf16[128,6144]{1,0:T(8,128)(2,1)S(1)} %copy-done, bf16[128,2048]{1,0:T(8,128)(2,1)} %u_hbm.1, f32[3,7,2048]{2,1,0:T(8,128)S(1)} %copy-done.1), custom_call_target="tpu_custom_call" | custom-call | flops 22020096 | bytes 2097152 | tf_op jit(solution)/shard_map/inner/pallas_call | solution.py:202
  8.4 0.0 collective-permute-done
  8.4 0.0 collective-permute-done.1
  8.5 0.5 %rim.1 = (f32[16,8,128]{2,1,0:T(8,128)S(1)}, f32[3,16,8,128]{3,2,1,0:T(8,128)S(1)}, f32[2,168,128]{2,1,0:T(8,128)S(1)}) custom-call(bf16[128,6144]{1,0:T(8,128)(2,1)S(1)} %copy-done, bf16[16,2048]{1,0:T(8,128)(2,1)S(1)} %get-tuple-element.25.u_head, f32[3,7,2048]{2,1,0:T(8,128)S(1)} %copy-done.1, bf16[8,6144]{1,0:T(8,128)(2,1)S(1)} %get-tuple-element.48.before, ...), custom_call_target="tpu_custom_call" | custom-call | tf_op jit(solution)/shard_map/rim/pallas_call | solution.py:227
  9.0 0.5 %collective-permute-start.2 = (f32[168,128]{1,0:T(8,128)S(1)}, f32[168,128]{1,0:T(8,128)S(1)}, u32[]{:S(2)}, u32[]{:S(2)}) collective-permute-start(f32[168,128]{1,0:T(8,128)S(1)} %select_bitcast_fusion), channel_id=1, source_target_pairs={{0,1},{1,0},{2,3},{3,2},{4,5},{5,4},{6,7},{7,6},{8,9},{9,8},{10,11... | collective-permute-start | bytes 258056 | tf_op jit(solution)/shard_map/ppermute | solution.py:348
  9.5 0.9 %collective-permute-done.2 = f32[168,128]{1,0:T(8,128)S(1)} collective-permute-done((f32[168,128]{1,0:T(8,128)S(1)}, f32[168,128]{1,0:T(8,128)S(1)}, u32[]{:S(2)}, u32[]{:S(2)}) %collective-permute-start.2) | collective-permute-done | bytes 86048 | tf_op jit(solution)/shard_map/ppermute | solution.py:348
  10.5 2.4 %collective-permute-start.3 = (bf16[168,128]{1,0:T(8,128)(2,1)S(1)}, bf16[168,128]{1,0:T(8,128)(2,1)S(1)}, u32[]{:S(2)}, u32[]{:S(2)}) collective-permute-start(bf16[168,128]{1,0:T(8,128)(2,1)S(1)} %fusion), channel_id=1, source_target_pairs={{0,9},{1,8},{2,11},{3,10},{4,13},{5,12},{6,15},{7,14},{8,1},{9,0},... | collective-permute-start | bytes 129032 | tf_op jit(solution)/shard_map/ppermute | solution.py:348
  12.9 0.3 %next.1.following = f32[3,16,8,128]{3,2,1,0:T(8,128)S(1)} custom-call(bf16[128,6144]{1,0:T(8,128)(2,1)S(1)} %copy-done, f32[3,7,2048]{2,1,0:T(8,128)S(1)} %copy-done.1, bf16[8,6144]{1,0:T(8,128)(2,1)S(1)} %get-tuple-element.31.after), custom_call_target="tpu_custom_call" | custom-call | tf_op jit(solution)/shard_map/next/pallas_call | solution.py:244
  13.1 1.8 %collective-permute-done.3 = bf16[168,128]{1,0:T(8,128)(2,1)S(1)} collective-permute-done((bf16[168,128]{1,0:T(8,128)(2,1)S(1)}, bf16[168,128]{1,0:T(8,128)(2,1)S(1)}, u32[]{:S(2)}, u32[]{:S(2)}) %collective-permute-start.3) | collective-permute-done | bytes 43040 | tf_op jit(solution)/shard_map/ppermute | solution.py:348
  14.9 2.7 %collective-permute-start.6 = (bf16[168,128]{1,0:T(8,128)(2,1)S(1)}, bf16[168,128]{1,0:T(8,128)(2,1)S(1)}, u32[]{:S(2)}, u32[]{:S(2)}) collective-permute-start(bf16[168,128]{1,0:T(8,128)(2,1)S(1)} %add_convert_fusion), channel_id=1, source_target_pairs={{0,6},{1,7},{2,4},{3,5},{4,2},{5,3},{6,0},{7,1},{8,14},{9,15},{10,... | collective-permute-start | bytes 129032 | tf_op jit(solution)/shard_map/ppermute | solution.py:348
  17.6 0.0 collective-permute-start.5
  17.6 0.6 %collective-permute-start.4 = (bf16[168,128]{1,0:T(8,128)(2,1)S(1)}, bf16[168,128]{1,0:T(8,128)(2,1)S(1)}, u32[]{:S(2)}, u32[]{:S(2)}) collective-permute-start(bf16[168,128]{1,0:T(8,128)(2,1)S(1)} %add_convert_fusion), channel_id=1, source_target_pairs={{0,3},{1,2},{2,1},{3,0},{4,7},{5,6},{6,5},{7,4},{8,11},{9,10},{10,... | collective-permute-start | bytes 129032 | tf_op jit(solution)/shard_map/ppermute | solution.py:348
  18.2 2.6 %back.1 = (bf16[128,2048]{1,0:T(8,128)(2,1)}, bf16[128,6144]{1,0:T(8,128)(2,1)}) custom-call(f32[3,7,2048]{2,1,0:T(8,128)S(1)} %copy-done.1, f32[16,128,128]{2,1,0:T(8,128)S(1)} %get-tuple-element.35.gated_in, f32[3,16,128,128]{3,2,1,0:T(8,128)S(1)} %get-tuple-element.36.grads, f32[16,8,128]{2,1,0:T(8,128)S(1)} %get-tuple-element.37.gated_head, ...), custom_call_target="tpu_custom_call" | custom-call | flops 11010048 | bytes 2097152 | tf_op jit(solution)/shard_map/back/pallas_call | solution.py:282
  20.8 0.0 collective-permute-done.6
  20.8 0.7 %collective-permute-done.5 = bf16[168,128]{1,0:T(8,128)(2,1)S(1)} collective-permute-done((bf16[168,128]{1,0:T(8,128)(2,1)S(1)}, bf16[168,128]{1,0:T(8,128)(2,1)S(1)}, u32[]{:S(2)}, u32[]{:S(2)}) %collective-permute-start.5) | collective-permute-done | bytes 43040 | tf_op jit(solution)/shard_map/ppermute | solution.py:348
  21.5 0.0 collective-permute-done.4
  21.5 0.2 collective-permute-start.7
  21.7 1.1 %collective-permute-done.7.other = f32[168,128]{1,0:T(8,128)S(1)} collective-permute-done((f32[168,128]{1,0:T(8,128)S(1)}, f32[168,128]{1,0:T(8,128)S(1)}, u32[]{:S(2)}, u32[]{:S(2)}) %collective-permute-start.7) | collective-permute-done | bytes 86048 | tf_op jit(solution)/shard_map/ppermute | solution.py:348
  22.9 0.7 %place.1 = f32[3,7,2048]{2,1,0:T(8,128)} custom-call(f32[168,128]{1,0:T(8,128)S(1)} %add_add_fusion.mine, f32[168,128]{1,0:T(8,128)S(1)} %collective-permute-done.7.other), custom_call_target="tpu_custom_call" | custom-call | tf_op jit(solution)/shard_map/place/pallas_call | solution.py:268
  (5 shorter events, 0.1 us)
Async XLA Ops:
  0.6 4.4 %copy-start = (bf16[128,6144]{1,0:T(8,128)(2,1)S(1)}, bf16[128,6144]{1,0:T(8,128)(2,1)}, u32[]{:S(2)}) copy-start(bf16[128,6144]{1,0:T(8,128)(2,1)} %p_ref.7) | copy-start | bytes 4718596
  0.6 4.4 %copy-start.1 = (f32[3,7,2048]{2,1,0:T(8,128)S(1)}, f32[3,7,2048]{2,1,0:T(8,128)}, u32[]{:S(2)}) copy-start(f32[3,7,2048]{2,1,0:T(8,128)} %filters.7) | copy-start | bytes 516100
  1.9 6.5 %collective-permute-start = (bf16[8,6144]{1,0:T(8,128)(2,1)S(1)}, bf16[8,6144]{1,0:T(8,128)(2,1)S(1)}, u32[]{:S(2)}, u32[]{:S(2)}) collective-permute-start(bf16[8,6144]{1,0:T(8,128)(2,1)S(1)} %get-tuple-element.26), channel_id=1, source_target_pairs={{0,16},{1,2},{2,1},{3,4},{4,3},{5,6},{6,5},{7,8},{8,7},{9,10},{10,... | collective-permute-start | bytes 294920 | tf_op jit(solution)/shard_map/ppermute | solution.py:361
  5.0 3.5 %collective-permute-start.1 = (bf16[8,6144]{1,0:T(8,128)(2,1)S(1)}, bf16[8,6144]{1,0:T(8,128)(2,1)S(1)}, u32[]{:S(2)}, u32[]{:S(2)}) collective-permute-start(bf16[8,6144]{1,0:T(8,128)(2,1)S(1)} %get-tuple-element.27), channel_id=1, source_target_pairs={{0,1},{1,0},{2,3},{3,2},{4,5},{5,4},{6,7},{7,6},{8,9},{9,8},{10,11... | collective-permute-start | bytes 294920 | tf_op jit(solution)/shard_map/ppermute | solution.py:348
  9.0 1.4 %collective-permute-start.2 = (f32[168,128]{1,0:T(8,128)S(1)}, f32[168,128]{1,0:T(8,128)S(1)}, u32[]{:S(2)}, u32[]{:S(2)}) collective-permute-start(f32[168,128]{1,0:T(8,128)S(1)} %select_bitcast_fusion), channel_id=1, source_target_pairs={{0,1},{1,0},{2,3},{3,2},{4,5},{5,4},{6,7},{7,6},{8,9},{9,8},{10,11... | collective-permute-start | bytes 258056 | tf_op jit(solution)/shard_map/ppermute | solution.py:348
  10.5 4.4 %collective-permute-start.3 = (bf16[168,128]{1,0:T(8,128)(2,1)S(1)}, bf16[168,128]{1,0:T(8,128)(2,1)S(1)}, u32[]{:S(2)}, u32[]{:S(2)}) collective-permute-start(bf16[168,128]{1,0:T(8,128)(2,1)S(1)} %fusion), channel_id=1, source_target_pairs={{0,9},{1,8},{2,11},{3,10},{4,13},{5,12},{6,15},{7,14},{8,1},{9,0},... | collective-permute-start | bytes 129032 | tf_op jit(solution)/shard_map/ppermute | solution.py:348
  14.9 5.9 %collective-permute-start.6 = (bf16[168,128]{1,0:T(8,128)(2,1)S(1)}, bf16[168,128]{1,0:T(8,128)(2,1)S(1)}, u32[]{:S(2)}, u32[]{:S(2)}) collective-permute-start(bf16[168,128]{1,0:T(8,128)(2,1)S(1)} %add_convert_fusion), channel_id=1, source_target_pairs={{0,6},{1,7},{2,4},{3,5},{4,2},{5,3},{6,0},{7,1},{8,14},{9,15},{10,... | collective-permute-start | bytes 129032 | tf_op jit(solution)/shard_map/ppermute | solution.py:348
  17.6 3.9 %collective-permute-start.5 = (bf16[168,128]{1,0:T(8,128)(2,1)S(1)}, bf16[168,128]{1,0:T(8,128)(2,1)S(1)}, u32[]{:S(2)}, u32[]{:S(2)}) collective-permute-start(bf16[168,128]{1,0:T(8,128)(2,1)S(1)} %add_convert_fusion), channel_id=1, source_target_pairs={{0,5},{1,4},{2,7},{3,6},{4,1},{5,0},{6,3},{7,2},{8,13},{9,12},{10,... | collective-permute-start | bytes 129032 | tf_op jit(solution)/shard_map/ppermute | solution.py:348
  17.6 3.9 %collective-permute-start.4 = (bf16[168,128]{1,0:T(8,128)(2,1)S(1)}, bf16[168,128]{1,0:T(8,128)(2,1)S(1)}, u32[]{:S(2)}, u32[]{:S(2)}) collective-permute-start(bf16[168,128]{1,0:T(8,128)(2,1)S(1)} %add_convert_fusion), channel_id=1, source_target_pairs={{0,3},{1,2},{2,1},{3,0},{4,7},{5,6},{6,5},{7,4},{8,11},{9,10},{10,... | collective-permute-start | bytes 129032 | tf_op jit(solution)/shard_map/ppermute | solution.py:348
  21.5 1.3 %collective-permute-start.7 = (f32[168,128]{1,0:T(8,128)S(1)}, f32[168,128]{1,0:T(8,128)S(1)}, u32[]{:S(2)}, u32[]{:S(2)}) collective-permute-start(f32[168,128]{1,0:T(8,128)S(1)} %add_add_fusion.mine), channel_id=1, source_target_pairs={{0,1},{1,0},{2,3},{3,2},{4,5},{5,4},{6,7},{7,6},{8,9},{9,8},{10,11... | collective-permute-start | bytes 258056 | tf_op jit(solution)/shard_map/ppermute | solution.py:348

commit v6 on v5

--- a/solution.py
+++ b/solution.py
@@ -16,6 +16,7 @@
 VMEM = pl.BlockSpec(memory_space=pltpu.VMEM)
 HBM = pl.BlockSpec(memory_space=pltpu.HBM)
 UNROLL = 4
+RIM_UNROLL = 4
 
 
 def lanes_at(start):
@@ -94,28 +95,34 @@
     return arrays[0]
 
 
-def rim_kernel(p_ref, u_head, filters, before, sums, gated, head, totals, slab):
-    rows, columns = p_ref.shape
+def own_half(bits):
+    me = lax.axis_index("seq")
+    return lax.rem(sum(lax.rem(me // 2**b, 2) for b in range(bits)), 2)
+
+
+def rim_kernel(bits, own, p_ref, u_head, filters, before, sums, gated, head, totals, slab):
+    _, columns = p_ref.shape
     chans = columns // 3
     taps = filters.shape[1]
     half = chans // 2 // LANES
-
-    def group(n, carry):
+    first = half * (own_half(bits) if own else 1 - own_half(bits))
+
+    def group(m, carry):
+        n = first + m
         for s in range(3):
             c = lanes_at(s * chans + n * LANES)
             slab[s, 0, 0:RIM, :] = pltpu.roll(before[:, c].astype(F32), RIM - REACH, 0)
             slab[s, 0, RIM : RIM + 16, :] = p_ref[0:16, c].astype(F32)
         conv = [convolve(tap_rows(filters, s, n), slab, s, 0, RIM) for s in range(3)]
         product, grad = gates(*conv, u_head[:, lanes_at(n * LANES)].astype(F32)[0:RIM])
-        gated[n] = product
-        for s in range(3):
-            head[s, n] = grad[s]
+        gated[m] = product
+        for s in range(3):
+            head[s, m] = grad[s]
             acc = [sums[n, s, j] + grad[s] * slab[s, 0, RIM - j : RIM - j + SUB, :] for j in range(taps)]
-            place = pl.ds(s * taps * half + lax.rem(n, half), taps, stride=half)
-            totals[n // half, place, :] = fold(acc)[:taps]
-        return carry
-
-    lax.fori_loop(0, chans // LANES, group, 0, unroll=UNROLL)
+            totals[pl.ds(s * taps * half + m, taps, stride=half), :] = fold(acc)[:taps]
+        return carry
+
+    lax.fori_loop(0, half, group, 0, unroll=RIM_UNROLL)
 
 
 def next_kernel(p_ref, filters, after, following, slab):
@@ -141,14 +148,16 @@
     lax.fori_loop(0, chans // LANES, group, 0, unroll=UNROLL)
 
 
-def back_kernel(filters, gated_in, grads, gated_head, head, following, gated, out, slab, gated_slab, out_slab, sems):
+def back_kernel(bits, filters, gated_in, grads, own_gated, own_head, other_gated, other_head, following, gated, out, slab, gated_slab, out_slab, sems):
     rows, columns = out.shape
     chans = columns // 3
     taps = filters.shape[1]
+    half = chans // 2 // LANES
+    mine = own_half(bits)
 
     def round_gated(n, carry):
         c = lanes_at(n * LANES)
-        gated_slab[0:16, c] = jnp.concatenate([gated_head[n], gated_in[n, RIM:16, :]], 0).astype(BF)
+        gated_slab[0:16, c] = jnp.concatenate([jnp.where(n // half == mine, own_gated[lax.rem(n, half)], other_gated[lax.rem(n, half)]), gated_in[n, RIM:16, :]], 0).astype(BF)
         gated_slab[16:rows, c] = gated_in[n, 16:rows, :].astype(BF)
         return carry
 
@@ -162,7 +171,8 @@
 
         def group(n, carry, s=s):
             tap = tap_rows(filters, s, n)
-            slab[s, 0:RIM, :] = head[s, n]
+            m = lax.rem(n, half)
+            slab[s, 0:RIM, :] = jnp.where(n // half == mine, own_head[s, m], other_head[s, m])
             slab[s, RIM : 2 * RIM, :] = grads[s, n, RIM : 2 * RIM, :]
             slab[s, 2 * RIM : 3 * RIM, :] = grads[s, n, rows - RIM : rows, :]
             slab[s, 3 * RIM : 4 * RIM, :] = following[s, n]
@@ -220,22 +230,21 @@
     )(projected, in_hbm(upstream), filters)
 
 
-def call_rim(projected, u_head, filters, before, sums):
-    chans = u_head.shape[1]
-    groups = chans // LANES
-    taps = filters.shape[1]
-    return pl.pallas_call(
-        rim_kernel,
+def call_rim(bits, own, projected, u_head, filters, before, sums):
+    half = u_head.shape[1] // 2 // LANES
+    taps = filters.shape[1]
+    return pl.pallas_call(
+        functools.partial(rim_kernel, bits, own),
         out_shape=(
-            jax.ShapeDtypeStruct((groups, RIM, LANES), F32),
-            jax.ShapeDtypeStruct((3, groups, RIM, LANES), F32),
-            jax.ShapeDtypeStruct((2, 3 * taps * groups // 2, LANES), F32),
+            jax.ShapeDtypeStruct((half, RIM, LANES), F32),
+            jax.ShapeDtypeStruct((3, half, RIM, LANES), F32),
+            jax.ShapeDtypeStruct((3 * taps * half, LANES), F32),
         ),
         in_specs=[VMEM] * 5,
         out_specs=(VMEM,) * 3,
         scratch_shapes=[pltpu.VMEM((3, 1, RIM + 16, LANES), F32)],
         compiler_params=params(),
-        name="rim",
+        name="rim_own" if own else "rim_other",
     )(projected, u_head, filters, before, sums)
 
 
@@ -255,8 +264,7 @@
 def place_kernel(scale, bits, mine, other, out):
     _, taps, chans = out.shape
     half = chans // 2 // LANES
-    me = lax.axis_index("seq")
-    odd = lax.rem(sum(lax.rem(me // 2**b, 2) for b in range(bits)), 2)
+    odd = own_half(bits)
     for s in range(3):
         for n in range(half):
             place = pl.ds(s * taps * half + n, taps, stride=half)
@@ -275,14 +283,14 @@
     )(mine, other)
 
 
-def call_back(filters, gated, grads, gated_head, head, following):
+def call_back(bits, filters, gated, grads, *edges):
     taps = filters.shape[1]
     groups, rows, _ = gated.shape
     chans = groups * LANES
     return pl.pallas_call(
-        back_kernel,
+        functools.partial(back_kernel, bits),
         out_shape=(jax.ShapeDtypeStruct((rows, chans), BF), jax.ShapeDtypeStruct((rows, 3 * chans), BF)),
-        in_specs=[VMEM] * 6,
+        in_specs=[VMEM] * 8,
         out_specs=(HBM,) * 2,
         scratch_shapes=[
             pltpu.VMEM((3, 4 * RIM, LANES), F32),
@@ -293,7 +301,7 @@
         cost_estimate=pl.CostEstimate(flops=6 * taps * rows * chans, bytes_accessed=8 * rows * chans, transcendentals=0),
         compiler_params=params(),
         name="back",
-    )(filters, gated, grads, gated_head, head, following)
+    )(filters, gated, grads, *edges)
 
 def rounds(bits):
     return [[(1 << b) ^ 1] for b in reversed(range(3, bits))] + [[m for m in (3, 5, 6) if m < 1 << bits]]
@@ -378,14 +386,15 @@
 def shards(projected, filters, upstream):
     rows = projected.shape[0]
     ways = lax.axis_size("seq")
-    me = lax.axis_index("seq")
     u_head, before, after = rims(projected, upstream)
     gated, grads, sums = call_inner(projected, upstream, filters)
-    gated_head, head, halves = call_rim(projected, u_head, filters, before, sums)
     bits = ways.bit_length() - 1
-    odd = sum((me >> b) & 1 for b in range(bits)) % 2 == 1
-    mine = jnp.where(odd, halves[1], halves[0])
-    mine = mine + swap(jnp.where(odd, halves[0], halves[1]), lambda i: i ^ 1)
+    *other_edges, sent = call_rim(bits, False, projected, u_head, filters, before, sums)
+    sent, before = lax.optimization_barrier((sent, before))
+    got = swap(sent, lambda i: i ^ 1)
+    *own_edges, mine = call_rim(bits, True, projected, u_head, filters, before, sums)
+    got, mine = lax.optimization_barrier((got, mine))
+    mine = mine + got
     steps = rounds(bits)
     for step, masks in enumerate(steps):
         sent = mine.astype(BF)
@@ -398,7 +407,7 @@
             following = call_next(projected, filters, after)
             got, following = lax.optimization_barrier((got, following))
         if step == len(steps) - 1:
-            gated, grad_projected = call_back(filters, gated, grads, gated_head, head, following)
+            gated, grad_projected = call_back(bits, filters, gated, grads, *own_edges, *other_edges, following)
             got, gated, grad_projected = lax.optimization_barrier((got, gated, grad_projected))
         terms = [sent.astype(F32)] + [g.astype(F32) for g in got]
         while len(terms) > 1:

time: 23.8 us -> 23.5 us (0.987)
  waiting for transfers between devices: 4.52 us -> 4.14 us
    ppermute x7, waiting for transfers between devices: 4.52 us -> 4.13 us  [swap(): return lax.ppermute(array, 'seq', [(i, partner(i)) for i in range(ways)])]
    pallas_call x2 -> x3, Pallas kernels: 3.11 us -> 3.26 us  [the longest x1 2.69 us: call_back(): pl.pallas_call(functools.partial(back_kernel, bits), out_shape=(jax.Shape...]
  transfers between devices with their start and end apart: 8 -> 8, of which waited for: 4 -> 4; matrix products, arithmetic and copies ran while one was open for 0% -> 0% of each run, Pallas kernels for 26% -> 28%
where the time goes in v6:
time: 23.5 us; the launch traced here: 23.3 us
  starting transfers between devices  9.5 us (40%)
  Pallas kernels  8.9 us (38%)
  waiting for transfers between devices  4.14 us (18%)
  between operations  0.73 us (3%)
    ppermute x7, starting transfers between devices, swap(): return lax.ppermute(array, 'seq', [(i, partner(i)) for i in range(ways)])  6.47 us
    ppermute x7, waiting for transfers between devices, swap(): return lax.ppermute(array, 'seq', [(i, partner(i)) for i in range(ways)])  4.13 us
    pallas_call x1, Pallas kernels, call_inner(): pl.pallas_call(inner_kernel, out_shape=(jax.ShapeDtypeStruct((groups, row...  3.36 us
    ppermute x1, starting transfers between devices, trade_far(): return lax.ppermute(array, ('groups', 'seq'), pairs)  3.03 us
    pallas_call x1, Pallas kernels, call_back(): pl.pallas_call(functools.partial(back_kernel, bits), out_shape=(jax.Shape...  2.69 us
    pallas_call x1, Pallas kernels, call_pack(): pl.pallas_call(pack_kernel, out_shape=(jax.ShapeDtypeStruct((16, upstream...  1.28 us
    pallas_call x1, Pallas kernels, call_place(): pl.pallas_call(functools.partial(place_kernel, scale, bits), out_shape=ja...  0.74 us
    pallas_call x2, Pallas kernels, call_rim(): pl.pallas_call(functools.partial(rim_kernel, bits, own), out_shape=(jax.S...  0.57 us
  transfers between devices with their start and end apart: 8, of which 4 were waited for; matrix products, arithmetic and copies ran while one was open for 0% of the time, Pallas kernels for 28%

profile of v6, /device:TPU:0, one launch (start us, length us, event | category | flops | bytes accessed | tf_op | source)
XLA Modules:
  0.0 23.3 jit_solution(11898118105485051657)
XLA Ops:
  0.6 0.0 copy-start
  0.6 0.0 copy-start.1
  0.6 1.3 %pack.1 = (bf16[16,2048]{1,0:T(8,128)(2,1)S(1)}, bf16[8,6144]{1,0:T(8,128)(2,1)S(1)}, bf16[8,6144]{1,0:T(8,128)(2,1)S(1)}) custom-call(bf16[128,6144]{1,0:T(8,128)(2,1)} %p_ref.9, bf16[128,2048]{1,0:T(8,128)(2,1)} %u_hbm.1), custom_call_target="tpu_custom_call" | custom-call | tf_op jit(solution)/shard_map/pack/pallas_call | solution.py:343
  1.9 3.0 %collective-permute-start = (bf16[8,6144]{1,0:T(8,128)(2,1)S(1)}, bf16[8,6144]{1,0:T(8,128)(2,1)S(1)}, u32[]{:S(2)}, u32[]{:S(2)}) collective-permute-start(bf16[8,6144]{1,0:T(8,128)(2,1)S(1)} %get-tuple-element.33), channel_id=1, source_target_pairs={{0,16},{1,2},{2,1},{3,4},{4,3},{5,6},{6,5},{7,8},{8,7},{9,10},{10,... | collective-permute-start | bytes 294920 | tf_op jit(solution)/shard_map/ppermute | solution.py:369
  5.0 0.1 collective-permute-start.1
  5.1 0.0 copy-done
  5.1 0.0 copy-done.1
  5.1 3.4 %inner.1 = (f32[16,128,128]{2,1,0:T(8,128)S(1)}, f32[3,16,128,128]{3,2,1,0:T(8,128)S(1)}, f32[16,3,7,8,128]{4,3,2,1,0:T(8,128)S(1)}) custom-call(bf16[128,6144]{1,0:T(8,128)(2,1)S(1)} %copy-done, bf16[128,2048]{1,0:T(8,128)(2,1)} %u_hbm.1, f32[3,7,2048]{2,1,0:T(8,128)S(1)} %copy-done.1), custom_call_target="tpu_custom_call" | custom-call | flops 22020096 | bytes 2097152 | tf_op jit(solution)/shard_map/inner/pallas_call | solution.py:212
  8.4 0.0 collective-permute-done
  8.4 0.0 collective-permute-done.1
  8.5 0.3 %rim_other.1 = (f32[8,8,128]{2,1,0:T(8,128)S(1)}, f32[3,8,8,128]{3,2,1,0:T(8,128)S(1)}, f32[168,128]{1,0:T(8,128)S(1)}) custom-call(bf16[128,6144]{1,0:T(8,128)(2,1)S(1)} %copy-done, bf16[16,2048]{1,0:T(8,128)(2,1)S(1)} %get-tuple-element.32.u_head, f32[3,7,2048]{2,1,0:T(8,128)S(1)} %copy-done.1, bf16[8,6144]{1,0:T(8,128)(2,1)S(1)} %get-tuple-element.38.before, ...), custom_call_target="tpu_custom_call" | custom-call | tf_op jit(solution)/shard_map/rim_other/pallas_call | solution.py:236
  8.8 0.5 %collective-permute-start.2 = (f32[168,128]{1,0:T(8,128)S(1)}, f32[168,128]{1,0:T(8,128)S(1)}, u32[]{:S(2)}, u32[]{:S(2)}) collective-permute-start(f32[168,128]{1,0:T(8,128)S(1)} %get-tuple-element.37), channel_id=1, source_target_pairs={{0,1},{1,0},{2,3},{3,2},{4,5},{5,4},{6,7},{7,6},{8,9},{9,8},{10,11... | collective-permute-start | bytes 258056 | tf_op jit(solution)/shard_map/ppermute | solution.py:356
  9.3 0.3 %rim_own.1 = (f32[8,8,128]{2,1,0:T(8,128)S(1)}, f32[3,8,8,128]{3,2,1,0:T(8,128)S(1)}, f32[168,128]{1,0:T(8,128)S(1)}) custom-call(bf16[128,6144]{1,0:T(8,128)(2,1)S(1)} %copy-done, bf16[16,2048]{1,0:T(8,128)(2,1)S(1)} %get-tuple-element.32.u_head, f32[3,7,2048]{2,1,0:T(8,128)S(1)} %copy-done.1, bf16[8,6144]{1,0:T(8,128)(2,1)S(1)} %get-tuple-element.38.before, ...), custom_call_target="tpu_custom_call" | custom-call | tf_op jit(solution)/shard_map/rim_own/pallas_call | solution.py:236
  9.6 0.7 %collective-permute-done.2 = f32[168,128]{1,0:T(8,128)S(1)} collective-permute-done((f32[168,128]{1,0:T(8,128)S(1)}, f32[168,128]{1,0:T(8,128)S(1)}, u32[]{:S(2)}, u32[]{:S(2)}) %collective-permute-start.2) | collective-permute-done | bytes 86048 | tf_op jit(solution)/shard_map/ppermute | solution.py:356
  10.2 2.4 %collective-permute-start.3 = (bf16[168,128]{1,0:T(8,128)(2,1)S(1)}, bf16[168,128]{1,0:T(8,128)(2,1)S(1)}, u32[]{:S(2)}, u32[]{:S(2)}) collective-permute-start(bf16[168,128]{1,0:T(8,128)(2,1)S(1)} %add_convert_fusion.1), channel_id=1, source_target_pairs={{0,9},{1,8},{2,11},{3,10},{4,13},{5,12},{6,15},{7,14},{8,1},{9,0},... | collective-permute-start | bytes 129032 | tf_op jit(solution)/shard_map/ppermute | solution.py:356
  12.6 0.3 %next.1.following = f32[3,16,8,128]{3,2,1,0:T(8,128)S(1)} custom-call(bf16[128,6144]{1,0:T(8,128)(2,1)S(1)} %copy-done, f32[3,7,2048]{2,1,0:T(8,128)S(1)} %copy-done.1, bf16[8,6144]{1,0:T(8,128)(2,1)S(1)} %get-tuple-element.43.after), custom_call_target="tpu_custom_call" | custom-call | tf_op jit(solution)/shard_map/next/pallas_call | solution.py:253
  12.9 1.8 %collective-permute-done.3 = bf16[168,128]{1,0:T(8,128)(2,1)S(1)} collective-permute-done((bf16[168,128]{1,0:T(8,128)(2,1)S(1)}, bf16[168,128]{1,0:T(8,128)(2,1)S(1)}, u32[]{:S(2)}, u32[]{:S(2)}) %collective-permute-start.3) | collective-permute-done | bytes 43040 | tf_op jit(solution)/shard_map/ppermute | solution.py:356
  14.7 2.7 %collective-permute-start.6 = (bf16[168,128]{1,0:T(8,128)(2,1)S(1)}, bf16[168,128]{1,0:T(8,128)(2,1)S(1)}, u32[]{:S(2)}, u32[]{:S(2)}) collective-permute-start(bf16[168,128]{1,0:T(8,128)(2,1)S(1)} %add_convert_fusion), channel_id=1, source_target_pairs={{0,6},{1,7},{2,4},{3,5},{4,2},{5,3},{6,0},{7,1},{8,14},{9,15},{10,... | collective-permute-start | bytes 129032 | tf_op jit(solution)/shard_map/ppermute | solution.py:356
  17.4 0.0 collective-permute-start.5
  17.4 0.6 %collective-permute-start.4 = (bf16[168,128]{1,0:T(8,128)(2,1)S(1)}, bf16[168,128]{1,0:T(8,128)(2,1)S(1)}, u32[]{:S(2)}, u32[]{:S(2)}) collective-permute-start(bf16[168,128]{1,0:T(8,128)(2,1)S(1)} %add_convert_fusion), channel_id=1, source_target_pairs={{0,3},{1,2},{2,1},{3,0},{4,7},{5,6},{6,5},{7,4},{8,11},{9,10},{10,... | collective-permute-start | bytes 129032 | tf_op jit(solution)/shard_map/ppermute | solution.py:356
  17.9 2.7 %back.1 = (bf16[128,2048]{1,0:T(8,128)(2,1)}, bf16[128,6144]{1,0:T(8,128)(2,1)}) custom-call(f32[3,7,2048]{2,1,0:T(8,128)S(1)} %copy-done.1, f32[16,128,128]{2,1,0:T(8,128)S(1)} %get-tuple-element.47.gated_in, f32[3,16,128,128]{3,2,1,0:T(8,128)S(1)} %get-tuple-element.48.grads, f32[8,8,128]{2,1,0:T(8,128)S(1)} %get-tuple-element.49.own_gated, ...), custom_call_target="tpu_custom_call" | custom-call | flops 11010048 | bytes 2097152 | tf_op jit(solution)/shard_map/back/pallas_call | solution.py:290
  20.6 0.0 collective-permute-done.6
  20.7 0.6 %collective-permute-done.5 = bf16[168,128]{1,0:T(8,128)(2,1)S(1)} collective-permute-done((bf16[168,128]{1,0:T(8,128)(2,1)S(1)}, bf16[168,128]{1,0:T(8,128)(2,1)S(1)}, u32[]{:S(2)}, u32[]{:S(2)}) %collective-permute-start.5) | collective-permute-done | bytes 43040 | tf_op jit(solution)/shard_map/ppermute | solution.py:356
  21.2 0.0 collective-permute-done.4
  21.3 0.2 collective-permute-start.7
  21.5 1.1 %collective-permute-done.7.other = f32[168,128]{1,0:T(8,128)S(1)} collective-permute-done((f32[168,128]{1,0:T(8,128)S(1)}, f32[168,128]{1,0:T(8,128)S(1)}, u32[]{:S(2)}, u32[]{:S(2)}) %collective-permute-start.7) | collective-permute-done | bytes 86048 | tf_op jit(solution)/shard_map/ppermute | solution.py:356
  22.6 0.7 %place.1 = f32[3,7,2048]{2,1,0:T(8,128)} custom-call(f32[168,128]{1,0:T(8,128)S(1)} %add_add_fusion.mine, f32[168,128]{1,0:T(8,128)S(1)} %collective-permute-done.7.other), custom_call_target="tpu_custom_call" | custom-call | tf_op jit(solution)/shard_map/place/pallas_call | solution.py:276
  (4 shorter events, 0.1 us)
Async XLA Ops:
  0.6 4.4 %copy-start = (bf16[128,6144]{1,0:T(8,128)(2,1)S(1)}, bf16[128,6144]{1,0:T(8,128)(2,1)}, u32[]{:S(2)}) copy-start(bf16[128,6144]{1,0:T(8,128)(2,1)} %p_ref.9) | copy-start | bytes 4718596
  0.6 4.4 %copy-start.1 = (f32[3,7,2048]{2,1,0:T(8,128)S(1)}, f32[3,7,2048]{2,1,0:T(8,128)}, u32[]{:S(2)}) copy-start(f32[3,7,2048]{2,1,0:T(8,128)} %filters.9) | copy-start | bytes 516100
  1.9 6.5 %collective-permute-start = (bf16[8,6144]{1,0:T(8,128)(2,1)S(1)}, bf16[8,6144]{1,0:T(8,128)(2,1)S(1)}, u32[]{:S(2)}, u32[]{:S(2)}) collective-permute-start(bf16[8,6144]{1,0:T(8,128)(2,1)S(1)} %get-tuple-element.33), channel_id=1, source_target_pairs={{0,16},{1,2},{2,1},{3,4},{4,3},{5,6},{6,5},{7,8},{8,7},{9,10},{10,... | collective-permute-start | bytes 294920 | tf_op jit(solution)/shard_map/ppermute | solution.py:369
  5.0 3.5 %collective-permute-start.1 = (bf16[8,6144]{1,0:T(8,128)(2,1)S(1)}, bf16[8,6144]{1,0:T(8,128)(2,1)S(1)}, u32[]{:S(2)}, u32[]{:S(2)}) collective-permute-start(bf16[8,6144]{1,0:T(8,128)(2,1)S(1)} %get-tuple-element.34), channel_id=1, source_target_pairs={{0,1},{1,0},{2,3},{3,2},{4,5},{5,4},{6,7},{7,6},{8,9},{9,8},{10,11... | collective-permute-start | bytes 294920 | tf_op jit(solution)/shard_map/ppermute | solution.py:356
  8.8 1.4 %collective-permute-start.2 = (f32[168,128]{1,0:T(8,128)S(1)}, f32[168,128]{1,0:T(8,128)S(1)}, u32[]{:S(2)}, u32[]{:S(2)}) collective-permute-start(f32[168,128]{1,0:T(8,128)S(1)} %get-tuple-element.37), channel_id=1, source_target_pairs={{0,1},{1,0},{2,3},{3,2},{4,5},{5,4},{6,7},{7,6},{8,9},{9,8},{10,11... | collective-permute-start | bytes 258056 | tf_op jit(solution)/shard_map/ppermute | solution.py:356
  10.2 4.4 %collective-permute-start.3 = (bf16[168,128]{1,0:T(8,128)(2,1)S(1)}, bf16[168,128]{1,0:T(8,128)(2,1)S(1)}, u32[]{:S(2)}, u32[]{:S(2)}) collective-permute-start(bf16[168,128]{1,0:T(8,128)(2,1)S(1)} %add_convert_fusion.1), channel_id=1, source_target_pairs={{0,9},{1,8},{2,11},{3,10},{4,13},{5,12},{6,15},{7,14},{8,1},{9,0},... | collective-permute-start | bytes 129032 | tf_op jit(solution)/shard_map/ppermute | solution.py:356
  14.7 6.0 %collective-permute-start.6 = (bf16[168,128]{1,0:T(8,128)(2,1)S(1)}, bf16[168,128]{1,0:T(8,128)(2,1)S(1)}, u32[]{:S(2)}, u32[]{:S(2)}) collective-permute-start(bf16[168,128]{1,0:T(8,128)(2,1)S(1)} %add_convert_fusion), channel_id=1, source_target_pairs={{0,6},{1,7},{2,4},{3,5},{4,2},{5,3},{6,0},{7,1},{8,14},{9,15},{10,... | collective-permute-start | bytes 129032 | tf_op jit(solution)/shard_map/ppermute | solution.py:356
  17.4 3.9 %collective-permute-start.5 = (bf16[168,128]{1,0:T(8,128)(2,1)S(1)}, bf16[168,128]{1,0:T(8,128)(2,1)S(1)}, u32[]{:S(2)}, u32[]{:S(2)}) collective-permute-start(bf16[168,128]{1,0:T(8,128)(2,1)S(1)} %add_convert_fusion), channel_id=1, source_target_pairs={{0,5},{1,4},{2,7},{3,6},{4,1},{5,0},{6,3},{7,2},{8,13},{9,12},{10,... | collective-permute-start | bytes 129032 | tf_op jit(solution)/shard_map/ppermute | solution.py:356
  17.4 3.9 %collective-permute-start.4 = (bf16[168,128]{1,0:T(8,128)(2,1)S(1)}, bf16[168,128]{1,0:T(8,128)(2,1)S(1)}, u32[]{:S(2)}, u32[]{:S(2)}) collective-permute-start(bf16[168,128]{1,0:T(8,128)(2,1)S(1)} %add_convert_fusion), channel_id=1, source_target_pairs={{0,3},{1,2},{2,1},{3,0},{4,7},{5,6},{6,5},{7,4},{8,11},{9,10},{10,... | collective-permute-start | bytes 129032 | tf_op jit(solution)/shard_map/ppermute | solution.py:356
  21.3 1.3 %collective-permute-start.7 = (f32[168,128]{1,0:T(8,128)S(1)}, f32[168,128]{1,0:T(8,128)S(1)}, u32[]{:S(2)}, u32[]{:S(2)}) collective-permute-start(f32[168,128]{1,0:T(8,128)S(1)} %add_add_fusion.mine), channel_id=1, source_target_pairs={{0,1},{1,0},{2,3},{3,2},{4,5},{5,4},{6,7},{7,6},{8,9},{9,8},{10,11... | collective-permute-start | bytes 258056 | tf_op jit(solution)/shard_map/ppermute | solution.py:356

commit v7 on v6

--- a/solution.py
+++ b/solution.py
@@ -100,7 +100,7 @@
     return lax.rem(sum(lax.rem(me // 2**b, 2) for b in range(bits)), 2)
 
 
-def rim_kernel(bits, own, p_ref, u_head, filters, before, sums, gated, head, totals, slab):
+def rim_kernel(bits, own, p_ref, u_head, filters, before, sums, gated, head, totals, slab, wide):
     _, columns = p_ref.shape
     chans = columns // 3
     taps = filters.shape[1]
@@ -119,10 +119,12 @@
         for s in range(3):
             head[s, m] = grad[s]
             acc = [sums[n, s, j] + grad[s] * slab[s, 0, RIM - j : RIM - j + SUB, :] for j in range(taps)]
-            totals[pl.ds(s * taps * half + m, taps, stride=half), :] = fold(acc)[:taps]
+            wide[pl.ds(s * SUB * half + m, SUB, stride=half), :] = fold(acc)
         return carry
 
     lax.fori_loop(0, half, group, 0, unroll=RIM_UNROLL)
+    for s in range(3):
+        totals[s * taps * half : (s + 1) * taps * half, :] = wide[s * SUB * half : (s * SUB + taps) * half, :]
 
 
 def next_kernel(p_ref, filters, after, following, slab):
@@ -242,7 +244,10 @@
         ),
         in_specs=[VMEM] * 5,
         out_specs=(VMEM,) * 3,
-        scratch_shapes=[pltpu.VMEM((3, 1, RIM + 16, LANES), F32)],
+        scratch_shapes=[
+            pltpu.VMEM((3, 1, RIM + 16, LANES), F32),
+            pltpu.VMEM((3 * SUB * half, LANES), F32),
+        ],
         compiler_params=params(),
         name="rim_own" if own else "rim_other",
     )(projected, u_head, filters, before, sums)
@@ -261,15 +266,16 @@
     )(projected, filters, after)
 
 
-def place_kernel(scale, bits, mine, other, out):
+def place_kernel(scale, bits, mine, other, out, wide):
     _, taps, chans = out.shape
     half = chans // 2 // LANES
     odd = own_half(bits)
-    for s in range(3):
-        for n in range(half):
-            place = pl.ds(s * taps * half + n, taps, stride=half)
-            out[s, :, lanes_at((odd * half + n) * LANES)] = mine[place, :] * scale
-            out[s, :, lanes_at(((1 - odd) * half + n) * LANES)] = other[place, :] * scale
+    for k, (array, side) in enumerate(((mine, odd), (other, 1 - odd))):
+        for s in range(3):
+            wide[k, s * SUB * half : (s * SUB + taps) * half, :] = array[s * taps * half : (s + 1) * taps * half, :]
+            for n in range(half):
+                tile = wide[k, pl.ds(s * SUB * half + n, SUB, stride=half), :]
+                out[s, :, lanes_at((side * half + n) * LANES)] = tile[:taps] * scale
 
 
 def call_place(mine, other, scale, bits, shape):
@@ -278,6 +284,7 @@
         out_shape=jax.ShapeDtypeStruct(shape, F32),
         in_specs=[VMEM] * 2,
         out_specs=VMEM,
+        scratch_shapes=[pltpu.VMEM((2, 3 * SUB * (shape[2] // 2 // LANES), LANES), F32)],
         compiler_params=params(),
         name="place",
     )(mine, other)

time: 23.5 us -> 23.5 us (level)
  no operation moved by 1% of the time
where the time goes in v7:
time: 23.5 us; the launch traced here: 23.4 us
  starting transfers between devices  9.5 us (40%)
  Pallas kernels  8.92 us (38%)
  waiting for transfers between devices  4.13 us (18%)
  between operations  0.72 us (3%)
    ppermute x7, starting transfers between devices, swap(): return lax.ppermute(array, 'seq', [(i, partner(i)) for i in range(ways)])  6.47 us
    ppermute x7, waiting for transfers between devices, swap(): return lax.ppermute(array, 'seq', [(i, partner(i)) for i in range(ways)])  4.13 us
    pallas_call x1, Pallas kernels, call_inner(): pl.pallas_call(inner_kernel, out_shape=(jax.ShapeDtypeStruct((groups, row...  3.36 us
    ppermute x1, starting transfers between devices, trade_far(): return lax.ppermute(array, ('groups', 'seq'), pairs)  3.03 us
    pallas_call x1, Pallas kernels, call_back(): pl.pallas_call(functools.partial(back_kernel, bits), out_shape=(jax.Shape...  2.69 us
    pallas_call x1, Pallas kernels, call_pack(): pl.pallas_call(pack_kernel, out_shape=(jax.ShapeDtypeStruct((16, upstream...  1.28 us
    pallas_call x1, Pallas kernels, call_place(): pl.pallas_call(functools.partial(place_kernel, scale, bits), out_shape=ja...  0.74 us
    pallas_call x2, Pallas kernels, call_rim(): pl.pallas_call(functools.partial(rim_kernel, bits, own), out_shape=(jax.S...  0.58 us
  transfers between devices with their start and end apart: 8, of which 4 were waited for; matrix products, arithmetic and copies ran while one was open for 0% of the time, Pallas kernels for 28%

profile of v7, /device:TPU:0, one launch (start us, length us, event | category | flops | bytes accessed | tf_op | source)
XLA Modules:
  0.0 23.4 jit_solution(5355000754256720006)
XLA Ops:
  0.6 0.0 copy-start
  0.6 0.0 copy-start.1
  0.6 1.3 %pack.1 = (bf16[16,2048]{1,0:T(8,128)(2,1)S(1)}, bf16[8,6144]{1,0:T(8,128)(2,1)S(1)}, bf16[8,6144]{1,0:T(8,128)(2,1)S(1)}) custom-call(bf16[128,6144]{1,0:T(8,128)(2,1)} %p_ref.9, bf16[128,2048]{1,0:T(8,128)(2,1)} %u_hbm.1), custom_call_target="tpu_custom_call" | custom-call | tf_op jit(solution)/shard_map/pack/pallas_call | solution.py:350
  1.9 3.0 %collective-permute-start = (bf16[8,6144]{1,0:T(8,128)(2,1)S(1)}, bf16[8,6144]{1,0:T(8,128)(2,1)S(1)}, u32[]{:S(2)}, u32[]{:S(2)}) collective-permute-start(bf16[8,6144]{1,0:T(8,128)(2,1)S(1)} %get-tuple-element.33), channel_id=1, source_target_pairs={{0,16},{1,2},{2,1},{3,4},{4,3},{5,6},{6,5},{7,8},{8,7},{9,10},{10,... | collective-permute-start | bytes 294920 | tf_op jit(solution)/shard_map/ppermute | solution.py:376
  5.0 0.1 collective-permute-start.1
  5.1 0.0 copy-done
  5.1 0.0 copy-done.1
  5.1 3.4 %inner.1 = (f32[16,128,128]{2,1,0:T(8,128)S(1)}, f32[3,16,128,128]{3,2,1,0:T(8,128)S(1)}, f32[16,3,7,8,128]{4,3,2,1,0:T(8,128)S(1)}) custom-call(bf16[128,6144]{1,0:T(8,128)(2,1)S(1)} %copy-done, bf16[128,2048]{1,0:T(8,128)(2,1)} %u_hbm.1, f32[3,7,2048]{2,1,0:T(8,128)S(1)} %copy-done.1), custom_call_target="tpu_custom_call" | custom-call | flops 22020096 | bytes 2097152 | tf_op jit(solution)/shard_map/inner/pallas_call | solution.py:214
  8.4 0.0 collective-permute-done
  8.4 0.0 collective-permute-done.1
  8.5 0.3 %rim_other.1 = (f32[8,8,128]{2,1,0:T(8,128)S(1)}, f32[3,8,8,128]{3,2,1,0:T(8,128)S(1)}, f32[168,128]{1,0:T(8,128)S(1)}) custom-call(bf16[128,6144]{1,0:T(8,128)(2,1)S(1)} %copy-done, bf16[16,2048]{1,0:T(8,128)(2,1)S(1)} %get-tuple-element.32.u_head, f32[3,7,2048]{2,1,0:T(8,128)S(1)} %copy-done.1, bf16[8,6144]{1,0:T(8,128)(2,1)S(1)} %get-tuple-element.38.before, ...), custom_call_target="tpu_custom_call" | custom-call | tf_op jit(solution)/shard_map/rim_other/pallas_call | solution.py:238
  8.8 0.5 %collective-permute-start.2 = (f32[168,128]{1,0:T(8,128)S(1)}, f32[168,128]{1,0:T(8,128)S(1)}, u32[]{:S(2)}, u32[]{:S(2)}) collective-permute-start(f32[168,128]{1,0:T(8,128)S(1)} %get-tuple-element.37), channel_id=1, source_target_pairs={{0,1},{1,0},{2,3},{3,2},{4,5},{5,4},{6,7},{7,6},{8,9},{9,8},{10,11... | collective-permute-start | bytes 258056 | tf_op jit(solution)/shard_map/ppermute | solution.py:363
  9.3 0.3 %rim_own.1 = (f32[8,8,128]{2,1,0:T(8,128)S(1)}, f32[3,8,8,128]{3,2,1,0:T(8,128)S(1)}, f32[168,128]{1,0:T(8,128)S(1)}) custom-call(bf16[128,6144]{1,0:T(8,128)(2,1)S(1)} %copy-done, bf16[16,2048]{1,0:T(8,128)(2,1)S(1)} %get-tuple-element.32.u_head, f32[3,7,2048]{2,1,0:T(8,128)S(1)} %copy-done.1, bf16[8,6144]{1,0:T(8,128)(2,1)S(1)} %get-tuple-element.38.before, ...), custom_call_target="tpu_custom_call" | custom-call | tf_op jit(solution)/shard_map/rim_own/pallas_call | solution.py:238
  9.6 0.7 %collective-permute-done.2 = f32[168,128]{1,0:T(8,128)S(1)} collective-permute-done((f32[168,128]{1,0:T(8,128)S(1)}, f32[168,128]{1,0:T(8,128)S(1)}, u32[]{:S(2)}, u32[]{:S(2)}) %collective-permute-start.2) | collective-permute-done | bytes 86048 | tf_op jit(solution)/shard_map/ppermute | solution.py:363
  10.2 2.4 %collective-permute-start.3 = (bf16[168,128]{1,0:T(8,128)(2,1)S(1)}, bf16[168,128]{1,0:T(8,128)(2,1)S(1)}, u32[]{:S(2)}, u32[]{:S(2)}) collective-permute-start(bf16[168,128]{1,0:T(8,128)(2,1)S(1)} %add_convert_fusion.1), channel_id=1, source_target_pairs={{0,9},{1,8},{2,11},{3,10},{4,13},{5,12},{6,15},{7,14},{8,1},{9,0},... | collective-permute-start | bytes 129032 | tf_op jit(solution)/shard_map/ppermute | solution.py:363
  12.6 0.3 %next.1.following = f32[3,16,8,128]{3,2,1,0:T(8,128)S(1)} custom-call(bf16[128,6144]{1,0:T(8,128)(2,1)S(1)} %copy-done, f32[3,7,2048]{2,1,0:T(8,128)S(1)} %copy-done.1, bf16[8,6144]{1,0:T(8,128)(2,1)S(1)} %get-tuple-element.43.after), custom_call_target="tpu_custom_call" | custom-call | tf_op jit(solution)/shard_map/next/pallas_call | solution.py:258
  12.9 1.8 %collective-permute-done.3 = bf16[168,128]{1,0:T(8,128)(2,1)S(1)} collective-permute-done((bf16[168,128]{1,0:T(8,128)(2,1)S(1)}, bf16[168,128]{1,0:T(8,128)(2,1)S(1)}, u32[]{:S(2)}, u32[]{:S(2)}) %collective-permute-start.3) | collective-permute-done | bytes 43040 | tf_op jit(solution)/shard_map/ppermute | solution.py:363
  14.7 2.7 %collective-permute-start.6 = (bf16[168,128]{1,0:T(8,128)(2,1)S(1)}, bf16[168,128]{1,0:T(8,128)(2,1)S(1)}, u32[]{:S(2)}, u32[]{:S(2)}) collective-permute-start(bf16[168,128]{1,0:T(8,128)(2,1)S(1)} %add_convert_fusion), channel_id=1, source_target_pairs={{0,6},{1,7},{2,4},{3,5},{4,2},{5,3},{6,0},{7,1},{8,14},{9,15},{10,... | collective-permute-start | bytes 129032 | tf_op jit(solution)/shard_map/ppermute | solution.py:363
  17.4 0.0 collective-permute-start.5
  17.4 0.6 %collective-permute-start.4 = (bf16[168,128]{1,0:T(8,128)(2,1)S(1)}, bf16[168,128]{1,0:T(8,128)(2,1)S(1)}, u32[]{:S(2)}, u32[]{:S(2)}) collective-permute-start(bf16[168,128]{1,0:T(8,128)(2,1)S(1)} %add_convert_fusion), channel_id=1, source_target_pairs={{0,3},{1,2},{2,1},{3,0},{4,7},{5,6},{6,5},{7,4},{8,11},{9,10},{10,... | collective-permute-start | bytes 129032 | tf_op jit(solution)/shard_map/ppermute | solution.py:363
  18.0 2.7 %back.1 = (bf16[128,2048]{1,0:T(8,128)(2,1)}, bf16[128,6144]{1,0:T(8,128)(2,1)}) custom-call(f32[3,7,2048]{2,1,0:T(8,128)S(1)} %copy-done.1, f32[16,128,128]{2,1,0:T(8,128)S(1)} %get-tuple-element.47.gated_in, f32[3,16,128,128]{3,2,1,0:T(8,128)S(1)} %get-tuple-element.48.grads, f32[8,8,128]{2,1,0:T(8,128)S(1)} %get-tuple-element.49.own_gated, ...), custom_call_target="tpu_custom_call" | custom-call | flops 11010048 | bytes 2097152 | tf_op jit(solution)/shard_map/back/pallas_call | solution.py:297
  20.6 0.0 collective-permute-done.6
  20.7 0.6 %collective-permute-done.5 = bf16[168,128]{1,0:T(8,128)(2,1)S(1)} collective-permute-done((bf16[168,128]{1,0:T(8,128)(2,1)S(1)}, bf16[168,128]{1,0:T(8,128)(2,1)S(1)}, u32[]{:S(2)}, u32[]{:S(2)}) %collective-permute-start.5) | collective-permute-done | bytes 43040 | tf_op jit(solution)/shard_map/ppermute | solution.py:363
  21.2 0.0 collective-permute-done.4
  21.3 0.2 collective-permute-start.7
  21.5 1.1 %collective-permute-done.7.other = f32[168,128]{1,0:T(8,128)S(1)} collective-permute-done((f32[168,128]{1,0:T(8,128)S(1)}, f32[168,128]{1,0:T(8,128)S(1)}, u32[]{:S(2)}, u32[]{:S(2)}) %collective-permute-start.7) | collective-permute-done | bytes 86048 | tf_op jit(solution)/shard_map/ppermute | solution.py:363
  22.6 0.7 %place.1 = f32[3,7,2048]{2,1,0:T(8,128)} custom-call(f32[168,128]{1,0:T(8,128)S(1)} %add_add_fusion.mine, f32[168,128]{1,0:T(8,128)S(1)} %collective-permute-done.7.other), custom_call_target="tpu_custom_call" | custom-call | tf_op jit(solution)/shard_map/place/pallas_call | solution.py:282
  (4 shorter events, 0.1 us)
Async XLA Ops:
  0.6 4.4 %copy-start = (bf16[128,6144]{1,0:T(8,128)(2,1)S(1)}, bf16[128,6144]{1,0:T(8,128)(2,1)}, u32[]{:S(2)}) copy-start(bf16[128,6144]{1,0:T(8,128)(2,1)} %p_ref.9) | copy-start | bytes 4718596
  0.6 4.4 %copy-start.1 = (f32[3,7,2048]{2,1,0:T(8,128)S(1)}, f32[3,7,2048]{2,1,0:T(8,128)}, u32[]{:S(2)}) copy-start(f32[3,7,2048]{2,1,0:T(8,128)} %filters.9) | copy-start | bytes 516100
  1.9 6.5 %collective-permute-start = (bf16[8,6144]{1,0:T(8,128)(2,1)S(1)}, bf16[8,6144]{1,0:T(8,128)(2,1)S(1)}, u32[]{:S(2)}, u32[]{:S(2)}) collective-permute-start(bf16[8,6144]{1,0:T(8,128)(2,1)S(1)} %get-tuple-element.33), channel_id=1, source_target_pairs={{0,16},{1,2},{2,1},{3,4},{4,3},{5,6},{6,5},{7,8},{8,7},{9,10},{10,... | collective-permute-start | bytes 294920 | tf_op jit(solution)/shard_map/ppermute | solution.py:376
  5.0 3.5 %collective-permute-start.1 = (bf16[8,6144]{1,0:T(8,128)(2,1)S(1)}, bf16[8,6144]{1,0:T(8,128)(2,1)S(1)}, u32[]{:S(2)}, u32[]{:S(2)}) collective-permute-start(bf16[8,6144]{1,0:T(8,128)(2,1)S(1)} %get-tuple-element.34), channel_id=1, source_target_pairs={{0,1},{1,0},{2,3},{3,2},{4,5},{5,4},{6,7},{7,6},{8,9},{9,8},{10,11... | collective-permute-start | bytes 294920 | tf_op jit(solution)/shard_map/ppermute | solution.py:363
  8.8 1.4 %collective-permute-start.2 = (f32[168,128]{1,0:T(8,128)S(1)}, f32[168,128]{1,0:T(8,128)S(1)}, u32[]{:S(2)}, u32[]{:S(2)}) collective-permute-start(f32[168,128]{1,0:T(8,128)S(1)} %get-tuple-element.37), channel_id=1, source_target_pairs={{0,1},{1,0},{2,3},{3,2},{4,5},{5,4},{6,7},{7,6},{8,9},{9,8},{10,11... | collective-permute-start | bytes 258056 | tf_op jit(solution)/shard_map/ppermute | solution.py:363
  10.2 4.4 %collective-permute-start.3 = (bf16[168,128]{1,0:T(8,128)(2,1)S(1)}, bf16[168,128]{1,0:T(8,128)(2,1)S(1)}, u32[]{:S(2)}, u32[]{:S(2)}) collective-permute-start(bf16[168,128]{1,0:T(8,128)(2,1)S(1)} %add_convert_fusion.1), channel_id=1, source_target_pairs={{0,9},{1,8},{2,11},{3,10},{4,13},{5,12},{6,15},{7,14},{8,1},{9,0},... | collective-permute-start | bytes 129032 | tf_op jit(solution)/shard_map/ppermute | solution.py:363
  14.7 6.0 %collective-permute-start.6 = (bf16[168,128]{1,0:T(8,128)(2,1)S(1)}, bf16[168,128]{1,0:T(8,128)(2,1)S(1)}, u32[]{:S(2)}, u32[]{:S(2)}) collective-permute-start(bf16[168,128]{1,0:T(8,128)(2,1)S(1)} %add_convert_fusion), channel_id=1, source_target_pairs={{0,6},{1,7},{2,4},{3,5},{4,2},{5,3},{6,0},{7,1},{8,14},{9,15},{10,... | collective-permute-start | bytes 129032 | tf_op jit(solution)/shard_map/ppermute | solution.py:363
  17.4 3.9 %collective-permute-start.5 = (bf16[168,128]{1,0:T(8,128)(2,1)S(1)}, bf16[168,128]{1,0:T(8,128)(2,1)S(1)}, u32[]{:S(2)}, u32[]{:S(2)}) collective-permute-start(bf16[168,128]{1,0:T(8,128)(2,1)S(1)} %add_convert_fusion), channel_id=1, source_target_pairs={{0,5},{1,4},{2,7},{3,6},{4,1},{5,0},{6,3},{7,2},{8,13},{9,12},{10,... | collective-permute-start | bytes 129032 | tf_op jit(solution)/shard_map/ppermute | solution.py:363
  17.4 3.9 %collective-permute-start.4 = (bf16[168,128]{1,0:T(8,128)(2,1)S(1)}, bf16[168,128]{1,0:T(8,128)(2,1)S(1)}, u32[]{:S(2)}, u32[]{:S(2)}) collective-permute-start(bf16[168,128]{1,0:T(8,128)(2,1)S(1)} %add_convert_fusion), channel_id=1, source_target_pairs={{0,3},{1,2},{2,1},{3,0},{4,7},{5,6},{6,5},{7,4},{8,11},{9,10},{10,... | collective-permute-start | bytes 129032 | tf_op jit(solution)/shard_map/ppermute | solution.py:363
  21.3 1.3 %collective-permute-start.7 = (f32[168,128]{1,0:T(8,128)S(1)}, f32[168,128]{1,0:T(8,128)S(1)}, u32[]{:S(2)}, u32[]{:S(2)}) collective-permute-start(f32[168,128]{1,0:T(8,128)S(1)} %add_add_fusion.mine), channel_id=1, source_target_pairs={{0,1},{1,0},{2,3},{3,2},{4,5},{5,4},{6,7},{7,6},{8,9},{9,8},{10,11... | collective-permute-start | bytes 258056 | tf_op jit(solution)/shard_map/ppermute | solution.py:363

commit v8 on v7

--- a/solution.py
+++ b/solution.py
@@ -15,8 +15,8 @@
 REACH = 6
 VMEM = pl.BlockSpec(memory_space=pltpu.VMEM)
 HBM = pl.BlockSpec(memory_space=pltpu.HBM)
-UNROLL = 4
-RIM_UNROLL = 4
+UNROLL = 8
+RIM_UNROLL = 8
 
 
 def lanes_at(start):
@@ -266,28 +266,37 @@
     )(projected, filters, after)
 
 
-def place_kernel(scale, bits, mine, other, out, wide):
-    _, taps, chans = out.shape
-    half = chans // 2 // LANES
-    odd = own_half(bits)
-    for k, (array, side) in enumerate(((mine, odd), (other, 1 - odd))):
-        for s in range(3):
-            wide[k, s * SUB * half : (s * SUB + taps) * half, :] = array[s * taps * half : (s + 1) * taps * half, :]
-            for n in range(half):
-                tile = wide[k, pl.ds(s * SUB * half + n, SUB, stride=half), :]
-                out[s, :, lanes_at((side * half + n) * LANES)] = tile[:taps] * scale
-
-
-def call_place(mine, other, scale, bits, shape):
-    return pl.pallas_call(
-        functools.partial(place_kernel, scale, bits),
+def place_kernel(scale, bits, own, array, *refs):
+    out, wide, stage, sem = refs[-4:]
+    _, taps, lanes = stage.shape
+    half = lanes // LANES
+    side = own_half(bits) if own else 1 - own_half(bits)
+    for s in range(3):
+        wide[s * SUB * half : (s * SUB + taps) * half, :] = array[s * taps * half : (s + 1) * taps * half, :]
+        for n in range(half):
+            tile = wide[pl.ds(s * SUB * half + n, SUB, stride=half), :]
+            stage[s, :, n * LANES : (n + 1) * LANES] = tile[:taps] * scale
+    copy = pltpu.make_async_copy(stage, out.at[:, :, pl.ds(pl.multiple_of(side * lanes, LANES), lanes)], sem)
+    copy.start()
+    copy.wait()
+
+
+def call_place(own, scale, bits, shape, array, *placed):
+    _, taps, chans = shape
+    return pl.pallas_call(
+        functools.partial(place_kernel, scale, bits, own),
         out_shape=jax.ShapeDtypeStruct(shape, F32),
-        in_specs=[VMEM] * 2,
-        out_specs=VMEM,
-        scratch_shapes=[pltpu.VMEM((2, 3 * SUB * (shape[2] // 2 // LANES), LANES), F32)],
-        compiler_params=params(),
-        name="place",
-    )(mine, other)
+        in_specs=[VMEM] + [HBM] * len(placed),
+        out_specs=HBM,
+        input_output_aliases={1: 0} if placed else {},
+        scratch_shapes=[
+            pltpu.VMEM((3 * SUB * (chans // 2 // LANES), LANES), F32),
+            pltpu.VMEM((3, taps, chans // 2), F32),
+            pltpu.SemaphoreType.DMA,
+        ],
+        compiler_params=params(),
+        name="place_own" if own else "place_other",
+    )(array, *placed)
 
 
 def call_back(bits, filters, gated, grads, *edges):
@@ -420,8 +429,11 @@
         while len(terms) > 1:
             terms = [sum(terms[k : k + 2]) for k in range(0, len(terms), 2)]
         mine = terms[0]
+    scale = float(rows * ways) ** -0.5
     other = swap(mine, lambda i: i ^ 1)
-    total = call_place(mine, other, float(rows * ways) ** -0.5, bits, filters.shape)
+    total = call_place(True, scale, bits, filters.shape, mine)
+    other, total = lax.optimization_barrier((other, total))
+    total = call_place(False, scale, bits, filters.shape, other, total)
     return gated, grad_projected, total
 
 

time: 23.5 us -> 23.4 us (level)
  waiting for transfers between devices: 4.13 us -> 3.5 us
  Pallas kernels: 8.92 us -> 9.46 us
    ppermute x7, waiting for transfers between devices: 4.13 us -> 3.5 us  [swap(): return lax.ppermute(array, 'seq', [(i, partner(i)) for i in range(ways)])]
    pallas_call x1 -> x2, Pallas kernels: 0.74 us -> 1.37 us  [call_place(): pl.pallas_call(functools.partial(place_kernel, scale, bits, own), out_sha...]
  transfers between devices with their start and end apart: 8 -> 8, of which waited for: 4 -> 4; matrix products, arithmetic and copies ran while one was open for 0% -> 0% of each run, Pallas kernels for 28% -> 31%
where the time goes in v8:
time: 23.4 us; the launch traced here: 23.3 us
  starting transfers between devices  9.51 us (41%)
  Pallas kernels  9.46 us (40%)
  waiting for transfers between devices  3.5 us (15%)
  between operations  0.73 us (3%)
    ppermute x7, starting transfers between devices, swap(): return lax.ppermute(array, 'seq', [(i, partner(i)) for i in range(ways)])  6.47 us
    ppermute x7, waiting for transfers between devices, swap(): return lax.ppermute(array, 'seq', [(i, partner(i)) for i in range(ways)])  3.5 us
    pallas_call x1, Pallas kernels, call_inner(): pl.pallas_call(inner_kernel, out_shape=(jax.ShapeDtypeStruct((groups, row...  3.34 us
    ppermute x1, starting transfers between devices, trade_far(): return lax.ppermute(array, ('groups', 'seq'), pairs)  3.03 us
    pallas_call x1, Pallas kernels, call_back(): pl.pallas_call(functools.partial(back_kernel, bits), out_shape=(jax.Shape...  2.67 us
    pallas_call x2, Pallas kernels, call_place(): pl.pallas_call(functools.partial(place_kernel, scale, bits, own), out_sha...  1.37 us
    pallas_call x1, Pallas kernels, call_pack(): pl.pallas_call(pack_kernel, out_shape=(jax.ShapeDtypeStruct((16, upstream...  1.28 us
    pallas_call x2, Pallas kernels, call_rim(): pl.pallas_call(functools.partial(rim_kernel, bits, own), out_shape=(jax.S...  0.56 us
  transfers between devices with their start and end apart: 8, of which 4 were waited for; matrix products, arithmetic and copies ran while one was open for 0% of the time, Pallas kernels for 31%

profile of v8, /device:TPU:0, one launch (start us, length us, event | category | flops | bytes accessed | tf_op | source)
XLA Modules:
  0.0 23.3 jit_solution(2016841970923396181)
XLA Ops:
  0.6 0.0 copy-start
  0.6 0.0 copy-start.1
  0.6 1.3 %pack.1 = (bf16[16,2048]{1,0:T(8,128)(2,1)S(1)}, bf16[8,6144]{1,0:T(8,128)(2,1)S(1)}, bf16[8,6144]{1,0:T(8,128)(2,1)S(1)}) custom-call(bf16[128,6144]{1,0:T(8,128)(2,1)} %p_ref.9, bf16[128,2048]{1,0:T(8,128)(2,1)} %u_hbm.1), custom_call_target="tpu_custom_call" | custom-call | tf_op jit(solution)/shard_map/pack/pallas_call | solution.py:359
  1.9 3.0 %collective-permute-start = (bf16[8,6144]{1,0:T(8,128)(2,1)S(1)}, bf16[8,6144]{1,0:T(8,128)(2,1)S(1)}, u32[]{:S(2)}, u32[]{:S(2)}) collective-permute-start(bf16[8,6144]{1,0:T(8,128)(2,1)S(1)} %get-tuple-element.35), channel_id=1, source_target_pairs={{0,16},{1,2},{2,1},{3,4},{4,3},{5,6},{6,5},{7,8},{8,7},{9,10},{10,... | collective-permute-start | bytes 294920 | tf_op jit(solution)/shard_map/ppermute | solution.py:385
  5.0 0.1 collective-permute-start.1
  5.1 0.0 copy-done
  5.1 0.0 copy-done.1
  5.1 3.3 %inner.1 = (f32[16,128,128]{2,1,0:T(8,128)S(1)}, f32[3,16,128,128]{3,2,1,0:T(8,128)S(1)}, f32[16,3,7,8,128]{4,3,2,1,0:T(8,128)S(1)}) custom-call(bf16[128,6144]{1,0:T(8,128)(2,1)S(1)} %copy-done, bf16[128,2048]{1,0:T(8,128)(2,1)} %u_hbm.1, f32[3,7,2048]{2,1,0:T(8,128)S(1)} %copy-done.1), custom_call_target="tpu_custom_call" | custom-call | flops 22020096 | bytes 2097152 | tf_op jit(solution)/shard_map/inner/pallas_call | solution.py:214
  8.4 0.0 collective-permute-done
  8.4 0.0 collective-permute-done.1
  8.5 0.3 %rim_other.1 = (f32[8,8,128]{2,1,0:T(8,128)S(1)}, f32[3,8,8,128]{3,2,1,0:T(8,128)S(1)}, f32[168,128]{1,0:T(8,128)S(1)}) custom-call(bf16[128,6144]{1,0:T(8,128)(2,1)S(1)} %copy-done, bf16[16,2048]{1,0:T(8,128)(2,1)S(1)} %get-tuple-element.34.u_head, f32[3,7,2048]{2,1,0:T(8,128)S(1)} %copy-done.1, bf16[8,6144]{1,0:T(8,128)(2,1)S(1)} %get-tuple-element.40.before, ...), custom_call_target="tpu_custom_call" | custom-call | tf_op jit(solution)/shard_map/rim_other/pallas_call | solution.py:238
  8.8 0.5 %collective-permute-start.2 = (f32[168,128]{1,0:T(8,128)S(1)}, f32[168,128]{1,0:T(8,128)S(1)}, u32[]{:S(2)}, u32[]{:S(2)}) collective-permute-start(f32[168,128]{1,0:T(8,128)S(1)} %get-tuple-element.39), channel_id=1, source_target_pairs={{0,1},{1,0},{2,3},{3,2},{4,5},{5,4},{6,7},{7,6},{8,9},{9,8},{10,11... | collective-permute-start | bytes 258056 | tf_op jit(solution)/shard_map/ppermute | solution.py:372
  9.2 0.3 %rim_own.1 = (f32[8,8,128]{2,1,0:T(8,128)S(1)}, f32[3,8,8,128]{3,2,1,0:T(8,128)S(1)}, f32[168,128]{1,0:T(8,128)S(1)}) custom-call(bf16[128,6144]{1,0:T(8,128)(2,1)S(1)} %copy-done, bf16[16,2048]{1,0:T(8,128)(2,1)S(1)} %get-tuple-element.34.u_head, f32[3,7,2048]{2,1,0:T(8,128)S(1)} %copy-done.1, bf16[8,6144]{1,0:T(8,128)(2,1)S(1)} %get-tuple-element.40.before, ...), custom_call_target="tpu_custom_call" | custom-call | tf_op jit(solution)/shard_map/rim_own/pallas_call | solution.py:238
  9.5 0.7 %collective-permute-done.2 = f32[168,128]{1,0:T(8,128)S(1)} collective-permute-done((f32[168,128]{1,0:T(8,128)S(1)}, f32[168,128]{1,0:T(8,128)S(1)}, u32[]{:S(2)}, u32[]{:S(2)}) %collective-permute-start.2) | collective-permute-done | bytes 86048 | tf_op jit(solution)/shard_map/ppermute | solution.py:372
  10.2 2.4 %collective-permute-start.3 = (bf16[168,128]{1,0:T(8,128)(2,1)S(1)}, bf16[168,128]{1,0:T(8,128)(2,1)S(1)}, u32[]{:S(2)}, u32[]{:S(2)}) collective-permute-start(bf16[168,128]{1,0:T(8,128)(2,1)S(1)} %add_convert_fusion.1), channel_id=1, source_target_pairs={{0,9},{1,8},{2,11},{3,10},{4,13},{5,12},{6,15},{7,14},{8,1},{9,0},... | collective-permute-start | bytes 129032 | tf_op jit(solution)/shard_map/ppermute | solution.py:372
  12.6 0.2 %next.1.following = f32[3,16,8,128]{3,2,1,0:T(8,128)S(1)} custom-call(bf16[128,6144]{1,0:T(8,128)(2,1)S(1)} %copy-done, f32[3,7,2048]{2,1,0:T(8,128)S(1)} %copy-done.1, bf16[8,6144]{1,0:T(8,128)(2,1)S(1)} %get-tuple-element.45.after), custom_call_target="tpu_custom_call" | custom-call | tf_op jit(solution)/shard_map/next/pallas_call | solution.py:258
  12.8 1.8 %collective-permute-done.3 = bf16[168,128]{1,0:T(8,128)(2,1)S(1)} collective-permute-done((bf16[168,128]{1,0:T(8,128)(2,1)S(1)}, bf16[168,128]{1,0:T(8,128)(2,1)S(1)}, u32[]{:S(2)}, u32[]{:S(2)}) %collective-permute-start.3) | collective-permute-done | bytes 43040 | tf_op jit(solution)/shard_map/ppermute | solution.py:372
  14.6 2.7 %collective-permute-start.6 = (bf16[168,128]{1,0:T(8,128)(2,1)S(1)}, bf16[168,128]{1,0:T(8,128)(2,1)S(1)}, u32[]{:S(2)}, u32[]{:S(2)}) collective-permute-start(bf16[168,128]{1,0:T(8,128)(2,1)S(1)} %add_convert_fusion), channel_id=1, source_target_pairs={{0,6},{1,7},{2,4},{3,5},{4,2},{5,3},{6,0},{7,1},{8,14},{9,15},{10,... | collective-permute-start | bytes 129032 | tf_op jit(solution)/shard_map/ppermute | solution.py:372
  17.4 0.0 collective-permute-start.5
  17.4 0.5 %collective-permute-start.4 = (bf16[168,128]{1,0:T(8,128)(2,1)S(1)}, bf16[168,128]{1,0:T(8,128)(2,1)S(1)}, u32[]{:S(2)}, u32[]{:S(2)}) collective-permute-start(bf16[168,128]{1,0:T(8,128)(2,1)S(1)} %add_convert_fusion), channel_id=1, source_target_pairs={{0,3},{1,2},{2,1},{3,0},{4,7},{5,6},{6,5},{7,4},{8,11},{9,10},{10,... | collective-permute-start | bytes 129032 | tf_op jit(solution)/shard_map/ppermute | solution.py:372
  17.9 2.7 %back.1 = (bf16[128,2048]{1,0:T(8,128)(2,1)}, bf16[128,6144]{1,0:T(8,128)(2,1)}) custom-call(f32[3,7,2048]{2,1,0:T(8,128)S(1)} %copy-done.1, f32[16,128,128]{2,1,0:T(8,128)S(1)} %get-tuple-element.49.gated_in, f32[3,16,128,128]{3,2,1,0:T(8,128)S(1)} %get-tuple-element.50.grads, f32[8,8,128]{2,1,0:T(8,128)S(1)} %get-tuple-element.51.own_gated, ...), custom_call_target="tpu_custom_call" | custom-call | flops 11010048 | bytes 2097152 | tf_op jit(solution)/shard_map/back/pallas_call | solution.py:306
  20.6 0.0 collective-permute-done.6
  20.6 0.6 %collective-permute-done.5 = bf16[168,128]{1,0:T(8,128)(2,1)S(1)} collective-permute-done((bf16[168,128]{1,0:T(8,128)(2,1)S(1)}, bf16[168,128]{1,0:T(8,128)(2,1)S(1)}, u32[]{:S(2)}, u32[]{:S(2)}) %collective-permute-start.5) | collective-permute-done | bytes 43040 | tf_op jit(solution)/shard_map/ppermute | solution.py:372
  21.2 0.0 collective-permute-done.4
  21.2 0.2 collective-permute-start.7
  21.5 0.7 %place_own.1.refs_0_ = f32[3,7,2048]{2,1,0:T(8,128)} custom-call(f32[168,128]{1,0:T(8,128)S(1)} %add_add_fusion.array), custom_call_target="tpu_custom_call" | custom-call | tf_op jit(solution)/shard_map/place_own/pallas_call | solution.py:286
  22.2 0.4 %collective-permute-done.7.array = f32[168,128]{1,0:T(8,128)S(1)} collective-permute-done((f32[168,128]{1,0:T(8,128)S(1)}, f32[168,128]{1,0:T(8,128)S(1)}, u32[]{:S(2)}, u32[]{:S(2)}) %collective-permute-start.7) | collective-permute-done | bytes 86048 | tf_op jit(solution)/shard_map/ppermute | solution.py:372
  22.6 0.7 %place_other.1 = f32[3,7,2048]{2,1,0:T(8,128)} custom-call(f32[168,128]{1,0:T(8,128)S(1)} %collective-permute-done.7.array, f32[3,7,2048]{2,1,0:T(8,128)} %place_own.1.refs_0_), custom_call_target="tpu_custom_call", output_to_operand_aliasing={{}: (1, {})} | custom-call | tf_op jit(solution)/shard_map/place_other/pallas_call | solution.py:286
  (4 shorter events, 0.1 us)
Async XLA Ops:
  0.6 4.4 %copy-start = (bf16[128,6144]{1,0:T(8,128)(2,1)S(1)}, bf16[128,6144]{1,0:T(8,128)(2,1)}, u32[]{:S(2)}) copy-start(bf16[128,6144]{1,0:T(8,128)(2,1)} %p_ref.9) | copy-start | bytes 4718596
  0.6 4.4 %copy-start.1 = (f32[3,7,2048]{2,1,0:T(8,128)S(1)}, f32[3,7,2048]{2,1,0:T(8,128)}, u32[]{:S(2)}) copy-start(f32[3,7,2048]{2,1,0:T(8,128)} %filters.9) | copy-start | bytes 516100
  1.9 6.5 %collective-permute-start = (bf16[8,6144]{1,0:T(8,128)(2,1)S(1)}, bf16[8,6144]{1,0:T(8,128)(2,1)S(1)}, u32[]{:S(2)}, u32[]{:S(2)}) collective-permute-start(bf16[8,6144]{1,0:T(8,128)(2,1)S(1)} %get-tuple-element.35), channel_id=1, source_target_pairs={{0,16},{1,2},{2,1},{3,4},{4,3},{5,6},{6,5},{7,8},{8,7},{9,10},{10,... | collective-permute-start | bytes 294920 | tf_op jit(solution)/shard_map/ppermute | solution.py:385
  5.0 3.5 %collective-permute-start.1 = (bf16[8,6144]{1,0:T(8,128)(2,1)S(1)}, bf16[8,6144]{1,0:T(8,128)(2,1)S(1)}, u32[]{:S(2)}, u32[]{:S(2)}) collective-permute-start(bf16[8,6144]{1,0:T(8,128)(2,1)S(1)} %get-tuple-element.36), channel_id=1, source_target_pairs={{0,1},{1,0},{2,3},{3,2},{4,5},{5,4},{6,7},{7,6},{8,9},{9,8},{10,11... | collective-permute-start | bytes 294920 | tf_op jit(solution)/shard_map/ppermute | solution.py:372
  8.8 1.4 %collective-permute-start.2 = (f32[168,128]{1,0:T(8,128)S(1)}, f32[168,128]{1,0:T(8,128)S(1)}, u32[]{:S(2)}, u32[]{:S(2)}) collective-permute-start(f32[168,128]{1,0:T(8,128)S(1)} %get-tuple-element.39), channel_id=1, source_target_pairs={{0,1},{1,0},{2,3},{3,2},{4,5},{5,4},{6,7},{7,6},{8,9},{9,8},{10,11... | collective-permute-start | bytes 258056 | tf_op jit(solution)/shard_map/ppermute | solution.py:372
  10.2 4.4 %collective-permute-start.3 = (bf16[168,128]{1,0:T(8,128)(2,1)S(1)}, bf16[168,128]{1,0:T(8,128)(2,1)S(1)}, u32[]{:S(2)}, u32[]{:S(2)}) collective-permute-start(bf16[168,128]{1,0:T(8,128)(2,1)S(1)} %add_convert_fusion.1), channel_id=1, source_target_pairs={{0,9},{1,8},{2,11},{3,10},{4,13},{5,12},{6,15},{7,14},{8,1},{9,0},... | collective-permute-start | bytes 129032 | tf_op jit(solution)/shard_map/ppermute | solution.py:372
  14.6 6.0 %collective-permute-start.6 = (bf16[168,128]{1,0:T(8,128)(2,1)S(1)}, bf16[168,128]{1,0:T(8,128)(2,1)S(1)}, u32[]{:S(2)}, u32[]{:S(2)}) collective-permute-start(bf16[168,128]{1,0:T(8,128)(2,1)S(1)} %add_convert_fusion), channel_id=1, source_target_pairs={{0,6},{1,7},{2,4},{3,5},{4,2},{5,3},{6,0},{7,1},{8,14},{9,15},{10,... | collective-permute-start | bytes 129032 | tf_op jit(solution)/shard_map/ppermute | solution.py:372
  17.4 3.9 %collective-permute-start.5 = (bf16[168,128]{1,0:T(8,128)(2,1)S(1)}, bf16[168,128]{1,0:T(8,128)(2,1)S(1)}, u32[]{:S(2)}, u32[]{:S(2)}) collective-permute-start(bf16[168,128]{1,0:T(8,128)(2,1)S(1)} %add_convert_fusion), channel_id=1, source_target_pairs={{0,5},{1,4},{2,7},{3,6},{4,1},{5,0},{6,3},{7,2},{8,13},{9,12},{10,... | collective-permute-start | bytes 129032 | tf_op jit(solution)/shard_map/ppermute | solution.py:372
  17.4 3.9 %collective-permute-start.4 = (bf16[168,128]{1,0:T(8,128)(2,1)S(1)}, bf16[168,128]{1,0:T(8,128)(2,1)S(1)}, u32[]{:S(2)}, u32[]{:S(2)}) collective-permute-start(bf16[168,128]{1,0:T(8,128)(2,1)S(1)} %add_convert_fusion), channel_id=1, source_target_pairs={{0,3},{1,2},{2,1},{3,0},{4,7},{5,6},{6,5},{7,4},{8,11},{9,10},{10,... | collective-permute-start | bytes 129032 | tf_op jit(solution)/shard_map/ppermute | solution.py:372
  21.2 1.3 %collective-permute-start.7 = (f32[168,128]{1,0:T(8,128)S(1)}, f32[168,128]{1,0:T(8,128)S(1)}, u32[]{:S(2)}, u32[]{:S(2)}) collective-permute-start(f32[168,128]{1,0:T(8,128)S(1)} %add_add_fusion.array), channel_id=1, source_target_pairs={{0,1},{1,0},{2,3},{3,2},{4,5},{5,4},{6,7},{7,6},{8,9},{9,8},{10,11... | collective-permute-start | bytes 258056 | tf_op jit(solution)/shard_map/ppermute | solution.py:372
